TPU v7x, 32 devices: a whole 2x2x4 slice. The times are simulated.
32 devices in a mesh: grp: 2 (over y), dap: 4 (over z), sub: 2 (over x), pair: 2 (over core).
Axes of the slice: x: 2, y: 2, z: 4, core: 2. Of those that a mesh axis runs over, the one named last changes fastest.
Arguments:
- pair_input: bfloat16 [320, 160, 128], P(('grp', 'dap'), ('sub', 'pair')), parts along dimension 0, may hold values from -6 to 6
- residue_mask: int32 [320], P('grp'), parts along dimension 0, may hold values 0 or 1
- entry_gain: float32 [2, 128], replicated, may hold values from 0.5 to 1.5
- input_weight: bfloat16 [2, 128, 640], replicated, may hold values from -0.5 to 0.5
- middle_gain: float32 [2, 128], replicated, may hold values from 0.5 to 1.5
- output_weight: bfloat16 [2, 128, 128], replicated, may hold values from -0.5 to 0.5
- final_gain: float32 [128], replicated, may hold values from 0.5 to 1.5
- expand_weight: bfloat16 [128, 512], replicated, may hold values from -0.5 to 0.5
- shrink_weight: bfloat16 [512, 128], replicated, may hold values from -0.25 to 0.25
Outputs:
- pair_output: bfloat16 [320, 160, 128], P(('grp', 'dap'), ('sub', 'pair')), parts along dimension 0
There are 2 independent parts, one for each index of `grp`. A program takes and returns all parts, laid end to end along the dimension named above; an argument that names none is the same for every part. Nothing has to cross between parts.
All inputs are finite; a program needn't handle non-finite values.
Results may differ from a plain program's by a relative error of at most 0.012.
Values may be sent and summed in bfloat16 or wider, within the bound.
No kernel may reach another device: no remote copies, remote signals or barrier semaphores. Data moves between devices by JAX's collectives and lax.ppermute only.
A program may use at most 64 MiB of HBM per device.

v0:
```python
import functools

import jax
import jax.numpy as jnp
from jax import lax
from jax.experimental import pallas as pl
from jax.experimental.pallas import tpu as pltpu
from jax.sharding import PartitionSpec as P

F32 = jnp.float32
BF16 = jnp.bfloat16
LANES = 128
GROUP = 8
CHIPS = ("dap", "sub", "pair")


def layer_norm(values, factor, dimension):
    average = jnp.mean(values, axis=dimension, keepdims=True)
    centred = values - average
    variance = jnp.mean(centred * centred, axis=dimension, keepdims=True)
    return centred * lax.rsqrt(variance + 1e-05) * factor


def spread_rows(left_side, right_side):
    return (
        lax.all_to_all(left_side, ("sub", "pair"), split_axis=0, concat_axis=2, tiled=True),
        lax.all_to_all(right_side, ("sub", "pair"), split_axis=0, concat_axis=2, tiled=True),
    )


def return_rows(mixed_sum):
    return lax.all_to_all(mixed_sum, ("sub", "pair"), split_axis=2, concat_axis=0, tiled=True)


def outgoing_rows(left_side, right_side):
    left_wide, right_wide = spread_rows(left_side, right_side)
    summed = jnp.einsum(
        "cik,cjk->cij",
        left_wide,
        lax.all_gather(right_wide, "dap", axis=1, tiled=True),
        preferred_element_type=jnp.float32,
    )
    return return_rows(summed.astype(jnp.bfloat16))


def incoming_rows(left_side, right_side):
    left_wide, right_wide = spread_rows(left_side, right_side)
    flipped = lax.all_to_all(left_wide, "dap", split_axis=2, concat_axis=1, tiled=True)
    summed = jnp.einsum(
        "cki,ckj->cij",
        flipped,
        lax.all_gather(right_wide, "dap", axis=1, tiled=True),
        preferred_element_type=jnp.float32,
    )
    return return_rows(summed.astype(jnp.bfloat16))


def triangle_update(
    stream, pair_mask, entry_gain, input_weight, middle_gain, output_weight, incoming
):
    row_count, col_count, channels = stream.shape
    hidden = output_weight.shape[0]
    normed = (
        layer_norm(stream, entry_gain, 2)
        .astype(jnp.bfloat16)
        .reshape(row_count * col_count, channels)
    )
    projected = lax.dot_general(
        input_weight[:, : 4 * hidden],
        normed,
        (((0,), (1,)), ((), ())),
        preferred_element_type=jnp.float32,
    )
    projected = projected.reshape(4 * hidden, row_count, col_count)
    left_side = (
        pair_mask * jax.nn.sigmoid(projected[hidden : 2 * hidden]) * projected[:hidden]
    ).astype(jnp.bfloat16)
    right_side = (
        pair_mask * jax.nn.sigmoid(projected[3 * hidden :]) * projected[2 * hidden : 3 * hidden]
    ).astype(jnp.bfloat16)
    gate_vals = jax.nn.sigmoid(
        jnp.dot(normed, input_weight[:, 4 * hidden :], preferred_element_type=jnp.float32)
    )
    mixed_sum = (
        incoming_rows(left_side, right_side) if incoming else outgoing_rows(left_side, right_side)
    )
    middle = layer_norm(mixed_sum.astype(jnp.float32), middle_gain[:, None, None], 0).astype(
        jnp.bfloat16
    )
    middle = middle.reshape(hidden, row_count * col_count)
    output = lax.dot_general(
        middle, output_weight, (((0,), (0,)), ((), ())), preferred_element_type=jnp.float32
    )
    return stream + (gate_vals * output).reshape(row_count, col_count, channels)


def general_device(
    pair_input,
    residue_mask,
    entry_gain,
    input_weight,
    middle_gain,
    output_weight,
    final_gain,
    expand_weight,
    shrink_weight,
):
    row_count, col_count, channels = pair_input.shape
    row_offset = lax.axis_index("dap") * row_count
    col_offset = lax.axis_index(("sub", "pair")) * col_count
    row_mask = lax.dynamic_slice_in_dim(residue_mask, row_offset, row_count).astype(jnp.float32)
    col_mask = lax.dynamic_slice_in_dim(residue_mask, col_offset, col_count).astype(jnp.float32)
    pair_mask = row_mask[:, None] * col_mask[None, :]
    stream = pair_input.astype(jnp.float32)
    for update_id in range(2):
        stream = triangle_update(
            stream,
            pair_mask,
            entry_gain[update_id],
            input_weight[update_id],
            middle_gain[update_id],
            output_weight[update_id],
            update_id == 1,
        )
    flat = stream.reshape(row_count * col_count, channels)
    normed = layer_norm(flat, final_gain, 1).astype(jnp.bfloat16)
    expanded = jax.nn.relu(
        jnp.dot(normed, expand_weight, preferred_element_type=jnp.float32)
    ).astype(jnp.bfloat16)
    result = flat + jnp.dot(expanded, shrink_weight, preferred_element_type=jnp.float32)
    return result.astype(jnp.bfloat16).reshape(row_count, col_count, channels)


def sigmoid(values):
    return 0.5 * jnp.tanh(0.5 * values) + 0.5


def norm_rows(values, factor):
    average = jnp.mean(values, axis=0, keepdims=True)
    centred = values - average
    variance = jnp.mean(centred * centred, axis=0, keepdims=True)
    return centred * lax.rsqrt(variance + 1e-05) * factor


def column_of(gain_row, width):
    square = jnp.broadcast_to(gain_row, (gain_row.shape[1], gain_row.shape[1])).T
    return jnp.concatenate([square] * (width // square.shape[1]), axis=1)


def lane_index():
    return lax.broadcasted_iota(jnp.int32, (GROUP, LANES), 1)


def split_group(chunk, width, lane):
    pieces = []
    for row in range(GROUP):
        first, offset = divmod(row * width, LANES)
        piece = chunk[:, first * LANES : (first + 1) * LANES]
        if offset:
            piece = pltpu.roll(piece, LANES - offset, 1)
            if offset + width > LANES:
                after = chunk[:, (first + 1) * LANES : (first + 2) * LANES]
                after = pltpu.roll(after, LANES - offset, 1)
                piece = jnp.where(lane < LANES - offset, piece, after)
        pieces.append(jnp.where(lane < width, piece, 0.0))
    return pieces


def join_group(pieces, width, lane):
    parts = []
    for part in range(GROUP * width // LANES):
        begin = part * LANES
        value = None
        for row in range(begin // width, (begin + LANES - 1) // width + 1):
            shift = row * width - begin
            piece = pieces[row]
            if shift % LANES:
                piece = pltpu.roll(piece, shift % LANES, 1)
            value = piece if value is None else jnp.where(lane >= shift, piece, value)
        parts.append(value)
    return jnp.concatenate(parts, axis=1)


def pick_rows(table, starts, size):
    return jnp.concatenate(
        [table[pl.ds(pl.multiple_of(start, GROUP), size), :] for start in starts], axis=0
    )


def side_weights(table, meta, incoming):
    core, chip = meta[0], meta[1]
    hidden = table.shape[0] // 5
    mine = hidden // 2
    count = 8 if incoming else 4
    size = mine // count
    picked = []
    for base in range(4):
        starts = [
            base * hidden + core * mine + size * ((chip & (count - 1)) ^ k) for k in range(count)
        ]
        picked.append(pick_rows(table, starts, size))
    return jnp.concatenate(picked, axis=0).astype(BF16)


def send_sides(normed, weights, mask, messages, lanes, incoming):
    quarter = weights.shape[0] // 4
    projected = jnp.dot(weights, normed, preferred_element_type=F32)
    left = mask * sigmoid(projected[quarter : 2 * quarter]) * projected[:quarter]
    right = mask * sigmoid(projected[3 * quarter :]) * projected[2 * quarter : 3 * quarter]
    count = 8 if incoming else 4
    size = quarter // count
    for k in range(count):
        rows = slice(k * size, (k + 1) * size)
        messages[k][:, lanes] = jnp.concatenate([left[rows], right[rows]], axis=0).astype(BF16)
        if not incoming:
            messages[4 + k][:, lanes] = right[rows].astype(BF16)


def first_kernel(meta, own, other, mask, gain, weight, *refs):
    stream, normed_out, *messages, both, table = refs
    core = meta[0]
    rows, cols, channels = own.shape
    both[:, pl.ds(pl.multiple_of(core * cols, GROUP), cols), :] = own[...].astype(F32)
    both[:, pl.ds(pl.multiple_of((1 - core) * cols, GROUP), cols), :] = other[...].astype(F32)
    table[...] = weight[0].astype(F32).T
    weights = side_weights(table, meta, False)
    width = GROUP * 2 * cols
    factor = column_of(gain[0:1, :], width)

    @pl.loop(0, rows // GROUP)
    def _(step):
        lanes = pl.ds(pl.multiple_of(step * width, LANES), width)
        values = both[pl.ds(step * GROUP, GROUP)].reshape(width, channels).T
        stream[:, lanes] = values
        normed = norm_rows(values, factor).astype(BF16)
        normed_out[:, lanes] = normed
        send_sides(normed, weights, mask[:, lanes], messages, lanes, False)


def gate_kernel(normed, weight, gate, *, update):
    channels = normed.shape[0]
    hidden = (weight.shape[2] - channels) // 4
    table = weight[update, :, 4 * hidden :].astype(F32).T.astype(BF16)
    gate[...] = sigmoid(jnp.dot(table, normed[...], preferred_element_type=F32))


def outgoing_kernel(meta, *refs, rows, width):
    messages, outs = refs[:8], refs[8:12]
    left, right, total = refs[12:]
    dap, sub = meta[1] >> 1, meta[1] & 1
    lane = lane_index()
    count = outs[0].shape[0]
    span = 2 * rows

    @pl.loop(0, rows // GROUP)
    def _(step):
        lanes = pl.ds(pl.multiple_of(step * GROUP * width, LANES), GROUP * width)
        for k in range(8):
            values = messages[k][:, lanes].astype(F32)
            source = dap ^ (k >> 1)
            half = (source >> 1) ^ sub
            near = (source & 1) * rows
            if k < 4:
                begin = ((k >> 1) & 1) * rows + step * GROUP
                for c in range(0, count, GROUP):
                    for i, piece in enumerate(split_group(values[c : c + GROUP], width, lane)):
                        left[k & 1, pl.ds(c * span + begin + i, GROUP, stride=span), :] = piece
                values = values[count:]
            begin = half * (count * span) + near + step * GROUP
            for c in range(0, count, GROUP):
                for i, piece in enumerate(split_group(values[c : c + GROUP], width, lane)):
                    right[k & 1, pl.ds(c * span + begin + i, GROUP, stride=span), :] = piece

    @pl.loop(0, count)
    def _(c):
        here = pl.ds(pl.multiple_of(c * span, GROUP), span)
        a = jnp.concatenate([left[0, here, :], left[1, here, :]], axis=1).astype(BF16)
        for half in range(2):
            there = pl.ds(pl.multiple_of(half * (count * span) + c * span, GROUP), span)
            b = jnp.concatenate([right[0, there, :], right[1, there, :]], axis=1).astype(BF16)
            total[half, here, 0:width] = lax.dot_general(
                a, b, (((1,), (1,)), ((), ())), preferred_element_type=F32
            )

    @pl.loop(0, rows // GROUP)
    def _(step):
        lanes = pl.ds(pl.multiple_of(step * GROUP * width, LANES), GROUP * width)
        for k in range(4):
            begin = (k >> 1) * rows + step * GROUP
            joined = []
            for c in range(0, count, GROUP):
                pieces = [
                    total[k & 1, pl.ds(c * span + begin + i, GROUP, stride=span), :]
                    for i in range(GROUP)
                ]
                joined.append(join_group(pieces, width, lane))
            outs[k][:, lanes] = jnp.concatenate(joined, axis=0).astype(BF16)


def incoming_kernel(meta, *refs, rows, width):
    messages, outs = refs[:8], refs[8:16]
    left, right, total = refs[16:]
    dap, sub = meta[1] >> 1, meta[1] & 1
    lane = lane_index()
    count = outs[0].shape[0]
    span = 4 * rows
    tall = 2 * LANES

    @pl.loop(0, rows // GROUP)
    def _(step):
        lanes = pl.ds(pl.multiple_of(step * GROUP * width, LANES), GROUP * width)
        for k in range(8):
            values = messages[k][:, lanes].astype(F32)
            begin = (k >> 1) * rows + step * GROUP
            for side, part in ((left, values[:count]), (right, values[count:])):
                for i, piece in enumerate(split_group(part, width, lane)):
                    side[k & 1, pl.ds(begin + i, GROUP, stride=span), :] = piece

    @pl.loop(0, count)
    def _(c):
        here = pl.ds(pl.multiple_of(c * span, GROUP), span)
        a = jnp.concatenate([left[0, here, :], left[1, here, :]], axis=1).astype(BF16)
        b = jnp.concatenate([right[0, here, :], right[1, here, :]], axis=1).astype(BF16)
        product = lax.dot_general(a, b, (((0,), (0,)), ((), ())), preferred_element_type=F32)
        there = pl.ds(pl.multiple_of(c * tall, GROUP), tall)
        total[0, there, :] = product[:, :LANES]
        total[1, there, :] = product[:, LANES:]

    @pl.loop(0, rows // GROUP)
    def _(step):
        lanes = pl.ds(pl.multiple_of(step * GROUP * width, LANES), GROUP * width)
        for k in range(8):
            target = dap ^ (k >> 1)
            begin = ((target >> 1) ^ sub) * LANES + (target & 1) * rows + step * GROUP
            pieces = [
                total[k & 1, pl.ds(begin + i, GROUP, stride=tall), :] for i in range(GROUP)
            ]
            outs[k][:, lanes] = join_group(pieces, width, lane).astype(BF16)


def output_weights(table, square, gain, meta, count):
    core, chip = meta[0], meta[1]
    mine = table.shape[0] // 2
    size = mine // count
    starts = [
        side * mine + size * ((chip & (count - 1)) ^ k)
        for side in (core, 1 - core)
        for k in range(count)
    ]
    square[...] = jnp.broadcast_to(gain, square.shape).T
    return pick_rows(table, starts, size).T.astype(BF16), pick_rows(square, starts, size)


def add_update(own, other, stream, gate, weights, factor, lanes):
    mixed = jnp.concatenate([own[:, lanes].astype(F32), other[:, lanes].astype(F32)], axis=0)
    middle = norm_rows(mixed, factor).astype(BF16)
    return stream[:, lanes] + gate[:, lanes] * jnp.dot(weights, middle, preferred_element_type=F32)


def second_kernel(
    meta, own, other, stream, gate, mask, entry_gain, weight, middle_gain, out_weight, *refs, width
):
    stream_out, normed_out, *messages, table, out_table, square = refs
    out_table[...] = out_weight[0].astype(F32)
    out_weights, middle = output_weights(out_table, square, middle_gain[0:1, :], meta, 4)
    table[...] = weight[1].astype(F32).T
    weights = side_weights(table, meta, True)
    middle_factor = jnp.concatenate([middle] * (width // middle.shape[1]), axis=1)
    factor = column_of(entry_gain[1:2, :], width)

    @pl.loop(0, stream.shape[1] // width)
    def _(step):
        lanes = pl.ds(pl.multiple_of(step * width, LANES), width)
        values = add_update(own, other, stream, gate, out_weights, middle_factor, lanes)
        stream_out[:, lanes] = values
        normed = norm_rows(values, factor).astype(BF16)
        normed_out[:, lanes] = normed
        send_sides(normed, weights, mask[:, lanes], messages, lanes, True)


def last_kernel(
    meta, own, other, stream, gate, middle_gain, out_weight, final_gain, expand, shrink, *refs, width
):
    result, out_table, square, both = refs
    core = meta[0]
    rows, cols, channels = result.shape
    out_table[...] = out_weight[1].astype(F32)
    out_weights, middle = output_weights(out_table, square, middle_gain[1:2, :], meta, 8)
    middle_factor = jnp.concatenate([middle] * (width // middle.shape[1]), axis=1)

    @pl.loop(0, rows // GROUP)
    def _(step):
        lanes = pl.ds(pl.multiple_of(step * width, LANES), width)
        values = add_update(own, other, stream, gate, out_weights, middle_factor, lanes)
        both[...] = values.T.reshape(GROUP, 2 * cols, channels)
        flat = both[:, pl.ds(pl.multiple_of(core * cols, GROUP), cols), :]
        flat = flat.reshape(GROUP * cols, channels)
        normed = layer_norm(flat, final_gain[...], 1).astype(BF16)
        expanded = jnp.dot(normed, expand[...], preferred_element_type=F32)
        expanded = jnp.maximum(expanded, 0.0).astype(BF16)
        out = flat + jnp.dot(expanded, shrink[...], preferred_element_type=F32)
        result[pl.ds(step * GROUP, GROUP)] = out.astype(BF16).reshape(GROUP, cols, channels)


def call(kernel, outs, scratch, args, scalars=1, flops=0):
    in_specs = [pl.BlockSpec(memory_space=pltpu.SMEM)] * scalars
    in_specs += [pl.BlockSpec(memory_space=pltpu.VMEM)] * (len(args) - scalars)
    moved = sum(a.size * a.dtype.itemsize for a in (*args, *outs))
    return pl.pallas_call(
        kernel,
        out_shape=outs,
        in_specs=in_specs,
        out_specs=[pl.BlockSpec(memory_space=pltpu.VMEM)] * len(outs),
        scratch_shapes=scratch,
        compiler_params=pltpu.CompilerParams(vmem_limit_bytes=40 * 1024 * 1024),
        cost_estimate=pl.CostEstimate(flops=flops, bytes_accessed=moved, transcendentals=0),
    )(*args)


def to_chip(value, distance):
    if distance == 0:
        return value
    pairs = [(device, device ^ (2 * distance)) for device in range(16)]
    return lax.ppermute(value, CHIPS, pairs)


def swap_cores(value):
    return lax.ppermute(value, "pair", [(0, 1), (1, 0)])


FAR_FIRST = (4, 5, 6, 7, 2, 3, 1, 0)


def chip_device(
    pair_input,
    residue_mask,
    entry_gain,
    input_weight,
    middle_gain,
    output_weight,
    final_gain,
    expand_weight,
    shrink_weight,
):
    rows, cols, channels = pair_input.shape
    hidden = output_weight.shape[1]
    width = 2 * cols
    pairs = rows * width
    wide = GROUP * width
    dap, sub, core = lax.axis_index("dap"), lax.axis_index("sub"), lax.axis_index("pair")
    meta = jnp.stack([core, dap * 2 + sub]).astype(jnp.int32)
    other_input = swap_cores(pair_input)
    mask_values = residue_mask.astype(F32)
    row_mask = lax.dynamic_slice_in_dim(mask_values, dap * rows, rows)
    col_mask = lax.dynamic_slice_in_dim(mask_values, sub * width, width)
    mask = (row_mask[:, None] * col_mask[None, :]).reshape(1, pairs)
    shape = jax.ShapeDtypeStruct
    flat32, flat16 = shape((channels, pairs), F32), shape((channels, pairs), BF16)
    quarter, eighth = hidden // 8, hidden // 16

    stream, normed, *messages = call(
        first_kernel,
        [flat32, flat16] + [shape((2 * quarter, pairs), BF16)] * 4 + [shape((quarter, pairs), BF16)] * 4,
        [pltpu.VMEM((rows, width, channels), F32), pltpu.VMEM((5 * hidden, channels), F32)],
        (meta, pair_input, other_input, mask, entry_gain, input_weight),
    )
    arrived = {k: to_chip(messages[k], k) for k in FAR_FIRST}
    (gate,) = call(
        functools.partial(gate_kernel, update=0), [flat32], [], (normed, input_weight), 0
    )
    sums = call(
        functools.partial(outgoing_kernel, rows=rows, width=width),
        [shape((quarter, pairs), BF16)] * 4,
        [
            pltpu.VMEM((2, quarter * 2 * rows, LANES), F32),
            pltpu.VMEM((2, quarter * 4 * rows, LANES), F32),
            pltpu.VMEM((2, quarter * 2 * rows, LANES), F32),
        ],
        (meta, *[arrived[k] for k in range(8)]),
    )
    returned = {k: to_chip(sums[k], k) for k in (2, 3, 1, 0)}
    own = jnp.concatenate([returned[k] for k in range(4)], axis=0)
    other = swap_cores(own)
    stream, normed, *messages = call(
        functools.partial(second_kernel, width=wide),
        [flat32, flat16] + [shape((2 * eighth, pairs), BF16)] * 8,
        [
            pltpu.VMEM((5 * hidden, channels), F32),
            pltpu.VMEM((hidden, channels), F32),
            pltpu.VMEM((hidden, LANES), F32),
        ],
        (meta, own, other, stream, gate, mask, entry_gain, input_weight, middle_gain, output_weight),
    )
    arrived = {k: to_chip(messages[k], k) for k in FAR_FIRST}
    (gate,) = call(
        functools.partial(gate_kernel, update=1), [flat32], [], (normed, input_weight), 0
    )
    sums = call(
        functools.partial(incoming_kernel, rows=rows, width=width),
        [shape((eighth, pairs), BF16)] * 8,
        [
            pltpu.VMEM((2, eighth * 4 * rows, LANES), F32),
            pltpu.VMEM((2, eighth * 4 * rows, LANES), F32),
            pltpu.VMEM((2, eighth * 2 * LANES, LANES), F32),
        ],
        (meta, *[arrived[k] for k in range(8)]),
    )
    returned = {k: to_chip(sums[k], k) for k in FAR_FIRST}
    own = jnp.concatenate([returned[k] for k in range(8)], axis=0)
    other = swap_cores(own)
    (result,) = call(
        functools.partial(last_kernel, width=wide),
        [shape((rows, cols, channels), BF16)],
        [
            pltpu.VMEM((hidden, channels), F32),
            pltpu.VMEM((hidden, LANES), F32),
            pltpu.VMEM((GROUP, width, channels), F32),
        ],
        (
            meta, own, other, stream, gate, middle_gain, output_weight,
            final_gain.reshape(1, channels), expand_weight, shrink_weight,
        ),
    )
    return result


def by_chips(mesh, pair_input, output_weight):
    sizes = dict(mesh.shape)
    rows = pair_input.shape[0] // (sizes["grp"] * sizes["dap"])
    cols = pair_input.shape[1] // (sizes["sub"] * sizes["pair"])
    return (
        (sizes["dap"], sizes["sub"], sizes["pair"]) == (4, 2, 2)
        and pair_input.shape[2] == LANES
        and output_weight.shape[1] == LANES
        and rows == cols
        and rows % GROUP == 0
        and 2 * cols <= LANES
        and GROUP * 2 * cols % LANES == 0
    )


def solution(mesh):
    placed = (P(("grp", "dap"), ("sub", "pair"), None), P("grp"), P(), P(), P(), P(), P(), P(), P())

    def run(*args):
        fits = by_chips(mesh, args[0], args[5])
        return jax.shard_map(
            chip_device if fits else general_device,
            mesh=mesh,
            in_specs=placed,
            out_specs=P(("grp", "dap"), ("sub", "pair"), None),
            check_vma=False,
        )(*args)

    return run
```

profile of v0, /device:TPU:0, one launch (start us, length us, event | category | flops | bytes accessed | tf_op | source)
XLA Modules:
  0.0 105.7 jit_solution(17431805738573008031)
XLA Ops:
  0.0 0.5 collective-permute-start
  0.5 0.7 convert_element_type.3
  1.5 0.5 collective-permute-done.other
  2.0 1.0 copy-done
  3.0 1.0 copy-done.2
  4.0 0.7 copy-done.6
  4.7 2.9 %shard_map.91 = (f32[128,3200]{1,0:T(8,128)S(1)}, bf16[128,3200]{1,0:T(8,128)(2,1)S(1)}, bf16[32,3200]{1,0:T(8,128)(2,1)S(1)}, bf16[32,3200]{1,0:T(8,128)(2,1)S(...) custom-call(s32[2]{0:T(128)S(1)} %pad_add_fusion.meta, ...), custom_call_target="tpu_custom_call" | custom-call | bytes 4847112 | tf_op jit(solution)/shard_map/pallas_call | solution.py:409
  7.6 4.0 %collective-permute-start.4 = (bf16[16,3200]{1,0:T(8,128)(2,1)S(1)}, bf16[16,3200]{1,0:T(8,128)(2,1)S(1)}, u32[]{:S(2)}, u32[]{:S(2)}) collective-permute-start(bf16[16,3200]{1,0:T(8,128)(2,1)S(1)} %get-tuple-element.41), channel_id=1, source_target_pairs={{0,8},{1,9},{2,10},{3,11},{4,12},{5,13},{6,14},{7,15},{8,0},{9,1},... | collective-permute-start | bytes 307208 | tf_op jit(solution)/shard_map/ppermute | solution.py:424
  11.6 1.2 %collective-permute-start.5 = (bf16[16,3200]{1,0:T(8,128)(2,1)S(1)}, bf16[16,3200]{1,0:T(8,128)(2,1)S(1)}, u32[]{:S(2)}, u32[]{:S(2)}) collective-permute-start(bf16[16,3200]{1,0:T(8,128)(2,1)S(1)} %get-tuple-element.42), channel_id=1, source_target_pairs={{0,10},{1,11},{2,8},{3,9},{4,14},{5,15},{6,12},{7,13},{8,2},{9,3},... | collective-permute-start | bytes 307208 | tf_op jit(solution)/shard_map/ppermute | solution.py:424
  12.8 0.3 collective-permute-start.1
  13.1 1.8 %collective-permute-start.2 = (bf16[32,3200]{1,0:T(8,128)(2,1)S(1)}, bf16[32,3200]{1,0:T(8,128)(2,1)S(1)}, u32[]{:S(2)}, u32[]{:S(2)}) collective-permute-start(bf16[32,3200]{1,0:T(8,128)(2,1)S(1)} %get-tuple-element.39), channel_id=1, source_target_pairs={{0,4},{1,5},{2,6},{3,7},{4,0},{5,1},{6,2},{7,3},{8,12},{9,13},{10,... | collective-permute-start | bytes 614408 | tf_op jit(solution)/shard_map/ppermute | solution.py:424
  14.9 1.4 %collective-permute-start.3 = (bf16[32,3200]{1,0:T(8,128)(2,1)S(1)}, bf16[32,3200]{1,0:T(8,128)(2,1)S(1)}, u32[]{:S(2)}, u32[]{:S(2)}) collective-permute-start(bf16[32,3200]{1,0:T(8,128)(2,1)S(1)} %get-tuple-element.40), channel_id=1, source_target_pairs={{0,6},{1,7},{2,4},{3,5},{4,2},{5,3},{6,0},{7,1},{8,14},{9,15},{10,... | collective-permute-start | bytes 614408 | tf_op jit(solution)/shard_map/ppermute | solution.py:424
  16.3 2.8 %collective-permute-done.4.refs_4_ = bf16[16,3200]{1,0:T(8,128)(2,1)S(1)} collective-permute-done((bf16[16,3200]{1,0:T(8,128)(2,1)S(1)}, bf16[16,3200]{1,0:T(8,128)(2,1)S(1)}, u32[]{:S(2)}, u32[]{:S(2)}) %collective-permute-start.4) | collective-permute-done | bytes 102432 | tf_op jit(solution)/shard_map/ppermute | solution.py:424
  19.1 3.7 %collective-permute-start.6 = (bf16[16,3200]{1,0:T(8,128)(2,1)S(1)}, bf16[16,3200]{1,0:T(8,128)(2,1)S(1)}, u32[]{:S(2)}, u32[]{:S(2)}) collective-permute-start(bf16[16,3200]{1,0:T(8,128)(2,1)S(1)} %get-tuple-element.43), channel_id=1, source_target_pairs={{0,12},{1,13},{2,14},{3,15},{4,8},{5,9},{6,10},{7,11},{8,4},{9,5},... | collective-permute-start | bytes 307208 | tf_op jit(solution)/shard_map/ppermute | solution.py:424
  22.9 3.0 %collective-permute-start.7 = (bf16[16,3200]{1,0:T(8,128)(2,1)S(1)}, bf16[16,3200]{1,0:T(8,128)(2,1)S(1)}, u32[]{:S(2)}, u32[]{:S(2)}) collective-permute-start(bf16[16,3200]{1,0:T(8,128)(2,1)S(1)} %get-tuple-element.44), channel_id=1, source_target_pairs={{0,14},{1,15},{2,12},{3,13},{4,10},{5,11},{6,8},{7,9},{8,6},{9,7},... | collective-permute-start | bytes 307208 | tf_op jit(solution)/shard_map/ppermute | solution.py:424
  25.9 5.4 %collective-permute-done.6.refs_6_ = bf16[16,3200]{1,0:T(8,128)(2,1)S(1)} collective-permute-done((bf16[16,3200]{1,0:T(8,128)(2,1)S(1)}, bf16[16,3200]{1,0:T(8,128)(2,1)S(1)}, u32[]{:S(2)}, u32[]{:S(2)}) %collective-permute-start.6) | collective-permute-done | bytes 102432 | tf_op jit(solution)/shard_map/ppermute | solution.py:424
  31.3 1.0 collective-permute-done.7.refs_7_
  32.3 0.4 collective-permute-done.3.refs_3_
  32.7 5.4 %shard_map.92 = (bf16[16,3200]{1,0:T(8,128)(2,1)S(1)}, bf16[16,3200]{1,0:T(8,128)(2,1)S(1)}, bf16[16,3200]{1,0:T(8,128)(2,1)S(1)}, bf16[16,3200]{1,0:T(8,128)(2,1)S(1)}) custom-call(s32[2]{0:T(128)S(1)} %pad_add_fusion.meta, bf16[32,3200]{1,0:T(8,128)(2,1)S(1)} %get-tuple-element.37.refs_0_, bf16[32,3200]{1,0:T(8,128)(2,1)S(1)} %collective-permute-done.1.refs_1_, ...), custom_call_target="tpu_custom_call" | custom-call | bytes 1638408 | tf_op jit(solution)/shard_map/pallas_call | solution.py:409
  38.1 1.3 %collective-permute-start.8 = (bf16[16,3200]{1,0:T(8,128)(2,1)S(1)}, bf16[16,3200]{1,0:T(8,128)(2,1)S(1)}, u32[]{:S(2)}, u32[]{:S(2)}) collective-permute-start(bf16[16,3200]{1,0:T(8,128)(2,1)S(1)} %get-tuple-element.46), channel_id=1, source_target_pairs={{0,2},{1,3},{2,0},{3,1},{4,6},{5,7},{6,4},{7,5},{8,10},{9,11},{10,... | collective-permute-start | bytes 307208 | tf_op jit(solution)/shard_map/ppermute | solution.py:424
  39.4 2.3 %collective-permute-start.10 = (bf16[16,3200]{1,0:T(8,128)(2,1)S(1)}, bf16[16,3200]{1,0:T(8,128)(2,1)S(1)}, u32[]{:S(2)}, u32[]{:S(2)}) collective-permute-start(bf16[16,3200]{1,0:T(8,128)(2,1)S(1)} %get-tuple-element.48), channel_id=1, source_target_pairs={{0,6},{1,7},{2,4},{3,5},{4,2},{5,3},{6,0},{7,1},{8,14},{9,15},{10,... | collective-permute-start | bytes 307208 | tf_op jit(solution)/shard_map/ppermute | solution.py:424
  41.6 2.3 %collective-permute-done.8 = bf16[16,3200]{1,0:T(8,128)(2,1)S(1)} collective-permute-done((bf16[16,3200]{1,0:T(8,128)(2,1)S(1)}, bf16[16,3200]{1,0:T(8,128)(2,1)S(1)}, u32[]{:S(2)}, u32[]{:S(2)}) %collective-permute-start.8) | collective-permute-done | bytes 102432 | tf_op jit(solution)/shard_map/ppermute | solution.py:424
  43.9 0.1 collective-permute-done.9
  44.1 1.3 %collective-permute-done.10 = bf16[16,3200]{1,0:T(8,128)(2,1)S(1)} collective-permute-done((bf16[16,3200]{1,0:T(8,128)(2,1)S(1)}, bf16[16,3200]{1,0:T(8,128)(2,1)S(1)}, u32[]{:S(2)}, u32[]{:S(2)}) %collective-permute-start.10) | collective-permute-done | bytes 102432 | tf_op jit(solution)/shard_map/ppermute | solution.py:424
  45.5 0.4 shard_map.93.gate
  45.9 1.3 %collective-permute-done.11.other = bf16[64,3200]{1,0:T(8,128)(2,1)S(1)} collective-permute-done((bf16[64,3200]{1,0:T(8,128)(2,1)S(1)}, bf16[64,3200]{1,0:T(8,128)(2,1)S(1)}, u32[]{:S(2)}, u32[]{:S(2)}) %collective-permute-start.11) | collective-permute-done | bytes 409632 | tf_op jit(solution)/shard_map/ppermute | solution.py:428
  47.2 3.7 %shard_map.94 = (f32[128,3200]{1,0:T(8,128)S(1)}, bf16[128,3200]{1,0:T(8,128)(2,1)S(1)}, bf16[16,3200]{1,0:T(8,128)(2,1)S(1)}, bf16[16,3200]{1,0:T(8,128)(2,1)S(...) custom-call(s32[2]{0:T(128)S(1)} %pad_add_fusion.meta, ...), custom_call_target="tpu_custom_call" | custom-call | bytes 7780872 | tf_op jit(solution)/shard_map/pallas_call | solution.py:409
  50.9 1.3 %collective-permute-start.12 = (bf16[16,3200]{1,0:T(8,128)(2,1)S(1)}, bf16[16,3200]{1,0:T(8,128)(2,1)S(1)}, u32[]{:S(2)}, u32[]{:S(2)}) collective-permute-start(bf16[16,3200]{1,0:T(8,128)(2,1)S(1)} %get-tuple-element.52), channel_id=1, source_target_pairs={{0,2},{1,3},{2,0},{3,1},{4,6},{5,7},{6,4},{7,5},{8,10},{9,11},{10,... | collective-permute-start | bytes 307208 | tf_op jit(solution)/shard_map/ppermute | solution.py:424
  52.2 1.1 %collective-permute-start.13 = (bf16[16,3200]{1,0:T(8,128)(2,1)S(1)}, bf16[16,3200]{1,0:T(8,128)(2,1)S(1)}, u32[]{:S(2)}, u32[]{:S(2)}) collective-permute-start(bf16[16,3200]{1,0:T(8,128)(2,1)S(1)} %get-tuple-element.53), channel_id=1, source_target_pairs={{0,4},{1,5},{2,6},{3,7},{4,0},{5,1},{6,2},{7,3},{8,12},{9,13},{10,... | collective-permute-start | bytes 307208 | tf_op jit(solution)/shard_map/ppermute | solution.py:424
  53.4 1.1 %collective-permute-start.14 = (bf16[16,3200]{1,0:T(8,128)(2,1)S(1)}, bf16[16,3200]{1,0:T(8,128)(2,1)S(1)}, u32[]{:S(2)}, u32[]{:S(2)}) collective-permute-start(bf16[16,3200]{1,0:T(8,128)(2,1)S(1)} %get-tuple-element.54), channel_id=1, source_target_pairs={{0,6},{1,7},{2,4},{3,5},{4,2},{5,3},{6,0},{7,1},{8,14},{9,15},{10,... | collective-permute-start | bytes 307208 | tf_op jit(solution)/shard_map/ppermute | solution.py:424
  54.5 4.0 %collective-permute-start.15 = (bf16[16,3200]{1,0:T(8,128)(2,1)S(1)}, bf16[16,3200]{1,0:T(8,128)(2,1)S(1)}, u32[]{:S(2)}, u32[]{:S(2)}) collective-permute-start(bf16[16,3200]{1,0:T(8,128)(2,1)S(1)} %get-tuple-element.55), channel_id=1, source_target_pairs={{0,8},{1,9},{2,10},{3,11},{4,12},{5,13},{6,14},{7,15},{8,0},{9,1},... | collective-permute-start | bytes 307208 | tf_op jit(solution)/shard_map/ppermute | solution.py:424
  58.5 0.9 collective-permute-start.16
  59.4 2.5 %collective-permute-start.17 = (bf16[16,3200]{1,0:T(8,128)(2,1)S(1)}, bf16[16,3200]{1,0:T(8,128)(2,1)S(1)}, u32[]{:S(2)}, u32[]{:S(2)}) collective-permute-start(bf16[16,3200]{1,0:T(8,128)(2,1)S(1)} %get-tuple-element.57), channel_id=1, source_target_pairs={{0,12},{1,13},{2,14},{3,15},{4,8},{5,9},{6,10},{7,11},{8,4},{9,5},... | collective-permute-start | bytes 307208 | tf_op jit(solution)/shard_map/ppermute | solution.py:424
  61.9 1.7 %collective-permute-start.18 = (bf16[16,3200]{1,0:T(8,128)(2,1)S(1)}, bf16[16,3200]{1,0:T(8,128)(2,1)S(1)}, u32[]{:S(2)}, u32[]{:S(2)}) collective-permute-start(bf16[16,3200]{1,0:T(8,128)(2,1)S(1)} %get-tuple-element.58), channel_id=1, source_target_pairs={{0,14},{1,15},{2,12},{3,13},{4,10},{5,11},{6,8},{7,9},{8,6},{9,7},... | collective-permute-start | bytes 307208 | tf_op jit(solution)/shard_map/ppermute | solution.py:424
  63.6 10.1 %collective-permute-done.16.refs_5_ = bf16[16,3200]{1,0:T(8,128)(2,1)S(1)} collective-permute-done((bf16[16,3200]{1,0:T(8,128)(2,1)S(1)}, bf16[16,3200]{1,0:T(8,128)(2,1)S(1)}, u32[]{:S(2)}, u32[]{:S(2)}) %collective-permute-start.16) | collective-permute-done | bytes 102432 | tf_op jit(solution)/shard_map/ppermute | solution.py:424
  73.7 5.5 %shard_map.95 = (bf16[8,3200]{1,0:T(8,128)(2,1)S(1)}, bf16[8,3200]{1,0:T(8,128)(2,1)S(1)}, bf16[8,3200]{1,0:T(8,128)(2,1)S(1)}, bf16[8,3200]{1,0:T(8,128)(2,1)S(...) custom-call(s32[2]{0:T(128)S(1)} %pad_add_fusion.meta, ...), custom_call_target="tpu_custom_call" | custom-call | bytes 1228808 | tf_op jit(solution)/shard_map/pallas_call | solution.py:409
  79.2 1.6 %collective-permute-start.19 = (bf16[8,3200]{1,0:T(8,128)(2,1)S(1)}, bf16[8,3200]{1,0:T(8,128)(2,1)S(1)}, u32[]{:S(2)}, u32[]{:S(2)}) collective-permute-start(bf16[8,3200]{1,0:T(8,128)(2,1)S(1)} %get-tuple-element.60), channel_id=1, source_target_pairs={{0,2},{1,3},{2,0},{3,1},{4,6},{5,7},{6,4},{7,5},{8,10},{9,11},{10,... | collective-permute-start | bytes 153608 | tf_op jit(solution)/shard_map/ppermute | solution.py:424
  80.8 3.9 %collective-permute-start.20 = (bf16[8,3200]{1,0:T(8,128)(2,1)S(1)}, bf16[8,3200]{1,0:T(8,128)(2,1)S(1)}, u32[]{:S(2)}, u32[]{:S(2)}) collective-permute-start(bf16[8,3200]{1,0:T(8,128)(2,1)S(1)} %get-tuple-element.61), channel_id=1, source_target_pairs={{0,4},{1,5},{2,6},{3,7},{4,0},{5,1},{6,2},{7,3},{8,12},{9,13},{10,... | collective-permute-start | bytes 153608 | tf_op jit(solution)/shard_map/ppermute | solution.py:424
  84.7 0.3 collective-permute-start.21
  84.9 2.7 %collective-permute-start.22 = (bf16[8,3200]{1,0:T(8,128)(2,1)S(1)}, bf16[8,3200]{1,0:T(8,128)(2,1)S(1)}, u32[]{:S(2)}, u32[]{:S(2)}) collective-permute-start(bf16[8,3200]{1,0:T(8,128)(2,1)S(1)} %get-tuple-element.63), channel_id=1, source_target_pairs={{0,8},{1,9},{2,10},{3,11},{4,12},{5,13},{6,14},{7,15},{8,0},{9,1},... | collective-permute-start | bytes 153608 | tf_op jit(solution)/shard_map/ppermute | solution.py:424
  87.6 0.9 collective-permute-start.23
  88.5 2.3 %collective-permute-start.24 = (bf16[8,3200]{1,0:T(8,128)(2,1)S(1)}, bf16[8,3200]{1,0:T(8,128)(2,1)S(1)}, u32[]{:S(2)}, u32[]{:S(2)}) collective-permute-start(bf16[8,3200]{1,0:T(8,128)(2,1)S(1)} %get-tuple-element.65), channel_id=1, source_target_pairs={{0,12},{1,13},{2,14},{3,15},{4,8},{5,9},{6,10},{7,11},{8,4},{9,5},... | collective-permute-start | bytes 153608 | tf_op jit(solution)/shard_map/ppermute | solution.py:424
  90.8 1.9 %collective-permute-start.25 = (bf16[8,3200]{1,0:T(8,128)(2,1)S(1)}, bf16[8,3200]{1,0:T(8,128)(2,1)S(1)}, u32[]{:S(2)}, u32[]{:S(2)}) collective-permute-start(bf16[8,3200]{1,0:T(8,128)(2,1)S(1)} %get-tuple-element.66), channel_id=1, source_target_pairs={{0,14},{1,15},{2,12},{3,13},{4,10},{5,11},{6,8},{7,9},{8,6},{9,7},... | collective-permute-start | bytes 153608 | tf_op jit(solution)/shard_map/ppermute | solution.py:424
  92.8 2.7 %collective-permute-done.23 = bf16[8,3200]{1,0:T(8,128)(2,1)S(1)} collective-permute-done((bf16[8,3200]{1,0:T(8,128)(2,1)S(1)}, bf16[8,3200]{1,0:T(8,128)(2,1)S(1)}, u32[]{:S(2)}, u32[]{:S(2)}) %collective-permute-start.23) | collective-permute-done | bytes 51232 | tf_op jit(solution)/shard_map/ppermute | solution.py:424
  95.5 2.2 %collective-permute-done.25 = bf16[8,3200]{1,0:T(8,128)(2,1)S(1)} collective-permute-done((bf16[8,3200]{1,0:T(8,128)(2,1)S(1)}, bf16[8,3200]{1,0:T(8,128)(2,1)S(1)}, u32[]{:S(2)}, u32[]{:S(2)}) %collective-permute-start.25) | collective-permute-done | bytes 51232 | tf_op jit(solution)/shard_map/ppermute | solution.py:424
  97.7 0.4 shard_map.96.gate
  98.2 1.3 %collective-permute-done.26.other = bf16[64,3200]{1,0:T(8,128)(2,1)S(1)} collective-permute-done((bf16[64,3200]{1,0:T(8,128)(2,1)S(1)}, bf16[64,3200]{1,0:T(8,128)(2,1)S(1)}, u32[]{:S(2)}, u32[]{:S(2)}) %collective-permute-start.26) | collective-permute-done | bytes 409632 | tf_op jit(solution)/shard_map/ppermute | solution.py:428
  99.5 6.2 %shard_map.97 = bf16[40,40,128]{2,1,0:T(8,128)(2,1)} custom-call(s32[2]{0:T(128)S(1)} %pad_add_fusion.meta, bf16[64,3200]{1,0:T(8,128)(2,1)S(1)} %constant_dynamic-update-slice_fusion.4.own, bf16[64,3200]{1,0:T(8,128)(2,1)S(1)} %collective-permute-done.26.other, f32[128,3200]{1,0:T(8,128)S(1)} %get-tuple-element.67.stream, f32[128,3200]{1,0:T(8,128)S(1)} %shard_map.96.gate, ...), custom_call_target="tpu_custom_call" | custom-call | bytes 4834824 | tf_op jit(solution)/shard_map/pallas_call | solution.py:409
  (49 shorter events, 0.7 us)
Async XLA Ops:
  0.0 2.0 %collective-permute-start = (bf16[40,40,128]{2,1,0:T(8,128)(2,1)}, bf16[40,40,128]{2,1,0:T(8,128)(2,1)S(1)}, u32[]{:S(2)}, u32[]{:S(2)}) collective-permute-start(bf16[40,40,128]{2,1,0:T(8,128)(2,1)} %own.1), channel_id=1, source_target_pairs={{0,1},{1,0},{2,3},{3,2},{4,5},{5,4},{6,7},{7,6},{8,9},{9,8},{10,11... | collective-permute-start | bytes 1228808 | tf_op jit(solution)/shard_map/ppermute | solution.py:428
  2.0 1.0 copy-start
  3.0 1.0 copy-start.2
  4.0 0.7 copy-start.6
  4.7 40.8 %copy-start.1 = (bf16[2,128,640]{2,1,0:T(8,128)(2,1)S(1)}, bf16[2,128,640]{2,1,0:T(8,128)(2,1)}, u32[]{:S(2)}) copy-start(bf16[2,128,640]{2,1,0:T(8,128)(2,1)} %weight.7) | copy-start | bytes 983044
  7.6 11.6 %collective-permute-start.4 = (bf16[16,3200]{1,0:T(8,128)(2,1)S(1)}, bf16[16,3200]{1,0:T(8,128)(2,1)S(1)}, u32[]{:S(2)}, u32[]{:S(2)}) collective-permute-start(bf16[16,3200]{1,0:T(8,128)(2,1)S(1)} %get-tuple-element.41), channel_id=1, source_target_pairs={{0,8},{1,9},{2,10},{3,11},{4,12},{5,13},{6,14},{7,15},{8,0},{9,1},... | collective-permute-start | bytes 307208 | tf_op jit(solution)/shard_map/ppermute | solution.py:424
  11.6 11.3 %collective-permute-start.5 = (bf16[16,3200]{1,0:T(8,128)(2,1)S(1)}, bf16[16,3200]{1,0:T(8,128)(2,1)S(1)}, u32[]{:S(2)}, u32[]{:S(2)}) collective-permute-start(bf16[16,3200]{1,0:T(8,128)(2,1)S(1)} %get-tuple-element.42), channel_id=1, source_target_pairs={{0,10},{1,11},{2,8},{3,9},{4,14},{5,15},{6,12},{7,13},{8,2},{9,3},... | collective-permute-start | bytes 307208 | tf_op jit(solution)/shard_map/ppermute | solution.py:424
  12.8 19.4 %collective-permute-start.1 = (bf16[32,3200]{1,0:T(8,128)(2,1)S(1)}, bf16[32,3200]{1,0:T(8,128)(2,1)S(1)}, u32[]{:S(2)}, u32[]{:S(2)}) collective-permute-start(bf16[32,3200]{1,0:T(8,128)(2,1)S(1)} %get-tuple-element.38), channel_id=1, source_target_pairs={{0,2},{1,3},{2,0},{3,1},{4,6},{5,7},{6,4},{7,5},{8,10},{9,11},{10,... | collective-permute-start | bytes 614408 | tf_op jit(solution)/shard_map/ppermute | solution.py:424
  13.1 19.1 %collective-permute-start.2 = (bf16[32,3200]{1,0:T(8,128)(2,1)S(1)}, bf16[32,3200]{1,0:T(8,128)(2,1)S(1)}, u32[]{:S(2)}, u32[]{:S(2)}) collective-permute-start(bf16[32,3200]{1,0:T(8,128)(2,1)S(1)} %get-tuple-element.39), channel_id=1, source_target_pairs={{0,4},{1,5},{2,6},{3,7},{4,0},{5,1},{6,2},{7,3},{8,12},{9,13},{10,... | collective-permute-start | bytes 614408 | tf_op jit(solution)/shard_map/ppermute | solution.py:424
  14.9 17.7 %collective-permute-start.3 = (bf16[32,3200]{1,0:T(8,128)(2,1)S(1)}, bf16[32,3200]{1,0:T(8,128)(2,1)S(1)}, u32[]{:S(2)}, u32[]{:S(2)}) collective-permute-start(bf16[32,3200]{1,0:T(8,128)(2,1)S(1)} %get-tuple-element.40), channel_id=1, source_target_pairs={{0,6},{1,7},{2,4},{3,5},{4,2},{5,3},{6,0},{7,1},{8,14},{9,15},{10,... | collective-permute-start | bytes 614408 | tf_op jit(solution)/shard_map/ppermute | solution.py:424
  19.1 12.2 %collective-permute-start.6 = (bf16[16,3200]{1,0:T(8,128)(2,1)S(1)}, bf16[16,3200]{1,0:T(8,128)(2,1)S(1)}, u32[]{:S(2)}, u32[]{:S(2)}) collective-permute-start(bf16[16,3200]{1,0:T(8,128)(2,1)S(1)} %get-tuple-element.43), channel_id=1, source_target_pairs={{0,12},{1,13},{2,14},{3,15},{4,8},{5,9},{6,10},{7,11},{8,4},{9,5},... | collective-permute-start | bytes 307208 | tf_op jit(solution)/shard_map/ppermute | solution.py:424
  22.9 9.4 %collective-permute-start.7 = (bf16[16,3200]{1,0:T(8,128)(2,1)S(1)}, bf16[16,3200]{1,0:T(8,128)(2,1)S(1)}, u32[]{:S(2)}, u32[]{:S(2)}) collective-permute-start(bf16[16,3200]{1,0:T(8,128)(2,1)S(1)} %get-tuple-element.44), channel_id=1, source_target_pairs={{0,14},{1,15},{2,12},{3,13},{4,10},{5,11},{6,8},{7,9},{8,6},{9,7},... | collective-permute-start | bytes 307208 | tf_op jit(solution)/shard_map/ppermute | solution.py:424
  38.1 5.8 %collective-permute-start.8 = (bf16[16,3200]{1,0:T(8,128)(2,1)S(1)}, bf16[16,3200]{1,0:T(8,128)(2,1)S(1)}, u32[]{:S(2)}, u32[]{:S(2)}) collective-permute-start(bf16[16,3200]{1,0:T(8,128)(2,1)S(1)} %get-tuple-element.46), channel_id=1, source_target_pairs={{0,2},{1,3},{2,0},{3,1},{4,6},{5,7},{6,4},{7,5},{8,10},{9,11},{10,... | collective-permute-start | bytes 307208 | tf_op jit(solution)/shard_map/ppermute | solution.py:424
  39.4 4.7 %collective-permute-start.9 = (bf16[16,3200]{1,0:T(8,128)(2,1)S(1)}, bf16[16,3200]{1,0:T(8,128)(2,1)S(1)}, u32[]{:S(2)}, u32[]{:S(2)}) collective-permute-start(bf16[16,3200]{1,0:T(8,128)(2,1)S(1)} %get-tuple-element.47), channel_id=1, source_target_pairs={{0,4},{1,5},{2,6},{3,7},{4,0},{5,1},{6,2},{7,3},{8,12},{9,13},{10,... | collective-permute-start | bytes 307208 | tf_op jit(solution)/shard_map/ppermute | solution.py:424
  39.4 6.0 %collective-permute-start.10 = (bf16[16,3200]{1,0:T(8,128)(2,1)S(1)}, bf16[16,3200]{1,0:T(8,128)(2,1)S(1)}, u32[]{:S(2)}, u32[]{:S(2)}) collective-permute-start(bf16[16,3200]{1,0:T(8,128)(2,1)S(1)} %get-tuple-element.48), channel_id=1, source_target_pairs={{0,6},{1,7},{2,4},{3,5},{4,2},{5,3},{6,0},{7,1},{8,14},{9,15},{10,... | collective-permute-start | bytes 307208 | tf_op jit(solution)/shard_map/ppermute | solution.py:424
  43.9 3.3 %copy-start.3 = (bf16[2,128,128]{2,1,0:T(8,128)(2,1)S(1)}, bf16[2,128,128]{2,1,0:T(8,128)(2,1)}, u32[]{:S(2)}) copy-start(bf16[2,128,128]{2,1,0:T(8,128)(2,1)} %out_weight.3) | copy-start | bytes 196612
  43.9 3.3 %copy-start.7 = (f32[2,128]{1,0:T(2,128)S(1)}, f32[2,128]{1,0:T(2,128)}, u32[]{:S(2)}) copy-start(f32[2,128]{1,0:T(2,128)} %middle_gain.3) | copy-start | bytes 3076
  45.4 1.8 %collective-permute-start.11 = (bf16[64,3200]{1,0:T(8,128)(2,1)S(1)}, bf16[64,3200]{1,0:T(8,128)(2,1)S(1)}, u32[]{:S(2)}, u32[]{:S(2)}) collective-permute-start(bf16[64,3200]{1,0:T(8,128)(2,1)S(1)} %constant_dynamic-update-slice_fusion.own), channel_id=1, source_target_pairs={{0,1},{1,0},{2,3},{3,2},{4,5},{5,4},{6,7},{7,6},{8,9},{9,8},{10,11... | collective-permute-start | bytes 1228808 | tf_op jit(solution)/shard_map/ppermute | solution.py:428
  50.9 8.5 %collective-permute-start.12 = (bf16[16,3200]{1,0:T(8,128)(2,1)S(1)}, bf16[16,3200]{1,0:T(8,128)(2,1)S(1)}, u32[]{:S(2)}, u32[]{:S(2)}) collective-permute-start(bf16[16,3200]{1,0:T(8,128)(2,1)S(1)} %get-tuple-element.52), channel_id=1, source_target_pairs={{0,2},{1,3},{2,0},{3,1},{4,6},{5,7},{6,4},{7,5},{8,10},{9,11},{10,... | collective-permute-start | bytes 307208 | tf_op jit(solution)/shard_map/ppermute | solution.py:424
  52.2 9.7 %collective-permute-start.13 = (bf16[16,3200]{1,0:T(8,128)(2,1)S(1)}, bf16[16,3200]{1,0:T(8,128)(2,1)S(1)}, u32[]{:S(2)}, u32[]{:S(2)}) collective-permute-start(bf16[16,3200]{1,0:T(8,128)(2,1)S(1)} %get-tuple-element.53), channel_id=1, source_target_pairs={{0,4},{1,5},{2,6},{3,7},{4,0},{5,1},{6,2},{7,3},{8,12},{9,13},{10,... | collective-permute-start | bytes 307208 | tf_op jit(solution)/shard_map/ppermute | solution.py:424
  53.4 10.3 %collective-permute-start.14 = (bf16[16,3200]{1,0:T(8,128)(2,1)S(1)}, bf16[16,3200]{1,0:T(8,128)(2,1)S(1)}, u32[]{:S(2)}, u32[]{:S(2)}) collective-permute-start(bf16[16,3200]{1,0:T(8,128)(2,1)S(1)} %get-tuple-element.54), channel_id=1, source_target_pairs={{0,6},{1,7},{2,4},{3,5},{4,2},{5,3},{6,0},{7,1},{8,14},{9,15},{10,... | collective-permute-start | bytes 307208 | tf_op jit(solution)/shard_map/ppermute | solution.py:424
  54.5 9.2 %collective-permute-start.15 = (bf16[16,3200]{1,0:T(8,128)(2,1)S(1)}, bf16[16,3200]{1,0:T(8,128)(2,1)S(1)}, u32[]{:S(2)}, u32[]{:S(2)}) collective-permute-start(bf16[16,3200]{1,0:T(8,128)(2,1)S(1)} %get-tuple-element.55), channel_id=1, source_target_pairs={{0,8},{1,9},{2,10},{3,11},{4,12},{5,13},{6,14},{7,15},{8,0},{9,1},... | collective-permute-start | bytes 307208 | tf_op jit(solution)/shard_map/ppermute | solution.py:424
  58.5 15.3 %collective-permute-start.16 = (bf16[16,3200]{1,0:T(8,128)(2,1)S(1)}, bf16[16,3200]{1,0:T(8,128)(2,1)S(1)}, u32[]{:S(2)}, u32[]{:S(2)}) collective-permute-start(bf16[16,3200]{1,0:T(8,128)(2,1)S(1)} %get-tuple-element.56), channel_id=1, source_target_pairs={{0,10},{1,11},{2,8},{3,9},{4,14},{5,15},{6,12},{7,13},{8,2},{9,3},... | collective-permute-start | bytes 307208 | tf_op jit(solution)/shard_map/ppermute | solution.py:424
  59.4 14.3 %collective-permute-start.17 = (bf16[16,3200]{1,0:T(8,128)(2,1)S(1)}, bf16[16,3200]{1,0:T(8,128)(2,1)S(1)}, u32[]{:S(2)}, u32[]{:S(2)}) collective-permute-start(bf16[16,3200]{1,0:T(8,128)(2,1)S(1)} %get-tuple-element.57), channel_id=1, source_target_pairs={{0,12},{1,13},{2,14},{3,15},{4,8},{5,9},{6,10},{7,11},{8,4},{9,5},... | collective-permute-start | bytes 307208 | tf_op jit(solution)/shard_map/ppermute | solution.py:424
  61.9 11.8 %collective-permute-start.18 = (bf16[16,3200]{1,0:T(8,128)(2,1)S(1)}, bf16[16,3200]{1,0:T(8,128)(2,1)S(1)}, u32[]{:S(2)}, u32[]{:S(2)}) collective-permute-start(bf16[16,3200]{1,0:T(8,128)(2,1)S(1)} %get-tuple-element.58), channel_id=1, source_target_pairs={{0,14},{1,15},{2,12},{3,13},{4,10},{5,11},{6,8},{7,9},{8,6},{9,7},... | collective-permute-start | bytes 307208 | tf_op jit(solution)/shard_map/ppermute | solution.py:424
  79.2 9.3 %collective-permute-start.19 = (bf16[8,3200]{1,0:T(8,128)(2,1)S(1)}, bf16[8,3200]{1,0:T(8,128)(2,1)S(1)}, u32[]{:S(2)}, u32[]{:S(2)}) collective-permute-start(bf16[8,3200]{1,0:T(8,128)(2,1)S(1)} %get-tuple-element.60), channel_id=1, source_target_pairs={{0,2},{1,3},{2,0},{3,1},{4,6},{5,7},{6,4},{7,5},{8,10},{9,11},{10,... | collective-permute-start | bytes 153608 | tf_op jit(solution)/shard_map/ppermute | solution.py:424
  80.8 10.1 %collective-permute-start.20 = (bf16[8,3200]{1,0:T(8,128)(2,1)S(1)}, bf16[8,3200]{1,0:T(8,128)(2,1)S(1)}, u32[]{:S(2)}, u32[]{:S(2)}) collective-permute-start(bf16[8,3200]{1,0:T(8,128)(2,1)S(1)} %get-tuple-element.61), channel_id=1, source_target_pairs={{0,4},{1,5},{2,6},{3,7},{4,0},{5,1},{6,2},{7,3},{8,12},{9,13},{10,... | collective-permute-start | bytes 153608 | tf_op jit(solution)/shard_map/ppermute | solution.py:424
  84.7 8.1 %collective-permute-start.21 = (bf16[8,3200]{1,0:T(8,128)(2,1)S(1)}, bf16[8,3200]{1,0:T(8,128)(2,1)S(1)}, u32[]{:S(2)}, u32[]{:S(2)}) collective-permute-start(bf16[8,3200]{1,0:T(8,128)(2,1)S(1)} %get-tuple-element.62), channel_id=1, source_target_pairs={{0,6},{1,7},{2,4},{3,5},{4,2},{5,3},{6,0},{7,1},{8,14},{9,15},{10,... | collective-permute-start | bytes 153608 | tf_op jit(solution)/shard_map/ppermute | solution.py:424
  84.9 7.9 %collective-permute-start.22 = (bf16[8,3200]{1,0:T(8,128)(2,1)S(1)}, bf16[8,3200]{1,0:T(8,128)(2,1)S(1)}, u32[]{:S(2)}, u32[]{:S(2)}) collective-permute-start(bf16[8,3200]{1,0:T(8,128)(2,1)S(1)} %get-tuple-element.63), channel_id=1, source_target_pairs={{0,8},{1,9},{2,10},{3,11},{4,12},{5,13},{6,14},{7,15},{8,0},{9,1},... | collective-permute-start | bytes 153608 | tf_op jit(solution)/shard_map/ppermute | solution.py:424
  87.6 7.9 %collective-permute-start.23 = (bf16[8,3200]{1,0:T(8,128)(2,1)S(1)}, bf16[8,3200]{1,0:T(8,128)(2,1)S(1)}, u32[]{:S(2)}, u32[]{:S(2)}) collective-permute-start(bf16[8,3200]{1,0:T(8,128)(2,1)S(1)} %get-tuple-element.64), channel_id=1, source_target_pairs={{0,10},{1,11},{2,8},{3,9},{4,14},{5,15},{6,12},{7,13},{8,2},{9,3},... | collective-permute-start | bytes 153608 | tf_op jit(solution)/shard_map/ppermute | solution.py:424
  88.5 7.0 %collective-permute-start.24 = (bf16[8,3200]{1,0:T(8,128)(2,1)S(1)}, bf16[8,3200]{1,0:T(8,128)(2,1)S(1)}, u32[]{:S(2)}, u32[]{:S(2)}) collective-permute-start(bf16[8,3200]{1,0:T(8,128)(2,1)S(1)} %get-tuple-element.65), channel_id=1, source_target_pairs={{0,12},{1,13},{2,14},{3,15},{4,8},{5,9},{6,10},{7,11},{8,4},{9,5},... | collective-permute-start | bytes 153608 | tf_op jit(solution)/shard_map/ppermute | solution.py:424
  90.8 6.9 %collective-permute-start.25 = (bf16[8,3200]{1,0:T(8,128)(2,1)S(1)}, bf16[8,3200]{1,0:T(8,128)(2,1)S(1)}, u32[]{:S(2)}, u32[]{:S(2)}) collective-permute-start(bf16[8,3200]{1,0:T(8,128)(2,1)S(1)} %get-tuple-element.66), channel_id=1, source_target_pairs={{0,14},{1,15},{2,12},{3,13},{4,10},{5,11},{6,8},{7,9},{8,6},{9,7},... | collective-permute-start | bytes 153608 | tf_op jit(solution)/shard_map/ppermute | solution.py:424
  92.8 6.7 %copy-start.4 = (bf16[128,512]{1,0:T(8,128)(2,1)S(1)}, bf16[128,512]{1,0:T(8,128)(2,1)}, u32[]{:S(2)}) copy-start(bf16[128,512]{1,0:T(8,128)(2,1)} %expand.1) | copy-start | bytes 393220
  92.8 6.7 %copy-start.5 = (bf16[512,128]{1,0:T(8,128)(2,1)S(1)}, bf16[512,128]{1,0:T(8,128)(2,1)}, u32[]{:S(2)}) copy-start(bf16[512,128]{1,0:T(8,128)(2,1)} %shrink.1) | copy-start | bytes 393220
  92.8 6.7 %copy-start.8 = (f32[128]{0:T(128)S(1)}, f32[128]{0:T(128)}, u32[]{:S(2)}) copy-start(f32[128]{0:T(128)} %param.15) | copy-start | bytes 1540
  97.7 1.7 %collective-permute-start.26 = (bf16[64,3200]{1,0:T(8,128)(2,1)S(1)}, bf16[64,3200]{1,0:T(8,128)(2,1)S(1)}, u32[]{:S(2)}, u32[]{:S(2)}) collective-permute-start(bf16[64,3200]{1,0:T(8,128)(2,1)S(1)} %constant_dynamic-update-slice_fusion.4.own), channel_id=1, source_target_pairs={{0,1},{1,0},{2,3},{3,2},{4,5},{5,4},{6,7},{7,6},{8,9},{9,8},{10,11... | collective-permute-start | bytes 1228808 | tf_op jit(solution)/shard_map/ppermute | solution.py:428
where the time goes:
time: 106 us
  starting transfers between devices  45.9 us (43%)
  waiting for transfers between devices  31.3 us (30%)
  Pallas kernels  24.5 us (23%)
  local copies, waits for them, and re-layouts  3.06 us (3%)
    ppermute x24, starting transfers between devices, to_chip(): return lax.ppermute(value, CHIPS, pairs)  45.3 us
    ppermute x24, waiting for transfers between devices, to_chip(): return lax.ppermute(value, CHIPS, pairs)  28.2 us
    pallas_call x7, Pallas kernels, call(): pl.pallas_call(kernel, out_shape=outs, in_specs=in_specs, out_specs=[pl.B...  24.5 us
    ppermute x3, waiting for transfers between devices, swap_cores(): return lax.ppermute(value, 'pair', [(0, 1), (1, 0)])  3.08 us
    unnamed x28, local copies, waits for them, and re-layouts  2.79 us
  transfers between devices with their start and end apart: 27, of which 13 were waited for; matrix products, arithmetic and copies ran while one was open for 1% of the time, Pallas kernels for 1%

commit v1 on v0

--- a/solution.py
+++ b/solution.py
@@ -131,6 +131,18 @@
     return result.astype(jnp.bfloat16).reshape(row_count, col_count, channels)
 
 
+def aligned(start, size):
+    return start if isinstance(start, int) else pl.multiple_of(start, size)
+
+
+def steps(count):
+    def run(body):
+        for step in range(count):
+            body(step)
+
+    return run
+
+
 def sigmoid(values):
     return 0.5 * jnp.tanh(0.5 * values) + 0.5
 
@@ -183,7 +195,7 @@
 
 def pick_rows(table, starts, size):
     return jnp.concatenate(
-        [table[pl.ds(pl.multiple_of(start, GROUP), size), :] for start in starts], axis=0
+        [table[pl.ds(aligned(start, GROUP), size), :] for start in starts], axis=0
     )
 
 
@@ -220,16 +232,16 @@
     stream, normed_out, *messages, both, table = refs
     core = meta[0]
     rows, cols, channels = own.shape
-    both[:, pl.ds(pl.multiple_of(core * cols, GROUP), cols), :] = own[...].astype(F32)
-    both[:, pl.ds(pl.multiple_of((1 - core) * cols, GROUP), cols), :] = other[...].astype(F32)
+    both[:, pl.ds(aligned(core * cols, GROUP), cols), :] = own[...].astype(F32)
+    both[:, pl.ds(aligned((1 - core) * cols, GROUP), cols), :] = other[...].astype(F32)
     table[...] = weight[0].astype(F32).T
     weights = side_weights(table, meta, False)
     width = GROUP * 2 * cols
     factor = column_of(gain[0:1, :], width)
 
-    @pl.loop(0, rows // GROUP)
-    def _(step):
-        lanes = pl.ds(pl.multiple_of(step * width, LANES), width)
+    @steps(rows // GROUP)
+    def _(step):
+        lanes = pl.ds(aligned(step * width, LANES), width)
         values = both[pl.ds(step * GROUP, GROUP)].reshape(width, channels).T
         stream[:, lanes] = values
         normed = norm_rows(values, factor).astype(BF16)
@@ -245,16 +257,16 @@
 
 
 def outgoing_kernel(meta, *refs, rows, width):
-    messages, outs = refs[:8], refs[8:12]
+    messages, outs = dict(zip(SIDES_OUT, refs[:8])), refs[8:12]
     left, right, total = refs[12:]
     dap, sub = meta[1] >> 1, meta[1] & 1
     lane = lane_index()
     count = outs[0].shape[0]
     span = 2 * rows
 
-    @pl.loop(0, rows // GROUP)
-    def _(step):
-        lanes = pl.ds(pl.multiple_of(step * GROUP * width, LANES), GROUP * width)
+    @steps(rows // GROUP)
+    def _(step):
+        lanes = pl.ds(aligned(step * GROUP * width, LANES), GROUP * width)
         for k in range(8):
             values = messages[k][:, lanes].astype(F32)
             source = dap ^ (k >> 1)
@@ -271,20 +283,20 @@
                 for i, piece in enumerate(split_group(values[c : c + GROUP], width, lane)):
                     right[k & 1, pl.ds(c * span + begin + i, GROUP, stride=span), :] = piece
 
-    @pl.loop(0, count)
+    @steps(count)
     def _(c):
-        here = pl.ds(pl.multiple_of(c * span, GROUP), span)
+        here = pl.ds(aligned(c * span, GROUP), span)
         a = jnp.concatenate([left[0, here, :], left[1, here, :]], axis=1).astype(BF16)
         for half in range(2):
-            there = pl.ds(pl.multiple_of(half * (count * span) + c * span, GROUP), span)
+            there = pl.ds(aligned(half * (count * span) + c * span, GROUP), span)
             b = jnp.concatenate([right[0, there, :], right[1, there, :]], axis=1).astype(BF16)
             total[half, here, 0:width] = lax.dot_general(
                 a, b, (((1,), (1,)), ((), ())), preferred_element_type=F32
             )
 
-    @pl.loop(0, rows // GROUP)
-    def _(step):
-        lanes = pl.ds(pl.multiple_of(step * GROUP * width, LANES), GROUP * width)
+    @steps(rows // GROUP)
+    def _(step):
+        lanes = pl.ds(aligned(step * GROUP * width, LANES), GROUP * width)
         for k in range(4):
             begin = (k >> 1) * rows + step * GROUP
             joined = []
@@ -298,7 +310,7 @@
 
 
 def incoming_kernel(meta, *refs, rows, width):
-    messages, outs = refs[:8], refs[8:16]
+    messages, outs = dict(zip(SIDES_IN, refs[:8])), refs[8:16]
     left, right, total = refs[16:]
     dap, sub = meta[1] >> 1, meta[1] & 1
     lane = lane_index()
@@ -306,9 +318,9 @@
     span = 4 * rows
     tall = 2 * LANES
 
-    @pl.loop(0, rows // GROUP)
-    def _(step):
-        lanes = pl.ds(pl.multiple_of(step * GROUP * width, LANES), GROUP * width)
+    @steps(rows // GROUP)
+    def _(step):
+        lanes = pl.ds(aligned(step * GROUP * width, LANES), GROUP * width)
         for k in range(8):
             values = messages[k][:, lanes].astype(F32)
             begin = (k >> 1) * rows + step * GROUP
@@ -316,19 +328,19 @@
                 for i, piece in enumerate(split_group(part, width, lane)):
                     side[k & 1, pl.ds(begin + i, GROUP, stride=span), :] = piece
 
-    @pl.loop(0, count)
+    @steps(count)
     def _(c):
-        here = pl.ds(pl.multiple_of(c * span, GROUP), span)
+        here = pl.ds(aligned(c * span, GROUP), span)
         a = jnp.concatenate([left[0, here, :], left[1, here, :]], axis=1).astype(BF16)
         b = jnp.concatenate([right[0, here, :], right[1, here, :]], axis=1).astype(BF16)
         product = lax.dot_general(a, b, (((0,), (0,)), ((), ())), preferred_element_type=F32)
-        there = pl.ds(pl.multiple_of(c * tall, GROUP), tall)
+        there = pl.ds(aligned(c * tall, GROUP), tall)
         total[0, there, :] = product[:, :LANES]
         total[1, there, :] = product[:, LANES:]
 
-    @pl.loop(0, rows // GROUP)
-    def _(step):
-        lanes = pl.ds(pl.multiple_of(step * GROUP * width, LANES), GROUP * width)
+    @steps(rows // GROUP)
+    def _(step):
+        lanes = pl.ds(aligned(step * GROUP * width, LANES), GROUP * width)
         for k in range(8):
             target = dap ^ (k >> 1)
             begin = ((target >> 1) ^ sub) * LANES + (target & 1) * rows + step * GROUP
@@ -338,14 +350,14 @@
             outs[k][:, lanes] = join_group(pieces, width, lane).astype(BF16)
 
 
-def output_weights(table, square, gain, meta, count):
+def output_weights(table, square, gain, meta, order):
     core, chip = meta[0], meta[1]
     mine = table.shape[0] // 2
-    size = mine // count
+    size = mine // len(order)
     starts = [
-        side * mine + size * ((chip & (count - 1)) ^ k)
+        side * mine + size * ((chip & (len(order) - 1)) ^ k)
         for side in (core, 1 - core)
-        for k in range(count)
+        for k in order
     ]
     square[...] = jnp.broadcast_to(gain, square.shape).T
     return pick_rows(table, starts, size).T.astype(BF16), pick_rows(square, starts, size)
@@ -362,15 +374,15 @@
 ):
     stream_out, normed_out, *messages, table, out_table, square = refs
     out_table[...] = out_weight[0].astype(F32)
-    out_weights, middle = output_weights(out_table, square, middle_gain[0:1, :], meta, 4)
+    out_weights, middle = output_weights(out_table, square, middle_gain[0:1, :], meta, SUMS_OUT)
     table[...] = weight[1].astype(F32).T
     weights = side_weights(table, meta, True)
     middle_factor = jnp.concatenate([middle] * (width // middle.shape[1]), axis=1)
     factor = column_of(entry_gain[1:2, :], width)
 
-    @pl.loop(0, stream.shape[1] // width)
-    def _(step):
-        lanes = pl.ds(pl.multiple_of(step * width, LANES), width)
+    @steps(stream.shape[1] // width)
+    def _(step):
+        lanes = pl.ds(aligned(step * width, LANES), width)
         values = add_update(own, other, stream, gate, out_weights, middle_factor, lanes)
         stream_out[:, lanes] = values
         normed = norm_rows(values, factor).astype(BF16)
@@ -385,15 +397,15 @@
     core = meta[0]
     rows, cols, channels = result.shape
     out_table[...] = out_weight[1].astype(F32)
-    out_weights, middle = output_weights(out_table, square, middle_gain[1:2, :], meta, 8)
+    out_weights, middle = output_weights(out_table, square, middle_gain[1:2, :], meta, SUMS_IN)
     middle_factor = jnp.concatenate([middle] * (width // middle.shape[1]), axis=1)
 
-    @pl.loop(0, rows // GROUP)
-    def _(step):
-        lanes = pl.ds(pl.multiple_of(step * width, LANES), width)
+    @steps(rows // GROUP)
+    def _(step):
+        lanes = pl.ds(aligned(step * width, LANES), width)
         values = add_update(own, other, stream, gate, out_weights, middle_factor, lanes)
         both[...] = values.T.reshape(GROUP, 2 * cols, channels)
-        flat = both[:, pl.ds(pl.multiple_of(core * cols, GROUP), cols), :]
+        flat = both[:, pl.ds(aligned(core * cols, GROUP), cols), :]
         flat = flat.reshape(GROUP * cols, channels)
         normed = layer_norm(flat, final_gain[...], 1).astype(BF16)
         expanded = jnp.dot(normed, expand[...], preferred_element_type=F32)
@@ -428,7 +440,10 @@
     return lax.ppermute(value, "pair", [(0, 1), (1, 0)])
 
 
-FAR_FIRST = (4, 5, 6, 7, 2, 3, 1, 0)
+SIDES_OUT = (4, 5, 2, 6, 3, 7, 1, 0)
+SIDES_IN = (4, 2, 5, 3, 6, 1, 7, 0)
+SUMS_OUT = (3, 2, 1, 0)
+SUMS_IN = (4, 5, 6, 2, 7, 3, 1, 0)
 
 
 def chip_device(
@@ -464,7 +479,7 @@
         [pltpu.VMEM((rows, width, channels), F32), pltpu.VMEM((5 * hidden, channels), F32)],
         (meta, pair_input, other_input, mask, entry_gain, input_weight),
     )
-    arrived = {k: to_chip(messages[k], k) for k in FAR_FIRST}
+    arrived = [to_chip(messages[k], k) for k in SIDES_OUT]
     (gate,) = call(
         functools.partial(gate_kernel, update=0), [flat32], [], (normed, input_weight), 0
     )
@@ -476,10 +491,9 @@
             pltpu.VMEM((2, quarter * 4 * rows, LANES), F32),
             pltpu.VMEM((2, quarter * 2 * rows, LANES), F32),
         ],
-        (meta, *[arrived[k] for k in range(8)]),
-    )
-    returned = {k: to_chip(sums[k], k) for k in (2, 3, 1, 0)}
-    own = jnp.concatenate([returned[k] for k in range(4)], axis=0)
+        (meta, *arrived),
+    )
+    own = jnp.concatenate([to_chip(sums[k], k) for k in SUMS_OUT], axis=0)
     other = swap_cores(own)
     stream, normed, *messages = call(
         functools.partial(second_kernel, width=wide),
@@ -491,7 +505,7 @@
         ],
         (meta, own, other, stream, gate, mask, entry_gain, input_weight, middle_gain, output_weight),
     )
-    arrived = {k: to_chip(messages[k], k) for k in FAR_FIRST}
+    arrived = [to_chip(messages[k], k) for k in SIDES_IN]
     (gate,) = call(
         functools.partial(gate_kernel, update=1), [flat32], [], (normed, input_weight), 0
     )
@@ -503,10 +517,9 @@
             pltpu.VMEM((2, eighth * 4 * rows, LANES), F32),
             pltpu.VMEM((2, eighth * 2 * LANES, LANES), F32),
         ],
-        (meta, *[arrived[k] for k in range(8)]),
-    )
-    returned = {k: to_chip(sums[k], k) for k in FAR_FIRST}
-    own = jnp.concatenate([returned[k] for k in range(8)], axis=0)
+        (meta, *arrived),
+    )
+    own = jnp.concatenate([to_chip(sums[k], k) for k in SUMS_IN], axis=0)
     other = swap_cores(own)
     (result,) = call(
         functools.partial(last_kernel, width=wide),

time: 106 us -> 92.5 us (0.87)
  Pallas kernels: 24.5 us -> 16.9 us
  waiting for transfers between devices: 31.3 us -> 25 us
    pallas_call x7, Pallas kernels: 24.5 us -> 16.9 us  [call(): pl.pallas_call(kernel, out_shape=outs, in_specs=in_specs, out_specs=[pl.B...]
    ppermute x24, waiting for transfers between devices: 28.2 us -> 21.9 us  [to_chip(): return lax.ppermute(value, CHIPS, pairs)]
  transfers between devices with their start and end apart: 27 -> 27, of which waited for: 13 -> 15; matrix products, arithmetic and copies ran while one was open for 1% -> 1% of each run, Pallas kernels for 1% -> 1%
where the time goes in v1:
time: 92.5 us; the launch traced here: 92.3 us
  starting transfers between devices  46.3 us (50%)
  waiting for transfers between devices  25 us (27%)
  Pallas kernels  16.9 us (18%)
  local copies, waits for them, and re-layouts  3.06 us (3%)
    ppermute x24, starting transfers between devices, to_chip(): return lax.ppermute(value, CHIPS, pairs)  45.7 us
    ppermute x24, waiting for transfers between devices, to_chip(): return lax.ppermute(value, CHIPS, pairs)  21.9 us
    pallas_call x7, Pallas kernels, call(): pl.pallas_call(kernel, out_shape=outs, in_specs=in_specs, out_specs=[pl.B...  16.9 us
    ppermute x3, waiting for transfers between devices, swap_cores(): return lax.ppermute(value, 'pair', [(0, 1), (1, 0)])  3.08 us
    unnamed x28, local copies, waits for them, and re-layouts  2.79 us
  transfers between devices with their start and end apart: 27, of which 15 were waited for; matrix products, arithmetic and copies ran while one was open for 1% of the time, Pallas kernels for 1%

profile of v1, /device:TPU:0, one launch (start us, length us, event | category | flops | bytes accessed | tf_op | source)
XLA Modules:
  0.0 92.3 jit_solution(8386026860143818603)
XLA Ops:
  0.0 0.5 collective-permute-start
  0.5 0.7 convert_element_type.3
  1.5 0.5 collective-permute-done.other
  2.0 1.0 %copy-done = bf16[2,128,640]{2,1,0:T(8,128)(2,1)S(1)} copy-done((bf16[2,128,640]{2,1,0:T(8,128)(2,1)S(1)}, bf16[2,128,640]{2,1,0:T(8,128)(2,1)}, u32[]{:S(2)}) %copy-start) | copy-done | bytes 327704
  3.0 1.0 %copy-done.2 = bf16[40,40,128]{2,1,0:T(8,128)(2,1)S(1)} copy-done((bf16[40,40,128]{2,1,0:T(8,128)(2,1)S(1)}, bf16[40,40,128]{2,1,0:T(8,128)(2,1)}, u32[]{:S(2)}) %copy-start.2) | copy-done | bytes 409624
  4.0 0.7 copy-done.6
  4.7 1.8 %shard_map.91 = (f32[128,3200]{1,0:T(8,128)S(1)}, bf16[128,3200]{1,0:T(8,128)(2,1)S(1)}, bf16[32,3200]{1,0:T(8,128)(2,1)S(1)}, bf16[32,3200]{1,0:T(8,128)(2,1)S(...) custom-call(s32[2]{0:T(128)S(1)} %pad_add_fusion.meta, ...), custom_call_target="tpu_custom_call" | custom-call | bytes 4847112 | tf_op jit(solution)/shard_map/pallas_call | solution.py:421
  6.5 4.0 %collective-permute-start.1 = (bf16[16,3200]{1,0:T(8,128)(2,1)S(1)}, bf16[16,3200]{1,0:T(8,128)(2,1)S(1)}, u32[]{:S(2)}, u32[]{:S(2)}) collective-permute-start(bf16[16,3200]{1,0:T(8,128)(2,1)S(1)} %get-tuple-element.37), channel_id=1, source_target_pairs={{0,8},{1,9},{2,10},{3,11},{4,12},{5,13},{6,14},{7,15},{8,0},{9,1},... | collective-permute-start | bytes 307208 | tf_op jit(solution)/shard_map/ppermute | solution.py:436
  10.5 1.3 %collective-permute-start.2 = (bf16[16,3200]{1,0:T(8,128)(2,1)S(1)}, bf16[16,3200]{1,0:T(8,128)(2,1)S(1)}, u32[]{:S(2)}, u32[]{:S(2)}) collective-permute-start(bf16[16,3200]{1,0:T(8,128)(2,1)S(1)} %get-tuple-element.38), channel_id=1, source_target_pairs={{0,10},{1,11},{2,8},{3,9},{4,14},{5,15},{6,12},{7,13},{8,2},{9,3},... | collective-permute-start | bytes 307208 | tf_op jit(solution)/shard_map/ppermute | solution.py:436
  11.8 1.6 %collective-permute-start.3 = (bf16[32,3200]{1,0:T(8,128)(2,1)S(1)}, bf16[32,3200]{1,0:T(8,128)(2,1)S(1)}, u32[]{:S(2)}, u32[]{:S(2)}) collective-permute-start(bf16[32,3200]{1,0:T(8,128)(2,1)S(1)} %get-tuple-element.39), channel_id=1, source_target_pairs={{0,4},{1,5},{2,6},{3,7},{4,0},{5,1},{6,2},{7,3},{8,12},{9,13},{10,... | collective-permute-start | bytes 614408 | tf_op jit(solution)/shard_map/ppermute | solution.py:436
  13.5 1.8 %collective-permute-start.7 = (bf16[32,3200]{1,0:T(8,128)(2,1)S(1)}, bf16[32,3200]{1,0:T(8,128)(2,1)S(1)}, u32[]{:S(2)}, u32[]{:S(2)}) collective-permute-start(bf16[32,3200]{1,0:T(8,128)(2,1)S(1)} %get-tuple-element.43), channel_id=1, source_target_pairs={{0,2},{1,3},{2,0},{3,1},{4,6},{5,7},{6,4},{7,5},{8,10},{9,11},{10,... | collective-permute-start | bytes 614408 | tf_op jit(solution)/shard_map/ppermute | solution.py:436
  15.3 2.7 %collective-permute-done.1.refs_0_ = bf16[16,3200]{1,0:T(8,128)(2,1)S(1)} collective-permute-done((bf16[16,3200]{1,0:T(8,128)(2,1)S(1)}, bf16[16,3200]{1,0:T(8,128)(2,1)S(1)}, u32[]{:S(2)}, u32[]{:S(2)}) %collective-permute-start.1) | collective-permute-done | bytes 102432 | tf_op jit(solution)/shard_map/ppermute | solution.py:436
  18.0 3.8 %collective-permute-start.4 = (bf16[16,3200]{1,0:T(8,128)(2,1)S(1)}, bf16[16,3200]{1,0:T(8,128)(2,1)S(1)}, u32[]{:S(2)}, u32[]{:S(2)}) collective-permute-start(bf16[16,3200]{1,0:T(8,128)(2,1)S(1)} %get-tuple-element.40), channel_id=1, source_target_pairs={{0,12},{1,13},{2,14},{3,15},{4,8},{5,9},{6,10},{7,11},{8,4},{9,5},... | collective-permute-start | bytes 307208 | tf_op jit(solution)/shard_map/ppermute | solution.py:436
  21.8 3.1 %collective-permute-start.6 = (bf16[16,3200]{1,0:T(8,128)(2,1)S(1)}, bf16[16,3200]{1,0:T(8,128)(2,1)S(1)}, u32[]{:S(2)}, u32[]{:S(2)}) collective-permute-start(bf16[16,3200]{1,0:T(8,128)(2,1)S(1)} %get-tuple-element.42), channel_id=1, source_target_pairs={{0,14},{1,15},{2,12},{3,13},{4,10},{5,11},{6,8},{7,9},{8,6},{9,7},... | collective-permute-start | bytes 307208 | tf_op jit(solution)/shard_map/ppermute | solution.py:436
  24.9 5.4 %collective-permute-done.4.refs_3_ = bf16[16,3200]{1,0:T(8,128)(2,1)S(1)} collective-permute-done((bf16[16,3200]{1,0:T(8,128)(2,1)S(1)}, bf16[16,3200]{1,0:T(8,128)(2,1)S(1)}, u32[]{:S(2)}, u32[]{:S(2)}) %collective-permute-start.4) | collective-permute-done | bytes 102432 | tf_op jit(solution)/shard_map/ppermute | solution.py:436
  30.3 0.9 collective-permute-done.6.refs_5_
  31.2 2.7 %shard_map.92 = (bf16[16,3200]{1,0:T(8,128)(2,1)S(1)}, bf16[16,3200]{1,0:T(8,128)(2,1)S(1)}, bf16[16,3200]{1,0:T(8,128)(2,1)S(1)}, bf16[16,3200]{1,0:T(8,128)(2,1)S(1)}) custom-call(s32[2]{0:T(128)S(1)} %pad_add_fusion.meta, bf16[16,3200]{1,0:T(8,128)(2,1)S(1)} %collective-permute-done.1.refs_0_, bf16[16,3200]{1,0:T(8,128)(2,1)S(1)} %collective-permute-done.2.refs_1_, ...), custom_call_target="tpu_custom_call" | custom-call | bytes 1638408 | tf_op jit(solution)/shard_map/pallas_call | solution.py:421
  34.0 3.2 %collective-permute-start.9 = (bf16[16,3200]{1,0:T(8,128)(2,1)S(1)}, bf16[16,3200]{1,0:T(8,128)(2,1)S(1)}, u32[]{:S(2)}, u32[]{:S(2)}) collective-permute-start(bf16[16,3200]{1,0:T(8,128)(2,1)S(1)} %get-tuple-element.46), channel_id=1, source_target_pairs={{0,4},{1,5},{2,6},{3,7},{4,0},{5,1},{6,2},{7,3},{8,12},{9,13},{10,... | collective-permute-start | bytes 307208 | tf_op jit(solution)/shard_map/ppermute | solution.py:436
  37.2 0.3 collective-permute-start.10
  37.5 2.2 %collective-permute-done.8 = bf16[16,3200]{1,0:T(8,128)(2,1)S(1)} collective-permute-done((bf16[16,3200]{1,0:T(8,128)(2,1)S(1)}, bf16[16,3200]{1,0:T(8,128)(2,1)S(1)}, u32[]{:S(2)}, u32[]{:S(2)}) %collective-permute-start.8) | collective-permute-done | bytes 102432 | tf_op jit(solution)/shard_map/ppermute | solution.py:436
  39.7 1.5 %collective-permute-done.9 = bf16[16,3200]{1,0:T(8,128)(2,1)S(1)} collective-permute-done((bf16[16,3200]{1,0:T(8,128)(2,1)S(1)}, bf16[16,3200]{1,0:T(8,128)(2,1)S(1)}, u32[]{:S(2)}, u32[]{:S(2)}) %collective-permute-start.9) | collective-permute-done | bytes 102432 | tf_op jit(solution)/shard_map/ppermute | solution.py:436
  41.2 0.6 collective-permute-done.10
  42.0 0.4 shard_map.93.gate
  42.4 1.3 %collective-permute-done.11.other = bf16[64,3200]{1,0:T(8,128)(2,1)S(1)} collective-permute-done((bf16[64,3200]{1,0:T(8,128)(2,1)S(1)}, bf16[64,3200]{1,0:T(8,128)(2,1)S(1)}, u32[]{:S(2)}, u32[]{:S(2)}) %collective-permute-start.11) | collective-permute-done | bytes 409632 | tf_op jit(solution)/shard_map/ppermute | solution.py:440
  43.7 2.7 %shard_map.94 = (f32[128,3200]{1,0:T(8,128)S(1)}, bf16[128,3200]{1,0:T(8,128)(2,1)S(1)}, bf16[16,3200]{1,0:T(8,128)(2,1)S(1)}, bf16[16,3200]{1,0:T(8,128)(2,1)S(...) custom-call(s32[2]{0:T(128)S(1)} %pad_add_fusion.meta, ...), custom_call_target="tpu_custom_call" | custom-call | bytes 7780872 | tf_op jit(solution)/shard_map/pallas_call | solution.py:421
  46.4 2.2 %collective-permute-start.12 = (bf16[16,3200]{1,0:T(8,128)(2,1)S(1)}, bf16[16,3200]{1,0:T(8,128)(2,1)S(1)}, u32[]{:S(2)}, u32[]{:S(2)}) collective-permute-start(bf16[16,3200]{1,0:T(8,128)(2,1)S(1)} %get-tuple-element.51), channel_id=1, source_target_pairs={{0,8},{1,9},{2,10},{3,11},{4,12},{5,13},{6,14},{7,15},{8,0},{9,1},... | collective-permute-start | bytes 307208 | tf_op jit(solution)/shard_map/ppermute | solution.py:436
  48.6 2.0 %collective-permute-start.13 = (bf16[16,3200]{1,0:T(8,128)(2,1)S(1)}, bf16[16,3200]{1,0:T(8,128)(2,1)S(1)}, u32[]{:S(2)}, u32[]{:S(2)}) collective-permute-start(bf16[16,3200]{1,0:T(8,128)(2,1)S(1)} %get-tuple-element.52), channel_id=1, source_target_pairs={{0,4},{1,5},{2,6},{3,7},{4,0},{5,1},{6,2},{7,3},{8,12},{9,13},{10,... | collective-permute-start | bytes 307208 | tf_op jit(solution)/shard_map/ppermute | solution.py:436
  50.7 1.6 %collective-permute-start.15 = (bf16[16,3200]{1,0:T(8,128)(2,1)S(1)}, bf16[16,3200]{1,0:T(8,128)(2,1)S(1)}, u32[]{:S(2)}, u32[]{:S(2)}) collective-permute-start(bf16[16,3200]{1,0:T(8,128)(2,1)S(1)} %get-tuple-element.54), channel_id=1, source_target_pairs={{0,6},{1,7},{2,4},{3,5},{4,2},{5,3},{6,0},{7,1},{8,14},{9,15},{10,... | collective-permute-start | bytes 307208 | tf_op jit(solution)/shard_map/ppermute | solution.py:436
  52.3 3.5 %collective-permute-start.16 = (bf16[16,3200]{1,0:T(8,128)(2,1)S(1)}, bf16[16,3200]{1,0:T(8,128)(2,1)S(1)}, u32[]{:S(2)}, u32[]{:S(2)}) collective-permute-start(bf16[16,3200]{1,0:T(8,128)(2,1)S(1)} %get-tuple-element.55), channel_id=1, source_target_pairs={{0,12},{1,13},{2,14},{3,15},{4,8},{5,9},{6,10},{7,11},{8,4},{9,5},... | collective-permute-start | bytes 307208 | tf_op jit(solution)/shard_map/ppermute | solution.py:436
  55.8 0.6 collective-permute-start.17
  56.5 3.2 %collective-permute-start.18 = (bf16[16,3200]{1,0:T(8,128)(2,1)S(1)}, bf16[16,3200]{1,0:T(8,128)(2,1)S(1)}, u32[]{:S(2)}, u32[]{:S(2)}) collective-permute-start(bf16[16,3200]{1,0:T(8,128)(2,1)S(1)} %get-tuple-element.57), channel_id=1, source_target_pairs={{0,14},{1,15},{2,12},{3,13},{4,10},{5,11},{6,8},{7,9},{8,6},{9,7},... | collective-permute-start | bytes 307208 | tf_op jit(solution)/shard_map/ppermute | solution.py:436
  59.7 0.3 collective-permute-done.14.refs_2_
  59.9 3.1 %collective-permute-done.16.refs_4_ = bf16[16,3200]{1,0:T(8,128)(2,1)S(1)} collective-permute-done((bf16[16,3200]{1,0:T(8,128)(2,1)S(1)}, bf16[16,3200]{1,0:T(8,128)(2,1)S(1)}, u32[]{:S(2)}, u32[]{:S(2)}) %collective-permute-start.16) | collective-permute-done | bytes 102432 | tf_op jit(solution)/shard_map/ppermute | solution.py:436
  63.1 1.8 %collective-permute-done.18.refs_6_ = bf16[16,3200]{1,0:T(8,128)(2,1)S(1)} collective-permute-done((bf16[16,3200]{1,0:T(8,128)(2,1)S(1)}, bf16[16,3200]{1,0:T(8,128)(2,1)S(1)}, u32[]{:S(2)}, u32[]{:S(2)}) %collective-permute-start.18) | collective-permute-done | bytes 102432 | tf_op jit(solution)/shard_map/ppermute | solution.py:436
  64.8 3.6 %shard_map.95 = (bf16[8,3200]{1,0:T(8,128)(2,1)S(1)}, bf16[8,3200]{1,0:T(8,128)(2,1)S(1)}, bf16[8,3200]{1,0:T(8,128)(2,1)S(1)}, bf16[8,3200]{1,0:T(8,128)(2,1)S(...) custom-call(s32[2]{0:T(128)S(1)} %pad_add_fusion.meta, ...), custom_call_target="tpu_custom_call" | custom-call | bytes 1228808 | tf_op jit(solution)/shard_map/pallas_call | solution.py:421
  68.4 5.1 %collective-permute-start.19 = (bf16[8,3200]{1,0:T(8,128)(2,1)S(1)}, bf16[8,3200]{1,0:T(8,128)(2,1)S(1)}, u32[]{:S(2)}, u32[]{:S(2)}) collective-permute-start(bf16[8,3200]{1,0:T(8,128)(2,1)S(1)} %get-tuple-element.59), channel_id=1, source_target_pairs={{0,8},{1,9},{2,10},{3,11},{4,12},{5,13},{6,14},{7,15},{8,0},{9,1},... | collective-permute-start | bytes 153608 | tf_op jit(solution)/shard_map/ppermute | solution.py:436
  73.5 0.9 %collective-permute-start.20 = (bf16[8,3200]{1,0:T(8,128)(2,1)S(1)}, bf16[8,3200]{1,0:T(8,128)(2,1)S(1)}, u32[]{:S(2)}, u32[]{:S(2)}) collective-permute-start(bf16[8,3200]{1,0:T(8,128)(2,1)S(1)} %get-tuple-element.60), channel_id=1, source_target_pairs={{0,10},{1,11},{2,8},{3,9},{4,14},{5,15},{6,12},{7,13},{8,2},{9,3},... | collective-permute-start | bytes 153608 | tf_op jit(solution)/shard_map/ppermute | solution.py:436
  74.4 0.8 collective-permute-start.21
  75.3 2.6 %collective-permute-start.22 = (bf16[8,3200]{1,0:T(8,128)(2,1)S(1)}, bf16[8,3200]{1,0:T(8,128)(2,1)S(1)}, u32[]{:S(2)}, u32[]{:S(2)}) collective-permute-start(bf16[8,3200]{1,0:T(8,128)(2,1)S(1)} %get-tuple-element.62), channel_id=1, source_target_pairs={{0,4},{1,5},{2,6},{3,7},{4,0},{5,1},{6,2},{7,3},{8,12},{9,13},{10,... | collective-permute-start | bytes 153608 | tf_op jit(solution)/shard_map/ppermute | solution.py:436
  77.8 1.1 %collective-permute-start.23 = (bf16[8,3200]{1,0:T(8,128)(2,1)S(1)}, bf16[8,3200]{1,0:T(8,128)(2,1)S(1)}, u32[]{:S(2)}, u32[]{:S(2)}) collective-permute-start(bf16[8,3200]{1,0:T(8,128)(2,1)S(1)} %get-tuple-element.63), channel_id=1, source_target_pairs={{0,14},{1,15},{2,12},{3,13},{4,10},{5,11},{6,8},{7,9},{8,6},{9,7},... | collective-permute-start | bytes 153608 | tf_op jit(solution)/shard_map/ppermute | solution.py:436
  78.9 1.4 %collective-permute-start.24 = (bf16[8,3200]{1,0:T(8,128)(2,1)S(1)}, bf16[8,3200]{1,0:T(8,128)(2,1)S(1)}, u32[]{:S(2)}, u32[]{:S(2)}) collective-permute-start(bf16[8,3200]{1,0:T(8,128)(2,1)S(1)} %get-tuple-element.64), channel_id=1, source_target_pairs={{0,6},{1,7},{2,4},{3,5},{4,2},{5,3},{6,0},{7,1},{8,14},{9,15},{10,... | collective-permute-start | bytes 153608 | tf_op jit(solution)/shard_map/ppermute | solution.py:436
  80.3 0.7 collective-permute-done.20
  81.0 1.4 %collective-permute-start.25 = (bf16[8,3200]{1,0:T(8,128)(2,1)S(1)}, bf16[8,3200]{1,0:T(8,128)(2,1)S(1)}, u32[]{:S(2)}, u32[]{:S(2)}) collective-permute-start(bf16[8,3200]{1,0:T(8,128)(2,1)S(1)} %get-tuple-element.65), channel_id=1, source_target_pairs={{0,2},{1,3},{2,0},{3,1},{4,6},{5,7},{6,4},{7,5},{8,10},{9,11},{10,... | collective-permute-start | bytes 153608 | tf_op jit(solution)/shard_map/ppermute | solution.py:436
  82.4 2.2 %collective-permute-done.23 = bf16[8,3200]{1,0:T(8,128)(2,1)S(1)} collective-permute-done((bf16[8,3200]{1,0:T(8,128)(2,1)S(1)}, bf16[8,3200]{1,0:T(8,128)(2,1)S(1)}, u32[]{:S(2)}, u32[]{:S(2)}) %collective-permute-start.23) | collective-permute-done | bytes 51232 | tf_op jit(solution)/shard_map/ppermute | solution.py:436
  84.7 0.5 collective-permute-done.25
  85.3 0.4 shard_map.96.gate
  85.7 1.3 %collective-permute-done.26.other = bf16[64,3200]{1,0:T(8,128)(2,1)S(1)} collective-permute-done((bf16[64,3200]{1,0:T(8,128)(2,1)S(1)}, bf16[64,3200]{1,0:T(8,128)(2,1)S(1)}, u32[]{:S(2)}, u32[]{:S(2)}) %collective-permute-start.26) | collective-permute-done | bytes 409632 | tf_op jit(solution)/shard_map/ppermute | solution.py:440
  87.0 5.3 %shard_map.97 = bf16[40,40,128]{2,1,0:T(8,128)(2,1)} custom-call(s32[2]{0:T(128)S(1)} %pad_add_fusion.meta, bf16[64,3200]{1,0:T(8,128)(2,1)S(1)} %constant_dynamic-update-slice_fusion.4.own, bf16[64,3200]{1,0:T(8,128)(2,1)S(1)} %collective-permute-done.26.other, f32[128,3200]{1,0:T(8,128)S(1)} %get-tuple-element.67.stream, f32[128,3200]{1,0:T(8,128)S(1)} %shard_map.96.gate, ...), custom_call_target="tpu_custom_call" | custom-call | bytes 4834824 | tf_op jit(solution)/shard_map/pallas_call | solution.py:421
  (49 shorter events, 1.1 us)
Async XLA Ops:
  0.0 2.0 %collective-permute-start = (bf16[40,40,128]{2,1,0:T(8,128)(2,1)}, bf16[40,40,128]{2,1,0:T(8,128)(2,1)S(1)}, u32[]{:S(2)}, u32[]{:S(2)}) collective-permute-start(bf16[40,40,128]{2,1,0:T(8,128)(2,1)} %own.1), channel_id=1, source_target_pairs={{0,1},{1,0},{2,3},{3,2},{4,5},{5,4},{6,7},{7,6},{8,9},{9,8},{10,11... | collective-permute-start | bytes 1228808 | tf_op jit(solution)/shard_map/ppermute | solution.py:440
  2.0 1.0 %copy-start = (bf16[2,128,640]{2,1,0:T(8,128)(2,1)S(1)}, bf16[2,128,640]{2,1,0:T(8,128)(2,1)}, u32[]{:S(2)}) copy-start(bf16[2,128,640]{2,1,0:T(8,128)(2,1)} %weight.7) | copy-start | bytes 983044
  3.0 1.0 %copy-start.2 = (bf16[40,40,128]{2,1,0:T(8,128)(2,1)S(1)}, bf16[40,40,128]{2,1,0:T(8,128)(2,1)}, u32[]{:S(2)}) copy-start(bf16[40,40,128]{2,1,0:T(8,128)(2,1)} %own.1) | copy-start | bytes 1228804
  4.0 0.7 copy-start.6
  4.7 37.3 %copy-start.1 = (bf16[2,128,640]{2,1,0:T(8,128)(2,1)S(1)}, bf16[2,128,640]{2,1,0:T(8,128)(2,1)}, u32[]{:S(2)}) copy-start(bf16[2,128,640]{2,1,0:T(8,128)(2,1)} %weight.7) | copy-start | bytes 983044
  6.5 11.5 %collective-permute-start.1 = (bf16[16,3200]{1,0:T(8,128)(2,1)S(1)}, bf16[16,3200]{1,0:T(8,128)(2,1)S(1)}, u32[]{:S(2)}, u32[]{:S(2)}) collective-permute-start(bf16[16,3200]{1,0:T(8,128)(2,1)S(1)} %get-tuple-element.37), channel_id=1, source_target_pairs={{0,8},{1,9},{2,10},{3,11},{4,12},{5,13},{6,14},{7,15},{8,0},{9,1},... | collective-permute-start | bytes 307208 | tf_op jit(solution)/shard_map/ppermute | solution.py:436
  10.5 11.3 %collective-permute-start.2 = (bf16[16,3200]{1,0:T(8,128)(2,1)S(1)}, bf16[16,3200]{1,0:T(8,128)(2,1)S(1)}, u32[]{:S(2)}, u32[]{:S(2)}) collective-permute-start(bf16[16,3200]{1,0:T(8,128)(2,1)S(1)} %get-tuple-element.38), channel_id=1, source_target_pairs={{0,10},{1,11},{2,8},{3,9},{4,14},{5,15},{6,12},{7,13},{8,2},{9,3},... | collective-permute-start | bytes 307208 | tf_op jit(solution)/shard_map/ppermute | solution.py:436
  11.8 19.4 %collective-permute-start.3 = (bf16[32,3200]{1,0:T(8,128)(2,1)S(1)}, bf16[32,3200]{1,0:T(8,128)(2,1)S(1)}, u32[]{:S(2)}, u32[]{:S(2)}) collective-permute-start(bf16[32,3200]{1,0:T(8,128)(2,1)S(1)} %get-tuple-element.39), channel_id=1, source_target_pairs={{0,4},{1,5},{2,6},{3,7},{4,0},{5,1},{6,2},{7,3},{8,12},{9,13},{10,... | collective-permute-start | bytes 614408 | tf_op jit(solution)/shard_map/ppermute | solution.py:436
  13.4 17.8 %collective-permute-start.5 = (bf16[32,3200]{1,0:T(8,128)(2,1)S(1)}, bf16[32,3200]{1,0:T(8,128)(2,1)S(1)}, u32[]{:S(2)}, u32[]{:S(2)}) collective-permute-start(bf16[32,3200]{1,0:T(8,128)(2,1)S(1)} %get-tuple-element.41), channel_id=1, source_target_pairs={{0,6},{1,7},{2,4},{3,5},{4,2},{5,3},{6,0},{7,1},{8,14},{9,15},{10,... | collective-permute-start | bytes 614408 | tf_op jit(solution)/shard_map/ppermute | solution.py:436
  13.5 17.7 %collective-permute-start.7 = (bf16[32,3200]{1,0:T(8,128)(2,1)S(1)}, bf16[32,3200]{1,0:T(8,128)(2,1)S(1)}, u32[]{:S(2)}, u32[]{:S(2)}) collective-permute-start(bf16[32,3200]{1,0:T(8,128)(2,1)S(1)} %get-tuple-element.43), channel_id=1, source_target_pairs={{0,2},{1,3},{2,0},{3,1},{4,6},{5,7},{6,4},{7,5},{8,10},{9,11},{10,... | collective-permute-start | bytes 614408 | tf_op jit(solution)/shard_map/ppermute | solution.py:436
  18.0 12.3 %collective-permute-start.4 = (bf16[16,3200]{1,0:T(8,128)(2,1)S(1)}, bf16[16,3200]{1,0:T(8,128)(2,1)S(1)}, u32[]{:S(2)}, u32[]{:S(2)}) collective-permute-start(bf16[16,3200]{1,0:T(8,128)(2,1)S(1)} %get-tuple-element.40), channel_id=1, source_target_pairs={{0,12},{1,13},{2,14},{3,15},{4,8},{5,9},{6,10},{7,11},{8,4},{9,5},... | collective-permute-start | bytes 307208 | tf_op jit(solution)/shard_map/ppermute | solution.py:436
  21.8 9.4 %collective-permute-start.6 = (bf16[16,3200]{1,0:T(8,128)(2,1)S(1)}, bf16[16,3200]{1,0:T(8,128)(2,1)S(1)}, u32[]{:S(2)}, u32[]{:S(2)}) collective-permute-start(bf16[16,3200]{1,0:T(8,128)(2,1)S(1)} %get-tuple-element.42), channel_id=1, source_target_pairs={{0,14},{1,15},{2,12},{3,13},{4,10},{5,11},{6,8},{7,9},{8,6},{9,7},... | collective-permute-start | bytes 307208 | tf_op jit(solution)/shard_map/ppermute | solution.py:436
  33.9 5.7 %collective-permute-start.8 = (bf16[16,3200]{1,0:T(8,128)(2,1)S(1)}, bf16[16,3200]{1,0:T(8,128)(2,1)S(1)}, u32[]{:S(2)}, u32[]{:S(2)}) collective-permute-start(bf16[16,3200]{1,0:T(8,128)(2,1)S(1)} %get-tuple-element.45), channel_id=1, source_target_pairs={{0,6},{1,7},{2,4},{3,5},{4,2},{5,3},{6,0},{7,1},{8,14},{9,15},{10,... | collective-permute-start | bytes 307208 | tf_op jit(solution)/shard_map/ppermute | solution.py:436
  34.0 7.2 %collective-permute-start.9 = (bf16[16,3200]{1,0:T(8,128)(2,1)S(1)}, bf16[16,3200]{1,0:T(8,128)(2,1)S(1)}, u32[]{:S(2)}, u32[]{:S(2)}) collective-permute-start(bf16[16,3200]{1,0:T(8,128)(2,1)S(1)} %get-tuple-element.46), channel_id=1, source_target_pairs={{0,4},{1,5},{2,6},{3,7},{4,0},{5,1},{6,2},{7,3},{8,12},{9,13},{10,... | collective-permute-start | bytes 307208 | tf_op jit(solution)/shard_map/ppermute | solution.py:436
  37.2 4.7 %collective-permute-start.10 = (bf16[16,3200]{1,0:T(8,128)(2,1)S(1)}, bf16[16,3200]{1,0:T(8,128)(2,1)S(1)}, u32[]{:S(2)}, u32[]{:S(2)}) collective-permute-start(bf16[16,3200]{1,0:T(8,128)(2,1)S(1)} %get-tuple-element.47), channel_id=1, source_target_pairs={{0,2},{1,3},{2,0},{3,1},{4,6},{5,7},{6,4},{7,5},{8,10},{9,11},{10,... | collective-permute-start | bytes 307208 | tf_op jit(solution)/shard_map/ppermute | solution.py:436
  41.2 2.5 %copy-start.3 = (bf16[2,128,128]{2,1,0:T(8,128)(2,1)S(1)}, bf16[2,128,128]{2,1,0:T(8,128)(2,1)}, u32[]{:S(2)}) copy-start(bf16[2,128,128]{2,1,0:T(8,128)(2,1)} %out_weight.3) | copy-start | bytes 196612
  41.2 2.5 %copy-start.7 = (f32[2,128]{1,0:T(2,128)S(1)}, f32[2,128]{1,0:T(2,128)}, u32[]{:S(2)}) copy-start(f32[2,128]{1,0:T(2,128)} %middle_gain.3) | copy-start | bytes 3076
  41.9 1.8 %collective-permute-start.11 = (bf16[64,3200]{1,0:T(8,128)(2,1)S(1)}, bf16[64,3200]{1,0:T(8,128)(2,1)S(1)}, u32[]{:S(2)}, u32[]{:S(2)}) collective-permute-start(bf16[64,3200]{1,0:T(8,128)(2,1)S(1)} %constant_dynamic-update-slice_fusion.own), channel_id=1, source_target_pairs={{0,1},{1,0},{2,3},{3,2},{4,5},{5,4},{6,7},{7,6},{8,9},{9,8},{10,11... | collective-permute-start | bytes 1228808 | tf_op jit(solution)/shard_map/ppermute | solution.py:440
  46.4 9.5 %collective-permute-start.12 = (bf16[16,3200]{1,0:T(8,128)(2,1)S(1)}, bf16[16,3200]{1,0:T(8,128)(2,1)S(1)}, u32[]{:S(2)}, u32[]{:S(2)}) collective-permute-start(bf16[16,3200]{1,0:T(8,128)(2,1)S(1)} %get-tuple-element.51), channel_id=1, source_target_pairs={{0,8},{1,9},{2,10},{3,11},{4,12},{5,13},{6,14},{7,15},{8,0},{9,1},... | collective-permute-start | bytes 307208 | tf_op jit(solution)/shard_map/ppermute | solution.py:436
  48.6 7.9 %collective-permute-start.13 = (bf16[16,3200]{1,0:T(8,128)(2,1)S(1)}, bf16[16,3200]{1,0:T(8,128)(2,1)S(1)}, u32[]{:S(2)}, u32[]{:S(2)}) collective-permute-start(bf16[16,3200]{1,0:T(8,128)(2,1)S(1)} %get-tuple-element.52), channel_id=1, source_target_pairs={{0,4},{1,5},{2,6},{3,7},{4,0},{5,1},{6,2},{7,3},{8,12},{9,13},{10,... | collective-permute-start | bytes 307208 | tf_op jit(solution)/shard_map/ppermute | solution.py:436
  50.5 9.4 %collective-permute-start.14 = (bf16[16,3200]{1,0:T(8,128)(2,1)S(1)}, bf16[16,3200]{1,0:T(8,128)(2,1)S(1)}, u32[]{:S(2)}, u32[]{:S(2)}) collective-permute-start(bf16[16,3200]{1,0:T(8,128)(2,1)S(1)} %get-tuple-element.53), channel_id=1, source_target_pairs={{0,10},{1,11},{2,8},{3,9},{4,14},{5,15},{6,12},{7,13},{8,2},{9,3},... | collective-permute-start | bytes 307208 | tf_op jit(solution)/shard_map/ppermute | solution.py:436
  50.7 9.2 %collective-permute-start.15 = (bf16[16,3200]{1,0:T(8,128)(2,1)S(1)}, bf16[16,3200]{1,0:T(8,128)(2,1)S(1)}, u32[]{:S(2)}, u32[]{:S(2)}) collective-permute-start(bf16[16,3200]{1,0:T(8,128)(2,1)S(1)} %get-tuple-element.54), channel_id=1, source_target_pairs={{0,6},{1,7},{2,4},{3,5},{4,2},{5,3},{6,0},{7,1},{8,14},{9,15},{10,... | collective-permute-start | bytes 307208 | tf_op jit(solution)/shard_map/ppermute | solution.py:436
  52.3 10.8 %collective-permute-start.16 = (bf16[16,3200]{1,0:T(8,128)(2,1)S(1)}, bf16[16,3200]{1,0:T(8,128)(2,1)S(1)}, u32[]{:S(2)}, u32[]{:S(2)}) collective-permute-start(bf16[16,3200]{1,0:T(8,128)(2,1)S(1)} %get-tuple-element.55), channel_id=1, source_target_pairs={{0,12},{1,13},{2,14},{3,15},{4,8},{5,9},{6,10},{7,11},{8,4},{9,5},... | collective-permute-start | bytes 307208 | tf_op jit(solution)/shard_map/ppermute | solution.py:436
  55.8 7.2 %collective-permute-start.17 = (bf16[16,3200]{1,0:T(8,128)(2,1)S(1)}, bf16[16,3200]{1,0:T(8,128)(2,1)S(1)}, u32[]{:S(2)}, u32[]{:S(2)}) collective-permute-start(bf16[16,3200]{1,0:T(8,128)(2,1)S(1)} %get-tuple-element.56), channel_id=1, source_target_pairs={{0,2},{1,3},{2,0},{3,1},{4,6},{5,7},{6,4},{7,5},{8,10},{9,11},{10,... | collective-permute-start | bytes 307208 | tf_op jit(solution)/shard_map/ppermute | solution.py:436
  56.5 8.4 %collective-permute-start.18 = (bf16[16,3200]{1,0:T(8,128)(2,1)S(1)}, bf16[16,3200]{1,0:T(8,128)(2,1)S(1)}, u32[]{:S(2)}, u32[]{:S(2)}) collective-permute-start(bf16[16,3200]{1,0:T(8,128)(2,1)S(1)} %get-tuple-element.57), channel_id=1, source_target_pairs={{0,14},{1,15},{2,12},{3,13},{4,10},{5,11},{6,8},{7,9},{8,6},{9,7},... | collective-permute-start | bytes 307208 | tf_op jit(solution)/shard_map/ppermute | solution.py:436
  68.4 10.5 %collective-permute-start.19 = (bf16[8,3200]{1,0:T(8,128)(2,1)S(1)}, bf16[8,3200]{1,0:T(8,128)(2,1)S(1)}, u32[]{:S(2)}, u32[]{:S(2)}) collective-permute-start(bf16[8,3200]{1,0:T(8,128)(2,1)S(1)} %get-tuple-element.59), channel_id=1, source_target_pairs={{0,8},{1,9},{2,10},{3,11},{4,12},{5,13},{6,14},{7,15},{8,0},{9,1},... | collective-permute-start | bytes 153608 | tf_op jit(solution)/shard_map/ppermute | solution.py:436
  73.5 7.5 %collective-permute-start.20 = (bf16[8,3200]{1,0:T(8,128)(2,1)S(1)}, bf16[8,3200]{1,0:T(8,128)(2,1)S(1)}, u32[]{:S(2)}, u32[]{:S(2)}) collective-permute-start(bf16[8,3200]{1,0:T(8,128)(2,1)S(1)} %get-tuple-element.60), channel_id=1, source_target_pairs={{0,10},{1,11},{2,8},{3,9},{4,14},{5,15},{6,12},{7,13},{8,2},{9,3},... | collective-permute-start | bytes 153608 | tf_op jit(solution)/shard_map/ppermute | solution.py:436
  74.4 7.9 %collective-permute-start.21 = (bf16[8,3200]{1,0:T(8,128)(2,1)S(1)}, bf16[8,3200]{1,0:T(8,128)(2,1)S(1)}, u32[]{:S(2)}, u32[]{:S(2)}) collective-permute-start(bf16[8,3200]{1,0:T(8,128)(2,1)S(1)} %get-tuple-element.61), channel_id=1, source_target_pairs={{0,12},{1,13},{2,14},{3,15},{4,8},{5,9},{6,10},{7,11},{8,4},{9,5},... | collective-permute-start | bytes 153608 | tf_op jit(solution)/shard_map/ppermute | solution.py:436
  75.3 7.2 %collective-permute-start.22 = (bf16[8,3200]{1,0:T(8,128)(2,1)S(1)}, bf16[8,3200]{1,0:T(8,128)(2,1)S(1)}, u32[]{:S(2)}, u32[]{:S(2)}) collective-permute-start(bf16[8,3200]{1,0:T(8,128)(2,1)S(1)} %get-tuple-element.62), channel_id=1, source_target_pairs={{0,4},{1,5},{2,6},{3,7},{4,0},{5,1},{6,2},{7,3},{8,12},{9,13},{10,... | collective-permute-start | bytes 153608 | tf_op jit(solution)/shard_map/ppermute | solution.py:436
  77.8 6.8 %collective-permute-start.23 = (bf16[8,3200]{1,0:T(8,128)(2,1)S(1)}, bf16[8,3200]{1,0:T(8,128)(2,1)S(1)}, u32[]{:S(2)}, u32[]{:S(2)}) collective-permute-start(bf16[8,3200]{1,0:T(8,128)(2,1)S(1)} %get-tuple-element.63), channel_id=1, source_target_pairs={{0,14},{1,15},{2,12},{3,13},{4,10},{5,11},{6,8},{7,9},{8,6},{9,7},... | collective-permute-start | bytes 153608 | tf_op jit(solution)/shard_map/ppermute | solution.py:436
  78.9 5.8 %collective-permute-start.24 = (bf16[8,3200]{1,0:T(8,128)(2,1)S(1)}, bf16[8,3200]{1,0:T(8,128)(2,1)S(1)}, u32[]{:S(2)}, u32[]{:S(2)}) collective-permute-start(bf16[8,3200]{1,0:T(8,128)(2,1)S(1)} %get-tuple-element.64), channel_id=1, source_target_pairs={{0,6},{1,7},{2,4},{3,5},{4,2},{5,3},{6,0},{7,1},{8,14},{9,15},{10,... | collective-permute-start | bytes 153608 | tf_op jit(solution)/shard_map/ppermute | solution.py:436
  81.0 4.2 %collective-permute-start.25 = (bf16[8,3200]{1,0:T(8,128)(2,1)S(1)}, bf16[8,3200]{1,0:T(8,128)(2,1)S(1)}, u32[]{:S(2)}, u32[]{:S(2)}) collective-permute-start(bf16[8,3200]{1,0:T(8,128)(2,1)S(1)} %get-tuple-element.65), channel_id=1, source_target_pairs={{0,2},{1,3},{2,0},{3,1},{4,6},{5,7},{6,4},{7,5},{8,10},{9,11},{10,... | collective-permute-start | bytes 153608 | tf_op jit(solution)/shard_map/ppermute | solution.py:436
  82.4 4.6 %copy-start.4 = (bf16[128,512]{1,0:T(8,128)(2,1)S(1)}, bf16[128,512]{1,0:T(8,128)(2,1)}, u32[]{:S(2)}) copy-start(bf16[128,512]{1,0:T(8,128)(2,1)} %expand.1) | copy-start | bytes 393220
  82.4 4.6 %copy-start.5 = (bf16[512,128]{1,0:T(8,128)(2,1)S(1)}, bf16[512,128]{1,0:T(8,128)(2,1)}, u32[]{:S(2)}) copy-start(bf16[512,128]{1,0:T(8,128)(2,1)} %shrink.1) | copy-start | bytes 393220
  82.4 4.6 %copy-start.8 = (f32[128]{0:T(128)S(1)}, f32[128]{0:T(128)}, u32[]{:S(2)}) copy-start(f32[128]{0:T(128)} %param.15) | copy-start | bytes 1540
  85.2 1.8 %collective-permute-start.26 = (bf16[64,3200]{1,0:T(8,128)(2,1)S(1)}, bf16[64,3200]{1,0:T(8,128)(2,1)S(1)}, u32[]{:S(2)}, u32[]{:S(2)}) collective-permute-start(bf16[64,3200]{1,0:T(8,128)(2,1)S(1)} %constant_dynamic-update-slice_fusion.4.own), channel_id=1, source_target_pairs={{0,1},{1,0},{2,3},{3,2},{4,5},{5,4},{6,7},{7,6},{8,9},{9,8},{10,11... | collective-permute-start | bytes 1228808 | tf_op jit(solution)/shard_map/ppermute | solution.py:440

commit v2 on v1

--- a/solution.py
+++ b/solution.py
@@ -131,6 +131,10 @@
     return result.astype(jnp.bfloat16).reshape(row_count, col_count, channels)
 
 
+EVERYWHERE = (4, 5, 2, 6, 3, 7, 1, 0)
+WITHIN_HALF = (3, 2, 1, 0)
+
+
 def aligned(start, size):
     return start if isinstance(start, int) else pl.multiple_of(start, size)
 
@@ -199,32 +203,28 @@
     )
 
 
-def side_weights(table, meta, incoming):
+def side_weights(table, meta):
     core, chip = meta[0], meta[1]
     hidden = table.shape[0] // 5
     mine = hidden // 2
-    count = 8 if incoming else 4
-    size = mine // count
+    size = mine // 4
     picked = []
     for base in range(4):
-        starts = [
-            base * hidden + core * mine + size * ((chip & (count - 1)) ^ k) for k in range(count)
-        ]
+        starts = [base * hidden + core * mine + size * ((chip & 3) ^ k) for k in range(4)]
         picked.append(pick_rows(table, starts, size))
     return jnp.concatenate(picked, axis=0).astype(BF16)
 
 
-def send_sides(normed, weights, mask, messages, lanes, incoming):
+def send_sides(normed, weights, mask, messages, lanes):
     quarter = weights.shape[0] // 4
     projected = jnp.dot(weights, normed, preferred_element_type=F32)
     left = mask * sigmoid(projected[quarter : 2 * quarter]) * projected[:quarter]
     right = mask * sigmoid(projected[3 * quarter :]) * projected[2 * quarter : 3 * quarter]
-    count = 8 if incoming else 4
-    size = quarter // count
-    for k in range(count):
+    size = quarter // 4
+    for k in range(4):
         rows = slice(k * size, (k + 1) * size)
         messages[k][:, lanes] = jnp.concatenate([left[rows], right[rows]], axis=0).astype(BF16)
-        if not incoming:
+        if len(messages) > 4:
             messages[4 + k][:, lanes] = right[rows].astype(BF16)
 
 
@@ -235,7 +235,7 @@
     both[:, pl.ds(aligned(core * cols, GROUP), cols), :] = own[...].astype(F32)
     both[:, pl.ds(aligned((1 - core) * cols, GROUP), cols), :] = other[...].astype(F32)
     table[...] = weight[0].astype(F32).T
-    weights = side_weights(table, meta, False)
+    weights = side_weights(table, meta)
     width = GROUP * 2 * cols
     factor = column_of(gain[0:1, :], width)
 
@@ -246,7 +246,7 @@
         stream[:, lanes] = values
         normed = norm_rows(values, factor).astype(BF16)
         normed_out[:, lanes] = normed
-        send_sides(normed, weights, mask[:, lanes], messages, lanes, False)
+        send_sides(normed, weights, mask[:, lanes], messages, lanes)
 
 
 def gate_kernel(normed, weight, gate, *, update):
@@ -257,12 +257,13 @@
 
 
 def outgoing_kernel(meta, *refs, rows, width):
-    messages, outs = dict(zip(SIDES_OUT, refs[:8])), refs[8:12]
+    messages, outs = dict(zip(EVERYWHERE, refs[:8])), refs[8:12]
     left, right, total = refs[12:]
     dap, sub = meta[1] >> 1, meta[1] & 1
     lane = lane_index()
     count = outs[0].shape[0]
     span = 2 * rows
+    pitch = span + GROUP
 
     @steps(rows // GROUP)
     def _(step):
@@ -276,19 +277,19 @@
                 begin = ((k >> 1) & 1) * rows + step * GROUP
                 for c in range(0, count, GROUP):
                     for i, piece in enumerate(split_group(values[c : c + GROUP], width, lane)):
-                        left[k & 1, pl.ds(c * span + begin + i, GROUP, stride=span), :] = piece
+                        left[k & 1, pl.ds(c * pitch + begin + i, GROUP, stride=pitch), :] = piece
                 values = values[count:]
-            begin = half * (count * span) + near + step * GROUP
+            begin = half * (count * pitch) + near + step * GROUP
             for c in range(0, count, GROUP):
                 for i, piece in enumerate(split_group(values[c : c + GROUP], width, lane)):
-                    right[k & 1, pl.ds(c * span + begin + i, GROUP, stride=span), :] = piece
+                    right[k & 1, pl.ds(c * pitch + begin + i, GROUP, stride=pitch), :] = piece
 
     @steps(count)
     def _(c):
-        here = pl.ds(aligned(c * span, GROUP), span)
+        here = pl.ds(aligned(c * pitch, GROUP), span)
         a = jnp.concatenate([left[0, here, :], left[1, here, :]], axis=1).astype(BF16)
         for half in range(2):
-            there = pl.ds(aligned(half * (count * span) + c * span, GROUP), span)
+            there = pl.ds(aligned(half * (count * pitch) + c * pitch, GROUP), span)
             b = jnp.concatenate([right[0, there, :], right[1, there, :]], axis=1).astype(BF16)
             total[half, here, 0:width] = lax.dot_general(
                 a, b, (((1,), (1,)), ((), ())), preferred_element_type=F32
@@ -302,7 +303,7 @@
             joined = []
             for c in range(0, count, GROUP):
                 pieces = [
-                    total[k & 1, pl.ds(c * span + begin + i, GROUP, stride=span), :]
+                    total[k & 1, pl.ds(c * pitch + begin + i, GROUP, stride=pitch), :]
                     for i in range(GROUP)
                 ]
                 joined.append(join_group(pieces, width, lane))
@@ -310,54 +311,60 @@
 
 
 def incoming_kernel(meta, *refs, rows, width):
-    messages, outs = dict(zip(SIDES_IN, refs[:8])), refs[8:16]
-    left, right, total = refs[16:]
+    messages, outs = dict(zip(WITHIN_HALF, refs[:4])), refs[4:12]
+    left, right, total = refs[12:]
     dap, sub = meta[1] >> 1, meta[1] & 1
     lane = lane_index()
     count = outs[0].shape[0]
-    span = 4 * rows
-    tall = 2 * LANES
+    span = 2 * rows
+    pitch = span + GROUP
+    tall = 2 * width
+    tall_pitch = tall + GROUP
 
     @steps(rows // GROUP)
     def _(step):
         lanes = pl.ds(aligned(step * GROUP * width, LANES), GROUP * width)
-        for k in range(8):
+        for k in range(4):
             values = messages[k][:, lanes].astype(F32)
             begin = (k >> 1) * rows + step * GROUP
             for side, part in ((left, values[:count]), (right, values[count:])):
-                for i, piece in enumerate(split_group(part, width, lane)):
-                    side[k & 1, pl.ds(begin + i, GROUP, stride=span), :] = piece
+                for c in range(0, count, GROUP):
+                    for i, piece in enumerate(split_group(part[c : c + GROUP], width, lane)):
+                        side[k & 1, pl.ds(c * pitch + begin + i, GROUP, stride=pitch), :] = piece
 
     @steps(count)
     def _(c):
-        here = pl.ds(aligned(c * span, GROUP), span)
-        a = jnp.concatenate([left[0, here, :], left[1, here, :]], axis=1).astype(BF16)
+        here = pl.ds(aligned(c * pitch, GROUP), span)
         b = jnp.concatenate([right[0, here, :], right[1, here, :]], axis=1).astype(BF16)
-        product = lax.dot_general(a, b, (((0,), (0,)), ((), ())), preferred_element_type=F32)
-        there = pl.ds(aligned(c * tall, GROUP), tall)
-        total[0, there, :] = product[:, :LANES]
-        total[1, there, :] = product[:, LANES:]
+        for block in range(2):
+            a = left[block, here, 0:width].astype(BF16)
+            product = lax.dot_general(a, b, (((0,), (0,)), ((), ())), preferred_element_type=F32)
+            there = pl.ds(aligned(c * tall_pitch + block * width, GROUP), width)
+            total[0, there, :] = product[:, :LANES]
+            total[1, there, :] = product[:, LANES:]
 
     @steps(rows // GROUP)
     def _(step):
         lanes = pl.ds(aligned(step * GROUP * width, LANES), GROUP * width)
         for k in range(8):
             target = dap ^ (k >> 1)
-            begin = ((target >> 1) ^ sub) * LANES + (target & 1) * rows + step * GROUP
-            pieces = [
-                total[k & 1, pl.ds(begin + i, GROUP, stride=tall), :] for i in range(GROUP)
-            ]
-            outs[k][:, lanes] = join_group(pieces, width, lane).astype(BF16)
-
-
-def output_weights(table, square, gain, meta, order):
+            begin = ((target >> 1) ^ sub) * width + (target & 1) * rows + step * GROUP
+            joined = []
+            for c in range(0, count, GROUP):
+                pieces = [
+                    total[k & 1, pl.ds(c * tall_pitch + begin + i, GROUP, stride=tall_pitch), :]
+                    for i in range(GROUP)
+                ]
+                joined.append(join_group(pieces, width, lane))
+            outs[k][:, lanes] = jnp.concatenate(joined, axis=0).astype(BF16)
+
+
+def output_weights(table, square, gain, meta):
     core, chip = meta[0], meta[1]
     mine = table.shape[0] // 2
-    size = mine // len(order)
+    size = mine // 4
     starts = [
-        side * mine + size * ((chip & (len(order) - 1)) ^ k)
-        for side in (core, 1 - core)
-        for k in order
+        side * mine + size * ((chip & 3) ^ k) for side in (core, 1 - core) for k in range(4)
     ]
     square[...] = jnp.broadcast_to(gain, square.shape).T
     return pick_rows(table, starts, size).T.astype(BF16), pick_rows(square, starts, size)
@@ -374,9 +381,9 @@
 ):
     stream_out, normed_out, *messages, table, out_table, square = refs
     out_table[...] = out_weight[0].astype(F32)
-    out_weights, middle = output_weights(out_table, square, middle_gain[0:1, :], meta, SUMS_OUT)
+    out_weights, middle = output_weights(out_table, square, middle_gain[0:1, :], meta)
     table[...] = weight[1].astype(F32).T
-    weights = side_weights(table, meta, True)
+    weights = side_weights(table, meta)
     middle_factor = jnp.concatenate([middle] * (width // middle.shape[1]), axis=1)
     factor = column_of(entry_gain[1:2, :], width)
 
@@ -387,7 +394,7 @@
         stream_out[:, lanes] = values
         normed = norm_rows(values, factor).astype(BF16)
         normed_out[:, lanes] = normed
-        send_sides(normed, weights, mask[:, lanes], messages, lanes, True)
+        send_sides(normed, weights, mask[:, lanes], messages, lanes)
 
 
 def last_kernel(
@@ -397,7 +404,7 @@
     core = meta[0]
     rows, cols, channels = result.shape
     out_table[...] = out_weight[1].astype(F32)
-    out_weights, middle = output_weights(out_table, square, middle_gain[1:2, :], meta, SUMS_IN)
+    out_weights, middle = output_weights(out_table, square, middle_gain[1:2, :], meta)
     middle_factor = jnp.concatenate([middle] * (width // middle.shape[1]), axis=1)
 
     @steps(rows // GROUP)
@@ -438,12 +445,6 @@
 
 def swap_cores(value):
     return lax.ppermute(value, "pair", [(0, 1), (1, 0)])
-
-
-SIDES_OUT = (4, 5, 2, 6, 3, 7, 1, 0)
-SIDES_IN = (4, 2, 5, 3, 6, 1, 7, 0)
-SUMS_OUT = (3, 2, 1, 0)
-SUMS_IN = (4, 5, 6, 2, 7, 3, 1, 0)
 
 
 def chip_device(
@@ -471,33 +472,36 @@
     mask = (row_mask[:, None] * col_mask[None, :]).reshape(1, pairs)
     shape = jax.ShapeDtypeStruct
     flat32, flat16 = shape((channels, pairs), F32), shape((channels, pairs), BF16)
-    quarter, eighth = hidden // 8, hidden // 16
+    part = hidden // 8
+    sides, rights = shape((2 * part, pairs), BF16), shape((part, pairs), BF16)
+    span, tall = 2 * rows + GROUP, 2 * width + GROUP
 
     stream, normed, *messages = call(
         first_kernel,
-        [flat32, flat16] + [shape((2 * quarter, pairs), BF16)] * 4 + [shape((quarter, pairs), BF16)] * 4,
+        [flat32, flat16] + [sides] * 4 + [rights] * 4,
         [pltpu.VMEM((rows, width, channels), F32), pltpu.VMEM((5 * hidden, channels), F32)],
         (meta, pair_input, other_input, mask, entry_gain, input_weight),
     )
-    arrived = [to_chip(messages[k], k) for k in SIDES_OUT]
+    arrived = [to_chip(messages[k], k) for k in EVERYWHERE]
     (gate,) = call(
         functools.partial(gate_kernel, update=0), [flat32], [], (normed, input_weight), 0
     )
     sums = call(
         functools.partial(outgoing_kernel, rows=rows, width=width),
-        [shape((quarter, pairs), BF16)] * 4,
+        [rights] * 4,
         [
-            pltpu.VMEM((2, quarter * 2 * rows, LANES), F32),
-            pltpu.VMEM((2, quarter * 4 * rows, LANES), F32),
-            pltpu.VMEM((2, quarter * 2 * rows, LANES), F32),
+            pltpu.VMEM((2, part * span, LANES), F32),
+            pltpu.VMEM((2, 2 * part * span, LANES), F32),
+            pltpu.VMEM((2, part * span, LANES), F32),
         ],
         (meta, *arrived),
     )
-    own = jnp.concatenate([to_chip(sums[k], k) for k in SUMS_OUT], axis=0)
+    returned = [to_chip(sums[k], k) for k in WITHIN_HALF]
+    own = jnp.concatenate(returned[::-1], axis=0)
     other = swap_cores(own)
     stream, normed, *messages = call(
         functools.partial(second_kernel, width=wide),
-        [flat32, flat16] + [shape((2 * eighth, pairs), BF16)] * 8,
+        [flat32, flat16] + [sides] * 4,
         [
             pltpu.VMEM((5 * hidden, channels), F32),
             pltpu.VMEM((hidden, channels), F32),
@@ -505,21 +509,24 @@
         ],
         (meta, own, other, stream, gate, mask, entry_gain, input_weight, middle_gain, output_weight),
     )
-    arrived = [to_chip(messages[k], k) for k in SIDES_IN]
+    arrived = [to_chip(messages[k], k) for k in WITHIN_HALF]
     (gate,) = call(
         functools.partial(gate_kernel, update=1), [flat32], [], (normed, input_weight), 0
     )
     sums = call(
         functools.partial(incoming_kernel, rows=rows, width=width),
-        [shape((eighth, pairs), BF16)] * 8,
+        [rights] * 8,
         [
-            pltpu.VMEM((2, eighth * 4 * rows, LANES), F32),
-            pltpu.VMEM((2, eighth * 4 * rows, LANES), F32),
-            pltpu.VMEM((2, eighth * 2 * LANES, LANES), F32),
+            pltpu.VMEM((2, part * span, LANES), F32),
+            pltpu.VMEM((2, part * span, LANES), F32),
+            pltpu.VMEM((2, part * tall, LANES), F32),
         ],
         (meta, *arrived),
     )
-    own = jnp.concatenate([to_chip(sums[k], k) for k in SUMS_IN], axis=0)
+    returned = {k: to_chip(sums[k], k) for k in EVERYWHERE}
+    near = jnp.concatenate([returned[k] for k in range(4)], axis=0)
+    far = jnp.concatenate([returned[4 + k] for k in range(4)], axis=0)
+    own = (near.astype(F32) + far.astype(F32)).astype(BF16)
     other = swap_cores(own)
     (result,) = call(
         functools.partial(last_kernel, width=wide),

time: 92.5 us -> 91 us (0.984); the launches traced: 92.3 us -> 89.6 us
  starting transfers between devices: 46.3 us -> 35.5 us
  waiting for transfers between devices: 25 us -> 35.4 us
  Pallas kernels: 16.9 us -> 14.6 us
    ppermute x24 -> x20, starting transfers between devices: 45.7 us -> 34.9 us  [to_chip(): return lax.ppermute(value, CHIPS, pairs)]
    ppermute x24 -> x20, waiting for transfers between devices: 21.9 us -> 32.3 us  [to_chip(): return lax.ppermute(value, CHIPS, pairs)]
    pallas_call x7, Pallas kernels: 16.9 us -> 14.6 us  [call(): pl.pallas_call(kernel, out_shape=outs, in_specs=in_specs, out_specs=[pl.B...]
    unnamed x28 -> x21, local copies, waits for them, and re-layouts: 2.79 us -> 2.72 us
  transfers between devices with their start and end apart: 27 -> 23, of which waited for: 15 -> 12; matrix products, arithmetic and copies ran while one was open for 1% -> 1% of each run, Pallas kernels for 1% -> 1%
where the time goes in v2:
time: 91 us; the launch traced here: 89.6 us
  starting transfers between devices  35.5 us (39%)
  waiting for transfers between devices  35.4 us (39%)
  Pallas kernels  14.6 us (16%)
  local copies, waits for them, and re-layouts  2.98 us (3%)
  other arithmetic  0.93 us (1%)
    ppermute x20, starting transfers between devices, to_chip(): return lax.ppermute(value, CHIPS, pairs)  34.9 us
    ppermute x20, waiting for transfers between devices, to_chip(): return lax.ppermute(value, CHIPS, pairs)  32.3 us
    pallas_call x7, Pallas kernels, call(): pl.pallas_call(kernel, out_shape=outs, in_specs=in_specs, out_specs=[pl.B...  14.6 us
    ppermute x3, waiting for transfers between devices, swap_cores(): return lax.ppermute(value, 'pair', [(0, 1), (1, 0)])  3.09 us
    unnamed x21, local copies, waits for them, and re-layouts  2.72 us
  transfers between devices with their start and end apart: 23, of which 12 were waited for; matrix products, arithmetic and copies ran while one was open for 1% of the time, Pallas kernels for 1%

profile of v2, /device:TPU:0, one launch (start us, length us, event | category | flops | bytes accessed | tf_op | source)
XLA Modules:
  0.0 89.6 jit_solution(9373099237406056137)
XLA Ops:
  0.0 0.5 collective-permute-start
  0.5 0.7 convert_element_type.12
  1.1 0.1 dynamic_slice.7
  1.2 0.1 dynamic_slice.6
  1.3 0.1 broadcast_multiply_fusion
  1.4 0.1 mul.38.mask
  1.5 0.1 pad_add_fusion.meta
  1.5 0.5 collective-permute-done.other
  2.0 1.0 %copy-done = bf16[2,128,640]{2,1,0:T(8,128)(2,1)S(1)} copy-done((bf16[2,128,640]{2,1,0:T(8,128)(2,1)S(1)}, bf16[2,128,640]{2,1,0:T(8,128)(2,1)}, u32[]{:S(2)}) %copy-start) | copy-done | bytes 327704
  3.0 1.0 %copy-done.2 = bf16[40,40,128]{2,1,0:T(8,128)(2,1)S(1)} copy-done((bf16[40,40,128]{2,1,0:T(8,128)(2,1)S(1)}, bf16[40,40,128]{2,1,0:T(8,128)(2,1)}, u32[]{:S(2)}) %copy-start.2) | copy-done | bytes 409624
  4.0 0.7 copy-done.6
  4.7 1.8 %shard_map.91 = (f32[128,3200]{1,0:T(8,128)S(1)}, bf16[128,3200]{1,0:T(8,128)(2,1)S(1)}, bf16[32,3200]{1,0:T(8,128)(2,1)S(1)}, bf16[32,3200]{1,0:T(8,128)(2,1)S(...) custom-call(s32[2]{0:T(128)S(1)} %pad_add_fusion.meta, ...), custom_call_target="tpu_custom_call" | custom-call | bytes 4847112 | tf_op jit(solution)/shard_map/pallas_call | solution.py:428
  6.5 4.0 %collective-permute-start.1 = (bf16[16,3200]{1,0:T(8,128)(2,1)S(1)}, bf16[16,3200]{1,0:T(8,128)(2,1)S(1)}, u32[]{:S(2)}, u32[]{:S(2)}) collective-permute-start(bf16[16,3200]{1,0:T(8,128)(2,1)S(1)} %get-tuple-element.33), channel_id=1, source_target_pairs={{0,8},{1,9},{2,10},{3,11},{4,12},{5,13},{6,14},{7,15},{8,0},{9,1},... | collective-permute-start | bytes 307208 | tf_op jit(solution)/shard_map/ppermute | solution.py:443
  10.5 1.3 %collective-permute-start.2 = (bf16[16,3200]{1,0:T(8,128)(2,1)S(1)}, bf16[16,3200]{1,0:T(8,128)(2,1)S(1)}, u32[]{:S(2)}, u32[]{:S(2)}) collective-permute-start(bf16[16,3200]{1,0:T(8,128)(2,1)S(1)} %get-tuple-element.34), channel_id=1, source_target_pairs={{0,10},{1,11},{2,8},{3,9},{4,14},{5,15},{6,12},{7,13},{8,2},{9,3},... | collective-permute-start | bytes 307208 | tf_op jit(solution)/shard_map/ppermute | solution.py:443
  11.8 1.6 %collective-permute-start.3 = (bf16[32,3200]{1,0:T(8,128)(2,1)S(1)}, bf16[32,3200]{1,0:T(8,128)(2,1)S(1)}, u32[]{:S(2)}, u32[]{:S(2)}) collective-permute-start(bf16[32,3200]{1,0:T(8,128)(2,1)S(1)} %get-tuple-element.35), channel_id=1, source_target_pairs={{0,4},{1,5},{2,6},{3,7},{4,0},{5,1},{6,2},{7,3},{8,12},{9,13},{10,... | collective-permute-start | bytes 614408 | tf_op jit(solution)/shard_map/ppermute | solution.py:443
  13.3 0.2 collective-permute-start.5
  13.5 1.7 %collective-permute-start.7 = (bf16[32,3200]{1,0:T(8,128)(2,1)S(1)}, bf16[32,3200]{1,0:T(8,128)(2,1)S(1)}, u32[]{:S(2)}, u32[]{:S(2)}) collective-permute-start(bf16[32,3200]{1,0:T(8,128)(2,1)S(1)} %get-tuple-element.39), channel_id=1, source_target_pairs={{0,2},{1,3},{2,0},{3,1},{4,6},{5,7},{6,4},{7,5},{8,10},{9,11},{10,... | collective-permute-start | bytes 614408 | tf_op jit(solution)/shard_map/ppermute | solution.py:443
  15.3 2.7 %collective-permute-done.1.refs_0_ = bf16[16,3200]{1,0:T(8,128)(2,1)S(1)} collective-permute-done((bf16[16,3200]{1,0:T(8,128)(2,1)S(1)}, bf16[16,3200]{1,0:T(8,128)(2,1)S(1)}, u32[]{:S(2)}, u32[]{:S(2)}) %collective-permute-start.1) | collective-permute-done | bytes 102432 | tf_op jit(solution)/shard_map/ppermute | solution.py:443
  18.0 3.8 %collective-permute-start.4 = (bf16[16,3200]{1,0:T(8,128)(2,1)S(1)}, bf16[16,3200]{1,0:T(8,128)(2,1)S(1)}, u32[]{:S(2)}, u32[]{:S(2)}) collective-permute-start(bf16[16,3200]{1,0:T(8,128)(2,1)S(1)} %get-tuple-element.36), channel_id=1, source_target_pairs={{0,12},{1,13},{2,14},{3,15},{4,8},{5,9},{6,10},{7,11},{8,4},{9,5},... | collective-permute-start | bytes 307208 | tf_op jit(solution)/shard_map/ppermute | solution.py:443
  21.8 3.1 %collective-permute-start.6 = (bf16[16,3200]{1,0:T(8,128)(2,1)S(1)}, bf16[16,3200]{1,0:T(8,128)(2,1)S(1)}, u32[]{:S(2)}, u32[]{:S(2)}) collective-permute-start(bf16[16,3200]{1,0:T(8,128)(2,1)S(1)} %get-tuple-element.38), channel_id=1, source_target_pairs={{0,14},{1,15},{2,12},{3,13},{4,10},{5,11},{6,8},{7,9},{8,6},{9,7},... | collective-permute-start | bytes 307208 | tf_op jit(solution)/shard_map/ppermute | solution.py:443
  24.9 5.4 %collective-permute-done.4.refs_3_ = bf16[16,3200]{1,0:T(8,128)(2,1)S(1)} collective-permute-done((bf16[16,3200]{1,0:T(8,128)(2,1)S(1)}, bf16[16,3200]{1,0:T(8,128)(2,1)S(1)}, u32[]{:S(2)}, u32[]{:S(2)}) %collective-permute-start.4) | collective-permute-done | bytes 102432 | tf_op jit(solution)/shard_map/ppermute | solution.py:443
  30.3 0.9 collective-permute-done.6.refs_5_
  31.2 2.0 %shard_map.92 = (bf16[16,3200]{1,0:T(8,128)(2,1)S(1)}, bf16[16,3200]{1,0:T(8,128)(2,1)S(1)}, bf16[16,3200]{1,0:T(8,128)(2,1)S(1)}, bf16[16,3200]{1,0:T(8,128)(2,1)S(1)}) custom-call(s32[2]{0:T(128)S(1)} %pad_add_fusion.meta, bf16[16,3200]{1,0:T(8,128)(2,1)S(1)} %collective-permute-done.1.refs_0_, bf16[16,3200]{1,0:T(8,128)(2,1)S(1)} %collective-permute-done.2.refs_1_, ...), custom_call_target="tpu_custom_call" | custom-call | bytes 1638408 | tf_op jit(solution)/shard_map/pallas_call | solution.py:428
  33.2 1.8 %collective-permute-start.8 = (bf16[16,3200]{1,0:T(8,128)(2,1)S(1)}, bf16[16,3200]{1,0:T(8,128)(2,1)S(1)}, u32[]{:S(2)}, u32[]{:S(2)}) collective-permute-start(bf16[16,3200]{1,0:T(8,128)(2,1)S(1)} %get-tuple-element.42), channel_id=1, source_target_pairs={{0,2},{1,3},{2,0},{3,1},{4,6},{5,7},{6,4},{7,5},{8,10},{9,11},{10,... | collective-permute-start | bytes 307208 | tf_op jit(solution)/shard_map/ppermute | solution.py:443
  35.0 1.8 %collective-permute-start.10 = (bf16[16,3200]{1,0:T(8,128)(2,1)S(1)}, bf16[16,3200]{1,0:T(8,128)(2,1)S(1)}, u32[]{:S(2)}, u32[]{:S(2)}) collective-permute-start(bf16[16,3200]{1,0:T(8,128)(2,1)S(1)} %get-tuple-element.44), channel_id=1, source_target_pairs={{0,6},{1,7},{2,4},{3,5},{4,2},{5,3},{6,0},{7,1},{8,14},{9,15},{10,... | collective-permute-start | bytes 307208 | tf_op jit(solution)/shard_map/ppermute | solution.py:443
  36.8 2.3 %collective-permute-done.8 = bf16[16,3200]{1,0:T(8,128)(2,1)S(1)} collective-permute-done((bf16[16,3200]{1,0:T(8,128)(2,1)S(1)}, bf16[16,3200]{1,0:T(8,128)(2,1)S(1)}, u32[]{:S(2)}, u32[]{:S(2)}) %collective-permute-start.8) | collective-permute-done | bytes 102432 | tf_op jit(solution)/shard_map/ppermute | solution.py:443
  39.1 0.6 collective-permute-done.9
  39.7 0.9 collective-permute-done.10
  40.7 0.4 shard_map.93.gate
  41.1 1.3 %collective-permute-done.11.other = bf16[64,3200]{1,0:T(8,128)(2,1)S(1)} collective-permute-done((bf16[64,3200]{1,0:T(8,128)(2,1)S(1)}, bf16[64,3200]{1,0:T(8,128)(2,1)S(1)}, u32[]{:S(2)}, u32[]{:S(2)}) %collective-permute-start.11) | collective-permute-done | bytes 409632 | tf_op jit(solution)/shard_map/ppermute | solution.py:447
  42.4 2.7 %shard_map.94 = (f32[128,3200]{1,0:T(8,128)S(1)}, bf16[128,3200]{1,0:T(8,128)(2,1)S(1)}, bf16[32,3200]{1,0:T(8,128)(2,1)S(1)}, bf16[32,3200]{1,0:T(8,128)(2,1)S(...) custom-call(s32[2]{0:T(128)S(1)} %pad_add_fusion.meta, ...), custom_call_target="tpu_custom_call" | custom-call | bytes 7780872 | tf_op jit(solution)/shard_map/pallas_call | solution.py:428
  45.1 1.8 %collective-permute-start.12 = (bf16[32,3200]{1,0:T(8,128)(2,1)S(1)}, bf16[32,3200]{1,0:T(8,128)(2,1)S(1)}, u32[]{:S(2)}, u32[]{:S(2)}) collective-permute-start(bf16[32,3200]{1,0:T(8,128)(2,1)S(1)} %get-tuple-element.47), channel_id=1, source_target_pairs={{0,6},{1,7},{2,4},{3,5},{4,2},{5,3},{6,0},{7,1},{8,14},{9,15},{10,... | collective-permute-start | bytes 614408 | tf_op jit(solution)/shard_map/ppermute | solution.py:443
  46.9 1.4 %collective-permute-start.13 = (bf16[32,3200]{1,0:T(8,128)(2,1)S(1)}, bf16[32,3200]{1,0:T(8,128)(2,1)S(1)}, u32[]{:S(2)}, u32[]{:S(2)}) collective-permute-start(bf16[32,3200]{1,0:T(8,128)(2,1)S(1)} %get-tuple-element.48), channel_id=1, source_target_pairs={{0,4},{1,5},{2,6},{3,7},{4,0},{5,1},{6,2},{7,3},{8,12},{9,13},{10,... | collective-permute-start | bytes 614408 | tf_op jit(solution)/shard_map/ppermute | solution.py:443
  48.3 0.4 collective-permute-start.14
  48.7 5.4 %collective-permute-done.12.refs_0_ = bf16[32,3200]{1,0:T(8,128)(2,1)S(1)} collective-permute-done((bf16[32,3200]{1,0:T(8,128)(2,1)S(1)}, bf16[32,3200]{1,0:T(8,128)(2,1)S(1)}, u32[]{:S(2)}, u32[]{:S(2)}) %collective-permute-start.12) | collective-permute-done | bytes 204832 | tf_op jit(solution)/shard_map/ppermute | solution.py:443
  54.0 3.8 %collective-permute-done.13.refs_1_ = bf16[32,3200]{1,0:T(8,128)(2,1)S(1)} collective-permute-done((bf16[32,3200]{1,0:T(8,128)(2,1)S(1)}, bf16[32,3200]{1,0:T(8,128)(2,1)S(1)}, u32[]{:S(2)}, u32[]{:S(2)}) %collective-permute-start.13) | collective-permute-done | bytes 204832 | tf_op jit(solution)/shard_map/ppermute | solution.py:443
  57.8 2.0 %shard_map.95 = (bf16[16,3200]{1,0:T(8,128)(2,1)S(1)}, bf16[16,3200]{1,0:T(8,128)(2,1)S(1)}, bf16[16,3200]{1,0:T(8,128)(2,1)S(1)}, bf16[16,3200]{1,0:T(8,128)(2,...) custom-call(s32[2]{0:T(128)S(1)} %pad_add_fusion.meta, ...), custom_call_target="tpu_custom_call" | custom-call | bytes 1638408 | tf_op jit(solution)/shard_map/pallas_call | solution.py:428
  59.8 1.5 %collective-permute-start.15 = (bf16[16,3200]{1,0:T(8,128)(2,1)S(1)}, bf16[16,3200]{1,0:T(8,128)(2,1)S(1)}, u32[]{:S(2)}, u32[]{:S(2)}) collective-permute-start(bf16[16,3200]{1,0:T(8,128)(2,1)S(1)} %get-tuple-element.52), channel_id=1, source_target_pairs={{0,2},{1,3},{2,0},{3,1},{4,6},{5,7},{6,4},{7,5},{8,10},{9,11},{10,... | collective-permute-start | bytes 307208 | tf_op jit(solution)/shard_map/ppermute | solution.py:443
  61.3 1.0 %collective-permute-start.16 = (bf16[16,3200]{1,0:T(8,128)(2,1)S(1)}, bf16[16,3200]{1,0:T(8,128)(2,1)S(1)}, u32[]{:S(2)}, u32[]{:S(2)}) collective-permute-start(bf16[16,3200]{1,0:T(8,128)(2,1)S(1)} %get-tuple-element.53), channel_id=1, source_target_pairs={{0,4},{1,5},{2,6},{3,7},{4,0},{5,1},{6,2},{7,3},{8,12},{9,13},{10,... | collective-permute-start | bytes 307208 | tf_op jit(solution)/shard_map/ppermute | solution.py:443
  62.3 1.1 %collective-permute-start.17 = (bf16[16,3200]{1,0:T(8,128)(2,1)S(1)}, bf16[16,3200]{1,0:T(8,128)(2,1)S(1)}, u32[]{:S(2)}, u32[]{:S(2)}) collective-permute-start(bf16[16,3200]{1,0:T(8,128)(2,1)S(1)} %get-tuple-element.54), channel_id=1, source_target_pairs={{0,6},{1,7},{2,4},{3,5},{4,2},{5,3},{6,0},{7,1},{8,14},{9,15},{10,... | collective-permute-start | bytes 307208 | tf_op jit(solution)/shard_map/ppermute | solution.py:443
  63.4 3.9 %collective-permute-start.18 = (bf16[16,3200]{1,0:T(8,128)(2,1)S(1)}, bf16[16,3200]{1,0:T(8,128)(2,1)S(1)}, u32[]{:S(2)}, u32[]{:S(2)}) collective-permute-start(bf16[16,3200]{1,0:T(8,128)(2,1)S(1)} %get-tuple-element.55), channel_id=1, source_target_pairs={{0,8},{1,9},{2,10},{3,11},{4,12},{5,13},{6,14},{7,15},{8,0},{9,1},... | collective-permute-start | bytes 307208 | tf_op jit(solution)/shard_map/ppermute | solution.py:443
  67.3 3.4 %collective-permute-start.20 = (bf16[16,3200]{1,0:T(8,128)(2,1)S(1)}, bf16[16,3200]{1,0:T(8,128)(2,1)S(1)}, u32[]{:S(2)}, u32[]{:S(2)}) collective-permute-start(bf16[16,3200]{1,0:T(8,128)(2,1)S(1)} %get-tuple-element.57), channel_id=1, source_target_pairs={{0,12},{1,13},{2,14},{3,15},{4,8},{5,9},{6,10},{7,11},{8,4},{9,5},... | collective-permute-start | bytes 307208 | tf_op jit(solution)/shard_map/ppermute | solution.py:443
  70.7 1.3 %collective-permute-start.21 = (bf16[16,3200]{1,0:T(8,128)(2,1)S(1)}, bf16[16,3200]{1,0:T(8,128)(2,1)S(1)}, u32[]{:S(2)}, u32[]{:S(2)}) collective-permute-start(bf16[16,3200]{1,0:T(8,128)(2,1)S(1)} %get-tuple-element.58), channel_id=1, source_target_pairs={{0,14},{1,15},{2,12},{3,13},{4,10},{5,11},{6,8},{7,9},{8,6},{9,7},... | collective-permute-start | bytes 307208 | tf_op jit(solution)/shard_map/ppermute | solution.py:443
  72.0 10.4 %collective-permute-done.19 = bf16[16,3200]{1,0:T(8,128)(2,1)S(1)} collective-permute-done((bf16[16,3200]{1,0:T(8,128)(2,1)S(1)}, bf16[16,3200]{1,0:T(8,128)(2,1)S(1)}, u32[]{:S(2)}, u32[]{:S(2)}) %collective-permute-start.19) | collective-permute-done | bytes 102432 | tf_op jit(solution)/shard_map/ppermute | solution.py:443
  82.4 0.1 add_convert_fusion.own
  82.6 0.4 shard_map.96.gate
  83.1 1.3 %collective-permute-done.22.other = bf16[64,3200]{1,0:T(8,128)(2,1)S(1)} collective-permute-done((bf16[64,3200]{1,0:T(8,128)(2,1)S(1)}, bf16[64,3200]{1,0:T(8,128)(2,1)S(1)}, u32[]{:S(2)}, u32[]{:S(2)}) %collective-permute-start.22) | collective-permute-done | bytes 409632 | tf_op jit(solution)/shard_map/ppermute | solution.py:447
  84.4 5.3 %shard_map.97 = bf16[40,40,128]{2,1,0:T(8,128)(2,1)} custom-call(s32[2]{0:T(128)S(1)} %pad_add_fusion.meta, bf16[64,3200]{1,0:T(8,128)(2,1)S(1)} %add_convert_fusion.own, bf16[64,3200]{1,0:T(8,128)(2,1)S(1)} %collective-permute-done.22.other, f32[128,3200]{1,0:T(8,128)S(1)} %get-tuple-element.59.stream, f32[128,3200]{1,0:T(8,128)S(1)} %shard_map.96.gate, ...), custom_call_target="tpu_custom_call" | custom-call | bytes 4834824 | tf_op jit(solution)/shard_map/pallas_call | solution.py:428
  (34 shorter events, 0.3 us)
Async XLA Ops:
  0.0 2.0 %collective-permute-start = (bf16[40,40,128]{2,1,0:T(8,128)(2,1)}, bf16[40,40,128]{2,1,0:T(8,128)(2,1)S(1)}, u32[]{:S(2)}, u32[]{:S(2)}) collective-permute-start(bf16[40,40,128]{2,1,0:T(8,128)(2,1)} %own.1), channel_id=1, source_target_pairs={{0,1},{1,0},{2,3},{3,2},{4,5},{5,4},{6,7},{7,6},{8,9},{9,8},{10,11... | collective-permute-start | bytes 1228808 | tf_op jit(solution)/shard_map/ppermute | solution.py:447
  2.0 1.0 %copy-start = (bf16[2,128,640]{2,1,0:T(8,128)(2,1)S(1)}, bf16[2,128,640]{2,1,0:T(8,128)(2,1)}, u32[]{:S(2)}) copy-start(bf16[2,128,640]{2,1,0:T(8,128)(2,1)} %weight.7) | copy-start | bytes 983044
  3.0 1.0 %copy-start.2 = (bf16[40,40,128]{2,1,0:T(8,128)(2,1)S(1)}, bf16[40,40,128]{2,1,0:T(8,128)(2,1)}, u32[]{:S(2)}) copy-start(bf16[40,40,128]{2,1,0:T(8,128)(2,1)} %own.1) | copy-start | bytes 1228804
  4.0 0.7 copy-start.6
  4.7 36.0 %copy-start.1 = (bf16[2,128,640]{2,1,0:T(8,128)(2,1)S(1)}, bf16[2,128,640]{2,1,0:T(8,128)(2,1)}, u32[]{:S(2)}) copy-start(bf16[2,128,640]{2,1,0:T(8,128)(2,1)} %weight.7) | copy-start | bytes 983044
  6.5 11.5 %collective-permute-start.1 = (bf16[16,3200]{1,0:T(8,128)(2,1)S(1)}, bf16[16,3200]{1,0:T(8,128)(2,1)S(1)}, u32[]{:S(2)}, u32[]{:S(2)}) collective-permute-start(bf16[16,3200]{1,0:T(8,128)(2,1)S(1)} %get-tuple-element.33), channel_id=1, source_target_pairs={{0,8},{1,9},{2,10},{3,11},{4,12},{5,13},{6,14},{7,15},{8,0},{9,1},... | collective-permute-start | bytes 307208 | tf_op jit(solution)/shard_map/ppermute | solution.py:443
  10.5 11.3 %collective-permute-start.2 = (bf16[16,3200]{1,0:T(8,128)(2,1)S(1)}, bf16[16,3200]{1,0:T(8,128)(2,1)S(1)}, u32[]{:S(2)}, u32[]{:S(2)}) collective-permute-start(bf16[16,3200]{1,0:T(8,128)(2,1)S(1)} %get-tuple-element.34), channel_id=1, source_target_pairs={{0,10},{1,11},{2,8},{3,9},{4,14},{5,15},{6,12},{7,13},{8,2},{9,3},... | collective-permute-start | bytes 307208 | tf_op jit(solution)/shard_map/ppermute | solution.py:443
  11.8 19.4 %collective-permute-start.3 = (bf16[32,3200]{1,0:T(8,128)(2,1)S(1)}, bf16[32,3200]{1,0:T(8,128)(2,1)S(1)}, u32[]{:S(2)}, u32[]{:S(2)}) collective-permute-start(bf16[32,3200]{1,0:T(8,128)(2,1)S(1)} %get-tuple-element.35), channel_id=1, source_target_pairs={{0,4},{1,5},{2,6},{3,7},{4,0},{5,1},{6,2},{7,3},{8,12},{9,13},{10,... | collective-permute-start | bytes 614408 | tf_op jit(solution)/shard_map/ppermute | solution.py:443
  13.3 17.8 %collective-permute-start.5 = (bf16[32,3200]{1,0:T(8,128)(2,1)S(1)}, bf16[32,3200]{1,0:T(8,128)(2,1)S(1)}, u32[]{:S(2)}, u32[]{:S(2)}) collective-permute-start(bf16[32,3200]{1,0:T(8,128)(2,1)S(1)} %get-tuple-element.37), channel_id=1, source_target_pairs={{0,6},{1,7},{2,4},{3,5},{4,2},{5,3},{6,0},{7,1},{8,14},{9,15},{10,... | collective-permute-start | bytes 614408 | tf_op jit(solution)/shard_map/ppermute | solution.py:443
  13.5 17.7 %collective-permute-start.7 = (bf16[32,3200]{1,0:T(8,128)(2,1)S(1)}, bf16[32,3200]{1,0:T(8,128)(2,1)S(1)}, u32[]{:S(2)}, u32[]{:S(2)}) collective-permute-start(bf16[32,3200]{1,0:T(8,128)(2,1)S(1)} %get-tuple-element.39), channel_id=1, source_target_pairs={{0,2},{1,3},{2,0},{3,1},{4,6},{5,7},{6,4},{7,5},{8,10},{9,11},{10,... | collective-permute-start | bytes 614408 | tf_op jit(solution)/shard_map/ppermute | solution.py:443
  18.0 12.3 %collective-permute-start.4 = (bf16[16,3200]{1,0:T(8,128)(2,1)S(1)}, bf16[16,3200]{1,0:T(8,128)(2,1)S(1)}, u32[]{:S(2)}, u32[]{:S(2)}) collective-permute-start(bf16[16,3200]{1,0:T(8,128)(2,1)S(1)} %get-tuple-element.36), channel_id=1, source_target_pairs={{0,12},{1,13},{2,14},{3,15},{4,8},{5,9},{6,10},{7,11},{8,4},{9,5},... | collective-permute-start | bytes 307208 | tf_op jit(solution)/shard_map/ppermute | solution.py:443
  21.8 9.4 %collective-permute-start.6 = (bf16[16,3200]{1,0:T(8,128)(2,1)S(1)}, bf16[16,3200]{1,0:T(8,128)(2,1)S(1)}, u32[]{:S(2)}, u32[]{:S(2)}) collective-permute-start(bf16[16,3200]{1,0:T(8,128)(2,1)S(1)} %get-tuple-element.38), channel_id=1, source_target_pairs={{0,14},{1,15},{2,12},{3,13},{4,10},{5,11},{6,8},{7,9},{8,6},{9,7},... | collective-permute-start | bytes 307208 | tf_op jit(solution)/shard_map/ppermute | solution.py:443
  33.2 5.8 %collective-permute-start.8 = (bf16[16,3200]{1,0:T(8,128)(2,1)S(1)}, bf16[16,3200]{1,0:T(8,128)(2,1)S(1)}, u32[]{:S(2)}, u32[]{:S(2)}) collective-permute-start(bf16[16,3200]{1,0:T(8,128)(2,1)S(1)} %get-tuple-element.42), channel_id=1, source_target_pairs={{0,2},{1,3},{2,0},{3,1},{4,6},{5,7},{6,4},{7,5},{8,10},{9,11},{10,... | collective-permute-start | bytes 307208 | tf_op jit(solution)/shard_map/ppermute | solution.py:443
  35.0 4.7 %collective-permute-start.9 = (bf16[16,3200]{1,0:T(8,128)(2,1)S(1)}, bf16[16,3200]{1,0:T(8,128)(2,1)S(1)}, u32[]{:S(2)}, u32[]{:S(2)}) collective-permute-start(bf16[16,3200]{1,0:T(8,128)(2,1)S(1)} %get-tuple-element.43), channel_id=1, source_target_pairs={{0,4},{1,5},{2,6},{3,7},{4,0},{5,1},{6,2},{7,3},{8,12},{9,13},{10,... | collective-permute-start | bytes 307208 | tf_op jit(solution)/shard_map/ppermute | solution.py:443
  35.0 5.6 %collective-permute-start.10 = (bf16[16,3200]{1,0:T(8,128)(2,1)S(1)}, bf16[16,3200]{1,0:T(8,128)(2,1)S(1)}, u32[]{:S(2)}, u32[]{:S(2)}) collective-permute-start(bf16[16,3200]{1,0:T(8,128)(2,1)S(1)} %get-tuple-element.44), channel_id=1, source_target_pairs={{0,6},{1,7},{2,4},{3,5},{4,2},{5,3},{6,0},{7,1},{8,14},{9,15},{10,... | collective-permute-start | bytes 307208 | tf_op jit(solution)/shard_map/ppermute | solution.py:443
  39.1 3.4 %copy-start.3 = (bf16[2,128,128]{2,1,0:T(8,128)(2,1)S(1)}, bf16[2,128,128]{2,1,0:T(8,128)(2,1)}, u32[]{:S(2)}) copy-start(bf16[2,128,128]{2,1,0:T(8,128)(2,1)} %out_weight.3) | copy-start | bytes 196612
  39.1 3.4 %copy-start.7 = (f32[2,128]{1,0:T(2,128)S(1)}, f32[2,128]{1,0:T(2,128)}, u32[]{:S(2)}) copy-start(f32[2,128]{1,0:T(2,128)} %middle_gain.3) | copy-start | bytes 3076
  40.6 1.8 %collective-permute-start.11 = (bf16[64,3200]{1,0:T(8,128)(2,1)S(1)}, bf16[64,3200]{1,0:T(8,128)(2,1)S(1)}, u32[]{:S(2)}, u32[]{:S(2)}) collective-permute-start(bf16[64,3200]{1,0:T(8,128)(2,1)S(1)} %constant_dynamic-update-slice_fusion.own), channel_id=1, source_target_pairs={{0,1},{1,0},{2,3},{3,2},{4,5},{5,4},{6,7},{7,6},{8,9},{9,8},{10,11... | collective-permute-start | bytes 1228808 | tf_op jit(solution)/shard_map/ppermute | solution.py:447
  45.1 8.9 %collective-permute-start.12 = (bf16[32,3200]{1,0:T(8,128)(2,1)S(1)}, bf16[32,3200]{1,0:T(8,128)(2,1)S(1)}, u32[]{:S(2)}, u32[]{:S(2)}) collective-permute-start(bf16[32,3200]{1,0:T(8,128)(2,1)S(1)} %get-tuple-element.47), channel_id=1, source_target_pairs={{0,6},{1,7},{2,4},{3,5},{4,2},{5,3},{6,0},{7,1},{8,14},{9,15},{10,... | collective-permute-start | bytes 614408 | tf_op jit(solution)/shard_map/ppermute | solution.py:443
  46.9 10.9 %collective-permute-start.13 = (bf16[32,3200]{1,0:T(8,128)(2,1)S(1)}, bf16[32,3200]{1,0:T(8,128)(2,1)S(1)}, u32[]{:S(2)}, u32[]{:S(2)}) collective-permute-start(bf16[32,3200]{1,0:T(8,128)(2,1)S(1)} %get-tuple-element.48), channel_id=1, source_target_pairs={{0,4},{1,5},{2,6},{3,7},{4,0},{5,1},{6,2},{7,3},{8,12},{9,13},{10,... | collective-permute-start | bytes 614408 | tf_op jit(solution)/shard_map/ppermute | solution.py:443
  48.3 9.5 %collective-permute-start.14 = (bf16[32,3200]{1,0:T(8,128)(2,1)S(1)}, bf16[32,3200]{1,0:T(8,128)(2,1)S(1)}, u32[]{:S(2)}, u32[]{:S(2)}) collective-permute-start(bf16[32,3200]{1,0:T(8,128)(2,1)S(1)} %get-tuple-element.49), channel_id=1, source_target_pairs={{0,2},{1,3},{2,0},{3,1},{4,6},{5,7},{6,4},{7,5},{8,10},{9,11},{10,... | collective-permute-start | bytes 614408 | tf_op jit(solution)/shard_map/ppermute | solution.py:443
  59.8 7.5 %collective-permute-start.15 = (bf16[16,3200]{1,0:T(8,128)(2,1)S(1)}, bf16[16,3200]{1,0:T(8,128)(2,1)S(1)}, u32[]{:S(2)}, u32[]{:S(2)}) collective-permute-start(bf16[16,3200]{1,0:T(8,128)(2,1)S(1)} %get-tuple-element.52), channel_id=1, source_target_pairs={{0,2},{1,3},{2,0},{3,1},{4,6},{5,7},{6,4},{7,5},{8,10},{9,11},{10,... | collective-permute-start | bytes 307208 | tf_op jit(solution)/shard_map/ppermute | solution.py:443
  61.3 9.4 %collective-permute-start.16 = (bf16[16,3200]{1,0:T(8,128)(2,1)S(1)}, bf16[16,3200]{1,0:T(8,128)(2,1)S(1)}, u32[]{:S(2)}, u32[]{:S(2)}) collective-permute-start(bf16[16,3200]{1,0:T(8,128)(2,1)S(1)} %get-tuple-element.53), channel_id=1, source_target_pairs={{0,4},{1,5},{2,6},{3,7},{4,0},{5,1},{6,2},{7,3},{8,12},{9,13},{10,... | collective-permute-start | bytes 307208 | tf_op jit(solution)/shard_map/ppermute | solution.py:443
  62.3 9.7 %collective-permute-start.17 = (bf16[16,3200]{1,0:T(8,128)(2,1)S(1)}, bf16[16,3200]{1,0:T(8,128)(2,1)S(1)}, u32[]{:S(2)}, u32[]{:S(2)}) collective-permute-start(bf16[16,3200]{1,0:T(8,128)(2,1)S(1)} %get-tuple-element.54), channel_id=1, source_target_pairs={{0,6},{1,7},{2,4},{3,5},{4,2},{5,3},{6,0},{7,1},{8,14},{9,15},{10,... | collective-permute-start | bytes 307208 | tf_op jit(solution)/shard_map/ppermute | solution.py:443
  63.4 8.6 %collective-permute-start.18 = (bf16[16,3200]{1,0:T(8,128)(2,1)S(1)}, bf16[16,3200]{1,0:T(8,128)(2,1)S(1)}, u32[]{:S(2)}, u32[]{:S(2)}) collective-permute-start(bf16[16,3200]{1,0:T(8,128)(2,1)S(1)} %get-tuple-element.55), channel_id=1, source_target_pairs={{0,8},{1,9},{2,10},{3,11},{4,12},{5,13},{6,14},{7,15},{8,0},{9,1},... | collective-permute-start | bytes 307208 | tf_op jit(solution)/shard_map/ppermute | solution.py:443
  67.3 15.1 %collective-permute-start.19 = (bf16[16,3200]{1,0:T(8,128)(2,1)S(1)}, bf16[16,3200]{1,0:T(8,128)(2,1)S(1)}, u32[]{:S(2)}, u32[]{:S(2)}) collective-permute-start(bf16[16,3200]{1,0:T(8,128)(2,1)S(1)} %get-tuple-element.56), channel_id=1, source_target_pairs={{0,10},{1,11},{2,8},{3,9},{4,14},{5,15},{6,12},{7,13},{8,2},{9,3},... | collective-permute-start | bytes 307208 | tf_op jit(solution)/shard_map/ppermute | solution.py:443
  67.3 15.1 %collective-permute-start.20 = (bf16[16,3200]{1,0:T(8,128)(2,1)S(1)}, bf16[16,3200]{1,0:T(8,128)(2,1)S(1)}, u32[]{:S(2)}, u32[]{:S(2)}) collective-permute-start(bf16[16,3200]{1,0:T(8,128)(2,1)S(1)} %get-tuple-element.57), channel_id=1, source_target_pairs={{0,12},{1,13},{2,14},{3,15},{4,8},{5,9},{6,10},{7,11},{8,4},{9,5},... | collective-permute-start | bytes 307208 | tf_op jit(solution)/shard_map/ppermute | solution.py:443
  70.7 11.7 %collective-permute-start.21 = (bf16[16,3200]{1,0:T(8,128)(2,1)S(1)}, bf16[16,3200]{1,0:T(8,128)(2,1)S(1)}, u32[]{:S(2)}, u32[]{:S(2)}) collective-permute-start(bf16[16,3200]{1,0:T(8,128)(2,1)S(1)} %get-tuple-element.58), channel_id=1, source_target_pairs={{0,14},{1,15},{2,12},{3,13},{4,10},{5,11},{6,8},{7,9},{8,6},{9,7},... | collective-permute-start | bytes 307208 | tf_op jit(solution)/shard_map/ppermute | solution.py:443
  82.5 1.9 %copy-start.4 = (bf16[128,512]{1,0:T(8,128)(2,1)S(1)}, bf16[128,512]{1,0:T(8,128)(2,1)}, u32[]{:S(2)}) copy-start(bf16[128,512]{1,0:T(8,128)(2,1)} %expand.1) | copy-start | bytes 393220
  82.5 1.8 %copy-start.5 = (bf16[512,128]{1,0:T(8,128)(2,1)S(1)}, bf16[512,128]{1,0:T(8,128)(2,1)}, u32[]{:S(2)}) copy-start(bf16[512,128]{1,0:T(8,128)(2,1)} %shrink.1) | copy-start | bytes 393220
  82.5 1.8 %copy-start.8 = (f32[128]{0:T(128)S(1)}, f32[128]{0:T(128)}, u32[]{:S(2)}) copy-start(f32[128]{0:T(128)} %param.15) | copy-start | bytes 1540
  82.5 1.8 %collective-permute-start.22 = (bf16[64,3200]{1,0:T(8,128)(2,1)S(1)}, bf16[64,3200]{1,0:T(8,128)(2,1)S(1)}, u32[]{:S(2)}, u32[]{:S(2)}) collective-permute-start(bf16[64,3200]{1,0:T(8,128)(2,1)S(1)} %add_convert_fusion.own), channel_id=1, source_target_pairs={{0,1},{1,0},{2,3},{3,2},{4,5},{5,4},{6,7},{7,6},{8,9},{9,8},{10,11... | collective-permute-start | bytes 1228808 | tf_op jit(solution)/shard_map/ppermute | solution.py:447

commit v3 on v2

--- a/solution.py
+++ b/solution.py
@@ -147,11 +147,29 @@
     return run
 
 
+def blocks(count, size=2 * LANES):
+    def run(body):
+        for begin in range(0, count, size):
+            body(slice(begin, min(begin + size, count)))
+
+    return run
+
+
 def sigmoid(values):
     return 0.5 * jnp.tanh(0.5 * values) + 0.5
 
 
 def norm_rows(values, factor):
+    return jnp.concatenate(
+        [
+            norm_block(values[:, b : b + LANES], factor[:, :LANES])
+            for b in range(0, values.shape[1], LANES)
+        ],
+        axis=1,
+    )
+
+
+def norm_block(values, factor):
     average = jnp.mean(values, axis=0, keepdims=True)
     centred = values - average
     variance = jnp.mean(centred * centred, axis=0, keepdims=True)
@@ -205,7 +223,7 @@
 
 def side_weights(table, meta):
     core, chip = meta[0], meta[1]
-    hidden = table.shape[0] // 5
+    hidden = table.shape[0] // 4
     mine = hidden // 2
     size = mine // 4
     picked = []
@@ -228,32 +246,58 @@
             messages[4 + k][:, lanes] = right[rows].astype(BF16)
 
 
-def first_kernel(meta, own, other, mask, gain, weight, *refs):
-    stream, normed_out, *messages, both, table = refs
-    core = meta[0]
+def pick_columns(first, own, other):
+    return jnp.where(
+        first, jnp.concatenate([own, other], axis=1), jnp.concatenate([other, own], axis=1)
+    )
+
+
+def first_kernel(meta, own, other, mask, weight, *refs):
+    stream, normed_out, *messages, table = refs
+    first = meta[0] == 0
     rows, cols, channels = own.shape
-    both[:, pl.ds(aligned(core * cols, GROUP), cols), :] = own[...].astype(F32)
-    both[:, pl.ds(aligned((1 - core) * cols, GROUP), cols), :] = other[...].astype(F32)
-    table[...] = weight[0].astype(F32).T
+    width = GROUP * 2 * cols
+    factors = column_of(mask[:, stream.shape[1] :], channels)
+    table[...] = weight[...].astype(F32).T
     weights = side_weights(table, meta)
-    width = GROUP * 2 * cols
-    factor = column_of(gain[0:1, :], width)
 
     @steps(rows // GROUP)
     def _(step):
-        lanes = pl.ds(aligned(step * width, LANES), width)
-        values = both[pl.ds(step * GROUP, GROUP)].reshape(width, channels).T
+        lanes = pl.ds(step * width, width)
+        here = pl.ds(step * GROUP, GROUP)
+        values = pick_columns(first, own[here].astype(F32), other[here].astype(F32))
+        values = values.reshape(width, channels).T
         stream[:, lanes] = values
-        normed = norm_rows(values, factor).astype(BF16)
+
+    @blocks(stream.shape[1])
+    def _(lanes):
+        normed = norm_rows(stream[:, lanes], factors).astype(BF16)
         normed_out[:, lanes] = normed
         send_sides(normed, weights, mask[:, lanes], messages, lanes)
 
 
-def gate_kernel(normed, weight, gate, *, update):
+def gate_of(normed, weight, update):
     channels = normed.shape[0]
     hidden = (weight.shape[2] - channels) // 4
     table = weight[update, :, 4 * hidden :].astype(F32).T.astype(BF16)
-    gate[...] = sigmoid(jnp.dot(table, normed[...], preferred_element_type=F32))
+    return sigmoid(jnp.dot(table, normed[...], preferred_element_type=F32))
+
+
+def first_gate_kernel(meta, normed, weight, entry_gain, middle_gain, out_weight, *refs):
+    gate, out_weights, middle, factor, weights, table, out_table, square = refs
+    gate[...] = gate_of(normed, weight, 0)
+    out_table[...] = out_weight[0].astype(F32)
+    out_weights[...], middle[...] = output_weights(out_table, square, middle_gain[0:1, :], meta)
+    factor[...] = column_of(entry_gain[1:2, :], factor.shape[1])
+    table[...] = weight[1, :, : table.shape[0]].astype(F32).T
+    weights[...] = side_weights(table, meta)
+
+
+def second_gate_kernel(meta, normed, weight, middle_gain, out_weight, *refs):
+    gate, out_weights, middle, out_table, square = refs
+    gate[...] = gate_of(normed, weight, 1)
+    out_table[...] = out_weight[1].astype(F32)
+    out_weights[...], middle[...] = output_weights(out_table, square, middle_gain[1:2, :], meta)
 
 
 def outgoing_kernel(meta, *refs, rows, width):
@@ -377,43 +421,42 @@
 
 
 def second_kernel(
-    meta, own, other, stream, gate, mask, entry_gain, weight, middle_gain, out_weight, *refs, width
+    own, other, stream, gate, mask, out_weights, middle, factor, weights, *refs, width
 ):
-    stream_out, normed_out, *messages, table, out_table, square = refs
-    out_table[...] = out_weight[0].astype(F32)
-    out_weights, middle = output_weights(out_table, square, middle_gain[0:1, :], meta)
-    table[...] = weight[1].astype(F32).T
-    weights = side_weights(table, meta)
-    middle_factor = jnp.concatenate([middle] * (width // middle.shape[1]), axis=1)
-    factor = column_of(entry_gain[1:2, :], width)
-
-    @steps(stream.shape[1] // width)
-    def _(step):
-        lanes = pl.ds(aligned(step * width, LANES), width)
-        values = add_update(own, other, stream, gate, out_weights, middle_factor, lanes)
+    stream_out, normed_out, *messages = refs
+    channels = stream.shape[0]
+    middles = jnp.concatenate([middle[...]] * (width // channels), axis=1)
+    factors = jnp.concatenate([factor[...]] * (width // channels), axis=1)
+
+    @blocks(stream.shape[1])
+    def _(lanes):
+        values = add_update(own, other, stream, gate, out_weights[...], middles, lanes)
         stream_out[:, lanes] = values
-        normed = norm_rows(values, factor).astype(BF16)
+        normed = norm_rows(values, factors).astype(BF16)
         normed_out[:, lanes] = normed
-        send_sides(normed, weights, mask[:, lanes], messages, lanes)
+        send_sides(normed, weights[...], mask[:, lanes], messages, lanes)
+
+
+def last_scratch(channels, pairs):
+    return [pltpu.VMEM((channels, pairs), F32)]
 
 
 def last_kernel(
-    meta, own, other, stream, gate, middle_gain, out_weight, final_gain, expand, shrink, *refs, width
+    meta, own, other, stream, gate, out_weights, middle, final_gain, expand, shrink, result, total
 ):
-    result, out_table, square, both = refs
-    core = meta[0]
+    first = meta[0] == 0
     rows, cols, channels = result.shape
-    out_table[...] = out_weight[1].astype(F32)
-    out_weights, middle = output_weights(out_table, square, middle_gain[1:2, :], meta)
-    middle_factor = jnp.concatenate([middle] * (width // middle.shape[1]), axis=1)
+    width = GROUP * 2 * cols
+    middles = jnp.concatenate([middle[...]] * (width // channels), axis=1)
+
+    @blocks(stream.shape[1])
+    def _(lanes):
+        total[:, lanes] = add_update(own, other, stream, gate, out_weights[...], middles, lanes)
 
     @steps(rows // GROUP)
     def _(step):
-        lanes = pl.ds(aligned(step * width, LANES), width)
-        values = add_update(own, other, stream, gate, out_weights, middle_factor, lanes)
-        both[...] = values.T.reshape(GROUP, 2 * cols, channels)
-        flat = both[:, pl.ds(aligned(core * cols, GROUP), cols), :]
-        flat = flat.reshape(GROUP * cols, channels)
+        values = total[:, pl.ds(step * width, width)].T.reshape(GROUP, 2 * cols, channels)
+        flat = jnp.where(first, values[:, :cols], values[:, cols:]).reshape(GROUP * cols, channels)
         normed = layer_norm(flat, final_gain[...], 1).astype(BF16)
         expanded = jnp.dot(normed, expand[...], preferred_element_type=F32)
         expanded = jnp.maximum(expanded, 0.0).astype(BF16)
@@ -466,25 +509,36 @@
     dap, sub, core = lax.axis_index("dap"), lax.axis_index("sub"), lax.axis_index("pair")
     meta = jnp.stack([core, dap * 2 + sub]).astype(jnp.int32)
     other_input = swap_cores(pair_input)
-    mask_values = residue_mask.astype(F32)
-    row_mask = lax.dynamic_slice_in_dim(mask_values, dap * rows, rows)
-    col_mask = lax.dynamic_slice_in_dim(mask_values, sub * width, width)
-    mask = (row_mask[:, None] * col_mask[None, :]).reshape(1, pairs)
     shape = jax.ShapeDtypeStruct
     flat32, flat16 = shape((channels, pairs), F32), shape((channels, pairs), BF16)
     part = hidden // 8
     sides, rights = shape((2 * part, pairs), BF16), shape((part, pairs), BF16)
     span, tall = 2 * rows + GROUP, 2 * width + GROUP
 
+    square32, square16 = shape((channels, channels), F32), shape((hidden, channels), BF16)
+    side_weight = shape((2 * hidden, channels), BF16)
+    mask_values = residue_mask.astype(F32)
+    row_mask = lax.dynamic_slice_in_dim(mask_values, dap * rows, rows)
+    col_mask = lax.dynamic_slice_in_dim(mask_values, sub * width, width)
+    mask = (row_mask[:, None] * col_mask[None, :]).reshape(1, pairs)
+    mask = jnp.concatenate([mask, entry_gain[0:1]], axis=1)
+
     stream, normed, *messages = call(
         first_kernel,
         [flat32, flat16] + [sides] * 4 + [rights] * 4,
-        [pltpu.VMEM((rows, width, channels), F32), pltpu.VMEM((5 * hidden, channels), F32)],
-        (meta, pair_input, other_input, mask, entry_gain, input_weight),
+        [pltpu.VMEM((4 * hidden, channels), F32)],
+        (meta, pair_input, other_input, mask, input_weight[0, :, : 4 * hidden]),
     )
     arrived = [to_chip(messages[k], k) for k in EVERYWHERE]
-    (gate,) = call(
-        functools.partial(gate_kernel, update=0), [flat32], [], (normed, input_weight), 0
+    gate, out_weights, middle, factor, weights = call(
+        first_gate_kernel,
+        [flat32, square16, square32, square32, side_weight],
+        [
+            pltpu.VMEM((4 * hidden, channels), F32),
+            pltpu.VMEM((hidden, channels), F32),
+            pltpu.VMEM((hidden, LANES), F32),
+        ],
+        (meta, normed, input_weight, entry_gain, middle_gain, output_weight),
     )
     sums = call(
         functools.partial(outgoing_kernel, rows=rows, width=width),
@@ -502,16 +556,16 @@
     stream, normed, *messages = call(
         functools.partial(second_kernel, width=wide),
         [flat32, flat16] + [sides] * 4,
-        [
-            pltpu.VMEM((5 * hidden, channels), F32),
-            pltpu.VMEM((hidden, channels), F32),
-            pltpu.VMEM((hidden, LANES), F32),
-        ],
-        (meta, own, other, stream, gate, mask, entry_gain, input_weight, middle_gain, output_weight),
+        [],
+        (own, other, stream, gate, mask, out_weights, middle, factor, weights),
+        0,
     )
     arrived = [to_chip(messages[k], k) for k in WITHIN_HALF]
-    (gate,) = call(
-        functools.partial(gate_kernel, update=1), [flat32], [], (normed, input_weight), 0
+    gate, out_weights, middle = call(
+        second_gate_kernel,
+        [flat32, square16, square32],
+        [pltpu.VMEM((hidden, channels), F32), pltpu.VMEM((hidden, LANES), F32)],
+        (meta, normed, input_weight, middle_gain, output_weight),
     )
     sums = call(
         functools.partial(incoming_kernel, rows=rows, width=width),
@@ -529,15 +583,11 @@
     own = (near.astype(F32) + far.astype(F32)).astype(BF16)
     other = swap_cores(own)
     (result,) = call(
-        functools.partial(last_kernel, width=wide),
+        last_kernel,
         [shape((rows, cols, channels), BF16)],
-        [
-            pltpu.VMEM((hidden, channels), F32),
-            pltpu.VMEM((hidden, LANES), F32),
-            pltpu.VMEM((GROUP, width, channels), F32),
-        ],
+        last_scratch(channels, pairs),
         (
-            meta, own, other, stream, gate, middle_gain, output_weight,
+            meta, own, other, stream, gate, out_weights, middle,
             final_gain.reshape(1, channels), expand_weight, shrink_weight,
         ),
     )

time: 91 us -> 88.7 us (0.975)
  waiting for transfers between devices: 35.4 us -> 34.2 us
    ppermute x3, waiting for transfers between devices: 3.09 us -> 1.41 us  [swap_cores(): return lax.ppermute(value, 'pair', [(0, 1), (1, 0)])]
    unnamed x21 -> x19, local copies, waits for them, and re-layouts: 2.72 us -> 1.06 us
    squeeze x0 -> x1, local copies, waits for them, and re-layouts: none -> 0.98 us  [chip_device(): input_weight[0, :, :4 * hidden]]
  transfers between devices with their start and end apart: 23 -> 23, of which waited for: 12 -> 11; matrix products, arithmetic and copies ran while one was open for 1% -> 3% of each run, Pallas kernels for 1% -> 2%
where the time goes in v3:
time: 88.7 us; the launch traced here: 87.4 us
  starting transfers between devices  35 us (39%)
  waiting for transfers between devices  34.2 us (39%)
  Pallas kernels  14 us (16%)
  local copies, waits for them, and re-layouts  2.97 us (3%)
  other arithmetic  0.96 us (1%)
    ppermute x20, starting transfers between devices, to_chip(): return lax.ppermute(value, CHIPS, pairs)  34.4 us
    ppermute x20, waiting for transfers between devices, to_chip(): return lax.ppermute(value, CHIPS, pairs)  32.8 us
    pallas_call x7, Pallas kernels, call(): pl.pallas_call(kernel, out_shape=outs, in_specs=in_specs, out_specs=[pl.B...  14 us
  transfers between devices with their start and end apart: 23, of which 11 were waited for; matrix products, arithmetic and copies ran while one was open for 3% of the time, Pallas kernels for 2%

profile of v3, /device:TPU:0, one launch (start us, length us, event | category | flops | bytes accessed | tf_op | source)
XLA Modules:
  0.0 87.4 jit_solution(11900370919451747736)
XLA Ops:
  0.0 0.5 collective-permute-start
  0.5 0.7 slice.6
  1.1 0.7 convert_element_type.12
  1.8 0.1 dynamic_slice.7
  1.9 0.1 dynamic_slice.6
  2.0 0.1 broadcast_multiply_fusion
  2.0 0.1 mul.38
  2.2 1.0 %slice_bitcast_fusion.weight = bf16[128,512]{1,0:T(8,128)(2,1)S(1)} fusion(bf16[2,128,640]{2,1,0:T(8,128)(2,1)} %weight.3), kind=kLoop, calls=%fused_computation.1 | loop fusion | bytes 262144 | tf_op jit(solution)/shard_map/squeeze | solution.py:530
  3.1 0.1 pad_add_fusion.meta
  3.3 1.0 %copy-done.1 = bf16[40,40,128]{2,1,0:T(8,128)(2,1)S(1)} copy-done((bf16[40,40,128]{2,1,0:T(8,128)(2,1)S(1)}, bf16[40,40,128]{2,1,0:T(8,128)(2,1)}, u32[]{:S(2)}) %copy-start.1) | copy-done | bytes 409624
  4.2 1.8 %shard_map.91 = (f32[128,3200]{1,0:T(8,128)S(1)}, bf16[128,3200]{1,0:T(8,128)(2,1)S(1)}, bf16[32,3200]{1,0:T(8,128)(2,1)S(1)}, bf16[32,3200]{1,0:T(8,128)(2,1)S(...) custom-call(s32[2]{0:T(128)S(1)} %pad_add_fusion.meta, ...), custom_call_target="tpu_custom_call" | custom-call | bytes 4649992 | tf_op jit(solution)/shard_map/pallas_call | solution.py:471
  6.0 3.7 %collective-permute-start.1 = (bf16[16,3200]{1,0:T(8,128)(2,1)S(1)}, bf16[16,3200]{1,0:T(8,128)(2,1)S(1)}, u32[]{:S(2)}, u32[]{:S(2)}) collective-permute-start(bf16[16,3200]{1,0:T(8,128)(2,1)S(1)} %get-tuple-element.41), channel_id=1, source_target_pairs={{0,8},{1,9},{2,10},{3,11},{4,12},{5,13},{6,14},{7,15},{8,0},{9,1},... | collective-permute-start | bytes 307208 | tf_op jit(solution)/shard_map/ppermute | solution.py:486
  9.7 1.3 %collective-permute-start.2 = (bf16[16,3200]{1,0:T(8,128)(2,1)S(1)}, bf16[16,3200]{1,0:T(8,128)(2,1)S(1)}, u32[]{:S(2)}, u32[]{:S(2)}) collective-permute-start(bf16[16,3200]{1,0:T(8,128)(2,1)S(1)} %get-tuple-element.42), channel_id=1, source_target_pairs={{0,10},{1,11},{2,8},{3,9},{4,14},{5,15},{6,12},{7,13},{8,2},{9,3},... | collective-permute-start | bytes 307208 | tf_op jit(solution)/shard_map/ppermute | solution.py:486
  10.9 1.6 %collective-permute-start.3 = (bf16[32,3200]{1,0:T(8,128)(2,1)S(1)}, bf16[32,3200]{1,0:T(8,128)(2,1)S(1)}, u32[]{:S(2)}, u32[]{:S(2)}) collective-permute-start(bf16[32,3200]{1,0:T(8,128)(2,1)S(1)} %get-tuple-element.43), channel_id=1, source_target_pairs={{0,4},{1,5},{2,6},{3,7},{4,0},{5,1},{6,2},{7,3},{8,12},{9,13},{10,... | collective-permute-start | bytes 614408 | tf_op jit(solution)/shard_map/ppermute | solution.py:486
  12.5 0.2 collective-permute-start.5
  12.7 1.8 %collective-permute-start.7 = (bf16[32,3200]{1,0:T(8,128)(2,1)S(1)}, bf16[32,3200]{1,0:T(8,128)(2,1)S(1)}, u32[]{:S(2)}, u32[]{:S(2)}) collective-permute-start(bf16[32,3200]{1,0:T(8,128)(2,1)S(1)} %get-tuple-element.47), channel_id=1, source_target_pairs={{0,2},{1,3},{2,0},{3,1},{4,6},{5,7},{6,4},{7,5},{8,10},{9,11},{10,... | collective-permute-start | bytes 614408 | tf_op jit(solution)/shard_map/ppermute | solution.py:486
  14.4 2.9 %collective-permute-done.1.refs_0_ = bf16[16,3200]{1,0:T(8,128)(2,1)S(1)} collective-permute-done((bf16[16,3200]{1,0:T(8,128)(2,1)S(1)}, bf16[16,3200]{1,0:T(8,128)(2,1)S(1)}, u32[]{:S(2)}, u32[]{:S(2)}) %collective-permute-start.1) | collective-permute-done | bytes 102432 | tf_op jit(solution)/shard_map/ppermute | solution.py:486
  17.3 4.0 %collective-permute-start.4 = (bf16[16,3200]{1,0:T(8,128)(2,1)S(1)}, bf16[16,3200]{1,0:T(8,128)(2,1)S(1)}, u32[]{:S(2)}, u32[]{:S(2)}) collective-permute-start(bf16[16,3200]{1,0:T(8,128)(2,1)S(1)} %get-tuple-element.44), channel_id=1, source_target_pairs={{0,12},{1,13},{2,14},{3,15},{4,8},{5,9},{6,10},{7,11},{8,4},{9,5},... | collective-permute-start | bytes 307208 | tf_op jit(solution)/shard_map/ppermute | solution.py:486
  21.3 3.2 %collective-permute-start.6 = (bf16[16,3200]{1,0:T(8,128)(2,1)S(1)}, bf16[16,3200]{1,0:T(8,128)(2,1)S(1)}, u32[]{:S(2)}, u32[]{:S(2)}) collective-permute-start(bf16[16,3200]{1,0:T(8,128)(2,1)S(1)} %get-tuple-element.46), channel_id=1, source_target_pairs={{0,14},{1,15},{2,12},{3,13},{4,10},{5,11},{6,8},{7,9},{8,6},{9,7},... | collective-permute-start | bytes 307208 | tf_op jit(solution)/shard_map/ppermute | solution.py:486
  24.5 5.3 %collective-permute-done.4.refs_3_ = bf16[16,3200]{1,0:T(8,128)(2,1)S(1)} collective-permute-done((bf16[16,3200]{1,0:T(8,128)(2,1)S(1)}, bf16[16,3200]{1,0:T(8,128)(2,1)S(1)}, u32[]{:S(2)}, u32[]{:S(2)}) %collective-permute-start.4) | collective-permute-done | bytes 102432 | tf_op jit(solution)/shard_map/ppermute | solution.py:486
  29.7 1.0 %collective-permute-done.6.refs_5_ = bf16[16,3200]{1,0:T(8,128)(2,1)S(1)} collective-permute-done((bf16[16,3200]{1,0:T(8,128)(2,1)S(1)}, bf16[16,3200]{1,0:T(8,128)(2,1)S(1)}, u32[]{:S(2)}, u32[]{:S(2)}) %collective-permute-start.6) | collective-permute-done | bytes 102432 | tf_op jit(solution)/shard_map/ppermute | solution.py:486
  30.7 2.0 %shard_map.92 = (bf16[16,3200]{1,0:T(8,128)(2,1)S(1)}, bf16[16,3200]{1,0:T(8,128)(2,1)S(1)}, bf16[16,3200]{1,0:T(8,128)(2,1)S(1)}, bf16[16,3200]{1,0:T(8,128)(2,1)S(1)}) custom-call(s32[2]{0:T(128)S(1)} %pad_add_fusion.meta, bf16[16,3200]{1,0:T(8,128)(2,1)S(1)} %collective-permute-done.1.refs_0_, bf16[16,3200]{1,0:T(8,128)(2,1)S(1)} %collective-permute-done.2.refs_1_, ...), custom_call_target="tpu_custom_call" | custom-call | bytes 1638408 | tf_op jit(solution)/shard_map/pallas_call | solution.py:471
  32.8 2.0 %collective-permute-start.8 = (bf16[16,3200]{1,0:T(8,128)(2,1)S(1)}, bf16[16,3200]{1,0:T(8,128)(2,1)S(1)}, u32[]{:S(2)}, u32[]{:S(2)}) collective-permute-start(bf16[16,3200]{1,0:T(8,128)(2,1)S(1)} %get-tuple-element.50), channel_id=1, source_target_pairs={{0,2},{1,3},{2,0},{3,1},{4,6},{5,7},{6,4},{7,5},{8,10},{9,11},{10,... | collective-permute-start | bytes 307208 | tf_op jit(solution)/shard_map/ppermute | solution.py:486
  34.8 1.5 %collective-permute-start.10 = (bf16[16,3200]{1,0:T(8,128)(2,1)S(1)}, bf16[16,3200]{1,0:T(8,128)(2,1)S(1)}, u32[]{:S(2)}, u32[]{:S(2)}) collective-permute-start(bf16[16,3200]{1,0:T(8,128)(2,1)S(1)} %get-tuple-element.52), channel_id=1, source_target_pairs={{0,6},{1,7},{2,4},{3,5},{4,2},{5,3},{6,0},{7,1},{8,14},{9,15},{10,... | collective-permute-start | bytes 307208 | tf_op jit(solution)/shard_map/ppermute | solution.py:486
  36.3 1.7 %collective-permute-done.8 = bf16[16,3200]{1,0:T(8,128)(2,1)S(1)} collective-permute-done((bf16[16,3200]{1,0:T(8,128)(2,1)S(1)}, bf16[16,3200]{1,0:T(8,128)(2,1)S(1)}, u32[]{:S(2)}, u32[]{:S(2)}) %collective-permute-start.8) | collective-permute-done | bytes 102432 | tf_op jit(solution)/shard_map/ppermute | solution.py:486
  38.0 1.8 %collective-permute-done.9 = bf16[16,3200]{1,0:T(8,128)(2,1)S(1)} collective-permute-done((bf16[16,3200]{1,0:T(8,128)(2,1)S(1)}, bf16[16,3200]{1,0:T(8,128)(2,1)S(1)}, u32[]{:S(2)}, u32[]{:S(2)}) %collective-permute-start.9) | collective-permute-done | bytes 102432 | tf_op jit(solution)/shard_map/ppermute | solution.py:486
  39.8 0.9 %collective-permute-done.10 = bf16[16,3200]{1,0:T(8,128)(2,1)S(1)} collective-permute-done((bf16[16,3200]{1,0:T(8,128)(2,1)S(1)}, bf16[16,3200]{1,0:T(8,128)(2,1)S(1)}, u32[]{:S(2)}, u32[]{:S(2)}) %collective-permute-start.10) | collective-permute-done | bytes 102432 | tf_op jit(solution)/shard_map/ppermute | solution.py:486
  40.8 1.0 %shard_map.93 = (f32[128,3200]{1,0:T(8,128)S(1)}, bf16[128,128]{1,0:T(8,128)(2,1)S(1)}, f32[128,128]{1,0:T(8,128)S(1)}, f32[128,128]{1,0:T(8,128)S(1)}, bf16[256,128]{1,0:T(8,128)(2,1)S(1)}) custom-call(s32[2]{0:T(128)S(1)} %pad_add_fusion.meta, bf16[128,3200]{1,0:T(8,128)(2,1)S(1)} %get-tuple-element.54.normed, bf16[2,128,640]{2,1,0:T(8,128)(2,1)S(1)} %copy-done, ...), custom_call_target="tpu_custom_call" | custom-call | bytes 3082248 | tf_op jit(solution)/shard_map/pallas_call | solution.py:471
  41.9 0.7 collective-permute-done.11.other
  42.5 2.2 %shard_map.94 = (f32[128,3200]{1,0:T(8,128)S(1)}, bf16[128,3200]{1,0:T(8,128)(2,1)S(1)}, bf16[32,3200]{1,0:T(8,128)(2,1)S(1)}, bf16[32,3200]{1,0:T(8,128)(2,1)S(...) custom-call(bf16[64,3200]{1,0:T(8,128)(2,1)S(1)} %constant_dynamic-update-slice_fusion.own, ...), custom_call_target="tpu_custom_call" | custom-call | bytes 7615488 | tf_op jit(solution)/shard_map/pallas_call | solution.py:471
  44.8 1.6 %collective-permute-start.12 = (bf16[32,3200]{1,0:T(8,128)(2,1)S(1)}, bf16[32,3200]{1,0:T(8,128)(2,1)S(1)}, u32[]{:S(2)}, u32[]{:S(2)}) collective-permute-start(bf16[32,3200]{1,0:T(8,128)(2,1)S(1)} %get-tuple-element.60), channel_id=1, source_target_pairs={{0,6},{1,7},{2,4},{3,5},{4,2},{5,3},{6,0},{7,1},{8,14},{9,15},{10,... | collective-permute-start | bytes 614408 | tf_op jit(solution)/shard_map/ppermute | solution.py:486
  46.4 1.6 %collective-permute-start.13 = (bf16[32,3200]{1,0:T(8,128)(2,1)S(1)}, bf16[32,3200]{1,0:T(8,128)(2,1)S(1)}, u32[]{:S(2)}, u32[]{:S(2)}) collective-permute-start(bf16[32,3200]{1,0:T(8,128)(2,1)S(1)} %get-tuple-element.61), channel_id=1, source_target_pairs={{0,4},{1,5},{2,6},{3,7},{4,0},{5,1},{6,2},{7,3},{8,12},{9,13},{10,... | collective-permute-start | bytes 614408 | tf_op jit(solution)/shard_map/ppermute | solution.py:486
  48.0 0.4 collective-permute-start.14
  48.3 5.4 %collective-permute-done.12.refs_0_ = bf16[32,3200]{1,0:T(8,128)(2,1)S(1)} collective-permute-done((bf16[32,3200]{1,0:T(8,128)(2,1)S(1)}, bf16[32,3200]{1,0:T(8,128)(2,1)S(1)}, u32[]{:S(2)}, u32[]{:S(2)}) %collective-permute-start.12) | collective-permute-done | bytes 204832 | tf_op jit(solution)/shard_map/ppermute | solution.py:486
  53.7 3.8 %collective-permute-done.13.refs_1_ = bf16[32,3200]{1,0:T(8,128)(2,1)S(1)} collective-permute-done((bf16[32,3200]{1,0:T(8,128)(2,1)S(1)}, bf16[32,3200]{1,0:T(8,128)(2,1)S(1)}, u32[]{:S(2)}, u32[]{:S(2)}) %collective-permute-start.13) | collective-permute-done | bytes 204832 | tf_op jit(solution)/shard_map/ppermute | solution.py:486
  57.5 2.0 %shard_map.95 = (bf16[16,3200]{1,0:T(8,128)(2,1)S(1)}, bf16[16,3200]{1,0:T(8,128)(2,1)S(1)}, bf16[16,3200]{1,0:T(8,128)(2,1)S(1)}, bf16[16,3200]{1,0:T(8,128)(2,...) custom-call(s32[2]{0:T(128)S(1)} %pad_add_fusion.meta, ...), custom_call_target="tpu_custom_call" | custom-call | bytes 1638408 | tf_op jit(solution)/shard_map/pallas_call | solution.py:471
  59.5 1.5 %collective-permute-start.15 = (bf16[16,3200]{1,0:T(8,128)(2,1)S(1)}, bf16[16,3200]{1,0:T(8,128)(2,1)S(1)}, u32[]{:S(2)}, u32[]{:S(2)}) collective-permute-start(bf16[16,3200]{1,0:T(8,128)(2,1)S(1)} %get-tuple-element.65), channel_id=1, source_target_pairs={{0,2},{1,3},{2,0},{3,1},{4,6},{5,7},{6,4},{7,5},{8,10},{9,11},{10,... | collective-permute-start | bytes 307208 | tf_op jit(solution)/shard_map/ppermute | solution.py:486
  61.0 0.6 collective-permute-start.16
  61.6 1.4 %collective-permute-start.17 = (bf16[16,3200]{1,0:T(8,128)(2,1)S(1)}, bf16[16,3200]{1,0:T(8,128)(2,1)S(1)}, u32[]{:S(2)}, u32[]{:S(2)}) collective-permute-start(bf16[16,3200]{1,0:T(8,128)(2,1)S(1)} %get-tuple-element.67), channel_id=1, source_target_pairs={{0,6},{1,7},{2,4},{3,5},{4,2},{5,3},{6,0},{7,1},{8,14},{9,15},{10,... | collective-permute-start | bytes 307208 | tf_op jit(solution)/shard_map/ppermute | solution.py:486
  63.1 3.3 %collective-permute-start.18 = (bf16[16,3200]{1,0:T(8,128)(2,1)S(1)}, bf16[16,3200]{1,0:T(8,128)(2,1)S(1)}, u32[]{:S(2)}, u32[]{:S(2)}) collective-permute-start(bf16[16,3200]{1,0:T(8,128)(2,1)S(1)} %get-tuple-element.68), channel_id=1, source_target_pairs={{0,8},{1,9},{2,10},{3,11},{4,12},{5,13},{6,14},{7,15},{8,0},{9,1},... | collective-permute-start | bytes 307208 | tf_op jit(solution)/shard_map/ppermute | solution.py:486
  66.4 0.5 collective-permute-start.19
  66.9 3.0 %collective-permute-start.20 = (bf16[16,3200]{1,0:T(8,128)(2,1)S(1)}, bf16[16,3200]{1,0:T(8,128)(2,1)S(1)}, u32[]{:S(2)}, u32[]{:S(2)}) collective-permute-start(bf16[16,3200]{1,0:T(8,128)(2,1)S(1)} %get-tuple-element.70), channel_id=1, source_target_pairs={{0,12},{1,13},{2,14},{3,15},{4,8},{5,9},{6,10},{7,11},{8,4},{9,5},... | collective-permute-start | bytes 307208 | tf_op jit(solution)/shard_map/ppermute | solution.py:486
  69.9 1.4 %collective-permute-start.21 = (bf16[16,3200]{1,0:T(8,128)(2,1)S(1)}, bf16[16,3200]{1,0:T(8,128)(2,1)S(1)}, u32[]{:S(2)}, u32[]{:S(2)}) collective-permute-start(bf16[16,3200]{1,0:T(8,128)(2,1)S(1)} %get-tuple-element.71), channel_id=1, source_target_pairs={{0,14},{1,15},{2,12},{3,13},{4,10},{5,11},{6,8},{7,9},{8,6},{9,7},... | collective-permute-start | bytes 307208 | tf_op jit(solution)/shard_map/ppermute | solution.py:486
  71.3 10.2 %collective-permute-done.19 = bf16[16,3200]{1,0:T(8,128)(2,1)S(1)} collective-permute-done((bf16[16,3200]{1,0:T(8,128)(2,1)S(1)}, bf16[16,3200]{1,0:T(8,128)(2,1)S(1)}, u32[]{:S(2)}, u32[]{:S(2)}) %collective-permute-start.19) | collective-permute-done | bytes 102432 | tf_op jit(solution)/shard_map/ppermute | solution.py:486
  81.5 0.1 add_convert_fusion.own
  81.7 1.0 %shard_map.96 = (f32[128,3200]{1,0:T(8,128)S(1)}, bf16[128,128]{1,0:T(8,128)(2,1)S(1)}, f32[128,128]{1,0:T(8,128)S(1)}) custom-call(s32[2]{0:T(128)S(1)} %pad_add_fusion.meta, bf16[128,3200]{1,0:T(8,128)(2,1)S(1)} %get-tuple-element.73.normed, bf16[2,128,640]{2,1,0:T(8,128)(2,1)S(1)} %copy-done, f32[2,128]{1,0:T(2,128)S(1)} %copy-done.5, ...), custom_call_target="tpu_custom_call" | custom-call | bytes 2950152 | tf_op jit(solution)/shard_map/pallas_call | solution.py:471
  82.7 0.7 collective-permute-done.22.other
  83.5 3.9 %shard_map.97 = bf16[40,40,128]{2,1,0:T(8,128)(2,1)} custom-call(s32[2]{0:T(128)S(1)} %pad_add_fusion.meta, bf16[64,3200]{1,0:T(8,128)(2,1)S(1)} %add_convert_fusion.own, bf16[64,3200]{1,0:T(8,128)(2,1)S(1)} %collective-permute-done.22.other, f32[128,3200]{1,0:T(8,128)S(1)} %get-tuple-element.72.stream, f32[128,3200]{1,0:T(8,128)S(1)} %get-tuple-element.74.gate, ...), custom_call_target="tpu_custom_call" | custom-call | bytes 4866568 | tf_op jit(solution)/shard_map/pallas_call | solution.py:471
  (35 shorter events, 0.3 us)
Async XLA Ops:
  0.0 3.2 %collective-permute-start = (bf16[40,40,128]{2,1,0:T(8,128)(2,1)}, bf16[40,40,128]{2,1,0:T(8,128)(2,1)S(1)}, u32[]{:S(2)}, u32[]{:S(2)}) collective-permute-start(bf16[40,40,128]{2,1,0:T(8,128)(2,1)} %own.1), channel_id=1, source_target_pairs={{0,1},{1,0},{2,3},{3,2},{4,5},{5,4},{6,7},{7,6},{8,9},{9,8},{10,11... | collective-permute-start | bytes 1228808 | tf_op jit(solution)/shard_map/ppermute | solution.py:490
  2.0 38.8 %copy-start.5 = (f32[2,128]{1,0:T(2,128)S(1)}, f32[2,128]{1,0:T(2,128)}, u32[]{:S(2)}) copy-start(f32[2,128]{1,0:T(2,128)} %middle_gain.3) | copy-start | bytes 3076
  2.0 38.8 %copy-start.6 = (f32[2,128]{1,0:T(2,128)S(1)}, f32[2,128]{1,0:T(2,128)}, u32[]{:S(2)}) copy-start(f32[2,128]{1,0:T(2,128)} %entry_gain.1) | copy-start | bytes 3076
  2.1 38.7 %copy-start = (bf16[2,128,640]{2,1,0:T(8,128)(2,1)S(1)}, bf16[2,128,640]{2,1,0:T(8,128)(2,1)}, u32[]{:S(2)}) copy-start(bf16[2,128,640]{2,1,0:T(8,128)(2,1)} %weight.3) | copy-start | bytes 983044
  3.2 1.0 %copy-start.1 = (bf16[40,40,128]{2,1,0:T(8,128)(2,1)S(1)}, bf16[40,40,128]{2,1,0:T(8,128)(2,1)}, u32[]{:S(2)}) copy-start(bf16[40,40,128]{2,1,0:T(8,128)(2,1)} %own.1) | copy-start | bytes 1228804
  4.2 36.6 %copy-start.2 = (bf16[2,128,128]{2,1,0:T(8,128)(2,1)S(1)}, bf16[2,128,128]{2,1,0:T(8,128)(2,1)}, u32[]{:S(2)}) copy-start(bf16[2,128,128]{2,1,0:T(8,128)(2,1)} %out_weight.3) | copy-start | bytes 196612
  6.0 11.3 %collective-permute-start.1 = (bf16[16,3200]{1,0:T(8,128)(2,1)S(1)}, bf16[16,3200]{1,0:T(8,128)(2,1)S(1)}, u32[]{:S(2)}, u32[]{:S(2)}) collective-permute-start(bf16[16,3200]{1,0:T(8,128)(2,1)S(1)} %get-tuple-element.41), channel_id=1, source_target_pairs={{0,8},{1,9},{2,10},{3,11},{4,12},{5,13},{6,14},{7,15},{8,0},{9,1},... | collective-permute-start | bytes 307208 | tf_op jit(solution)/shard_map/ppermute | solution.py:486
  9.7 11.6 %collective-permute-start.2 = (bf16[16,3200]{1,0:T(8,128)(2,1)S(1)}, bf16[16,3200]{1,0:T(8,128)(2,1)S(1)}, u32[]{:S(2)}, u32[]{:S(2)}) collective-permute-start(bf16[16,3200]{1,0:T(8,128)(2,1)S(1)} %get-tuple-element.42), channel_id=1, source_target_pairs={{0,10},{1,11},{2,8},{3,9},{4,14},{5,15},{6,12},{7,13},{8,2},{9,3},... | collective-permute-start | bytes 307208 | tf_op jit(solution)/shard_map/ppermute | solution.py:486
  10.9 19.8 %collective-permute-start.3 = (bf16[32,3200]{1,0:T(8,128)(2,1)S(1)}, bf16[32,3200]{1,0:T(8,128)(2,1)S(1)}, u32[]{:S(2)}, u32[]{:S(2)}) collective-permute-start(bf16[32,3200]{1,0:T(8,128)(2,1)S(1)} %get-tuple-element.43), channel_id=1, source_target_pairs={{0,4},{1,5},{2,6},{3,7},{4,0},{5,1},{6,2},{7,3},{8,12},{9,13},{10,... | collective-permute-start | bytes 614408 | tf_op jit(solution)/shard_map/ppermute | solution.py:486
  12.5 18.2 %collective-permute-start.5 = (bf16[32,3200]{1,0:T(8,128)(2,1)S(1)}, bf16[32,3200]{1,0:T(8,128)(2,1)S(1)}, u32[]{:S(2)}, u32[]{:S(2)}) collective-permute-start(bf16[32,3200]{1,0:T(8,128)(2,1)S(1)} %get-tuple-element.45), channel_id=1, source_target_pairs={{0,6},{1,7},{2,4},{3,5},{4,2},{5,3},{6,0},{7,1},{8,14},{9,15},{10,... | collective-permute-start | bytes 614408 | tf_op jit(solution)/shard_map/ppermute | solution.py:486
  12.7 18.0 %collective-permute-start.7 = (bf16[32,3200]{1,0:T(8,128)(2,1)S(1)}, bf16[32,3200]{1,0:T(8,128)(2,1)S(1)}, u32[]{:S(2)}, u32[]{:S(2)}) collective-permute-start(bf16[32,3200]{1,0:T(8,128)(2,1)S(1)} %get-tuple-element.47), channel_id=1, source_target_pairs={{0,2},{1,3},{2,0},{3,1},{4,6},{5,7},{6,4},{7,5},{8,10},{9,11},{10,... | collective-permute-start | bytes 614408 | tf_op jit(solution)/shard_map/ppermute | solution.py:486
  17.3 12.4 %collective-permute-start.4 = (bf16[16,3200]{1,0:T(8,128)(2,1)S(1)}, bf16[16,3200]{1,0:T(8,128)(2,1)S(1)}, u32[]{:S(2)}, u32[]{:S(2)}) collective-permute-start(bf16[16,3200]{1,0:T(8,128)(2,1)S(1)} %get-tuple-element.44), channel_id=1, source_target_pairs={{0,12},{1,13},{2,14},{3,15},{4,8},{5,9},{6,10},{7,11},{8,4},{9,5},... | collective-permute-start | bytes 307208 | tf_op jit(solution)/shard_map/ppermute | solution.py:486
  21.3 9.4 %collective-permute-start.6 = (bf16[16,3200]{1,0:T(8,128)(2,1)S(1)}, bf16[16,3200]{1,0:T(8,128)(2,1)S(1)}, u32[]{:S(2)}, u32[]{:S(2)}) collective-permute-start(bf16[16,3200]{1,0:T(8,128)(2,1)S(1)} %get-tuple-element.46), channel_id=1, source_target_pairs={{0,14},{1,15},{2,12},{3,13},{4,10},{5,11},{6,8},{7,9},{8,6},{9,7},... | collective-permute-start | bytes 307208 | tf_op jit(solution)/shard_map/ppermute | solution.py:486
  32.8 5.3 %collective-permute-start.8 = (bf16[16,3200]{1,0:T(8,128)(2,1)S(1)}, bf16[16,3200]{1,0:T(8,128)(2,1)S(1)}, u32[]{:S(2)}, u32[]{:S(2)}) collective-permute-start(bf16[16,3200]{1,0:T(8,128)(2,1)S(1)} %get-tuple-element.50), channel_id=1, source_target_pairs={{0,2},{1,3},{2,0},{3,1},{4,6},{5,7},{6,4},{7,5},{8,10},{9,11},{10,... | collective-permute-start | bytes 307208 | tf_op jit(solution)/shard_map/ppermute | solution.py:486
  34.8 5.0 %collective-permute-start.9 = (bf16[16,3200]{1,0:T(8,128)(2,1)S(1)}, bf16[16,3200]{1,0:T(8,128)(2,1)S(1)}, u32[]{:S(2)}, u32[]{:S(2)}) collective-permute-start(bf16[16,3200]{1,0:T(8,128)(2,1)S(1)} %get-tuple-element.51), channel_id=1, source_target_pairs={{0,4},{1,5},{2,6},{3,7},{4,0},{5,1},{6,2},{7,3},{8,12},{9,13},{10,... | collective-permute-start | bytes 307208 | tf_op jit(solution)/shard_map/ppermute | solution.py:486
  34.8 5.9 %collective-permute-start.10 = (bf16[16,3200]{1,0:T(8,128)(2,1)S(1)}, bf16[16,3200]{1,0:T(8,128)(2,1)S(1)}, u32[]{:S(2)}, u32[]{:S(2)}) collective-permute-start(bf16[16,3200]{1,0:T(8,128)(2,1)S(1)} %get-tuple-element.52), channel_id=1, source_target_pairs={{0,6},{1,7},{2,4},{3,5},{4,2},{5,3},{6,0},{7,1},{8,14},{9,15},{10,... | collective-permute-start | bytes 307208 | tf_op jit(solution)/shard_map/ppermute | solution.py:486
  40.7 1.8 %collective-permute-start.11 = (bf16[64,3200]{1,0:T(8,128)(2,1)S(1)}, bf16[64,3200]{1,0:T(8,128)(2,1)S(1)}, u32[]{:S(2)}, u32[]{:S(2)}) collective-permute-start(bf16[64,3200]{1,0:T(8,128)(2,1)S(1)} %constant_dynamic-update-slice_fusion.own), channel_id=1, source_target_pairs={{0,1},{1,0},{2,3},{3,2},{4,5},{5,4},{6,7},{7,6},{8,9},{9,8},{10,11... | collective-permute-start | bytes 1228808 | tf_op jit(solution)/shard_map/ppermute | solution.py:490
  44.8 8.9 %collective-permute-start.12 = (bf16[32,3200]{1,0:T(8,128)(2,1)S(1)}, bf16[32,3200]{1,0:T(8,128)(2,1)S(1)}, u32[]{:S(2)}, u32[]{:S(2)}) collective-permute-start(bf16[32,3200]{1,0:T(8,128)(2,1)S(1)} %get-tuple-element.60), channel_id=1, source_target_pairs={{0,6},{1,7},{2,4},{3,5},{4,2},{5,3},{6,0},{7,1},{8,14},{9,15},{10,... | collective-permute-start | bytes 614408 | tf_op jit(solution)/shard_map/ppermute | solution.py:486
  46.4 11.1 %collective-permute-start.13 = (bf16[32,3200]{1,0:T(8,128)(2,1)S(1)}, bf16[32,3200]{1,0:T(8,128)(2,1)S(1)}, u32[]{:S(2)}, u32[]{:S(2)}) collective-permute-start(bf16[32,3200]{1,0:T(8,128)(2,1)S(1)} %get-tuple-element.61), channel_id=1, source_target_pairs={{0,4},{1,5},{2,6},{3,7},{4,0},{5,1},{6,2},{7,3},{8,12},{9,13},{10,... | collective-permute-start | bytes 614408 | tf_op jit(solution)/shard_map/ppermute | solution.py:486
  48.0 9.5 %collective-permute-start.14 = (bf16[32,3200]{1,0:T(8,128)(2,1)S(1)}, bf16[32,3200]{1,0:T(8,128)(2,1)S(1)}, u32[]{:S(2)}, u32[]{:S(2)}) collective-permute-start(bf16[32,3200]{1,0:T(8,128)(2,1)S(1)} %get-tuple-element.62), channel_id=1, source_target_pairs={{0,2},{1,3},{2,0},{3,1},{4,6},{5,7},{6,4},{7,5},{8,10},{9,11},{10,... | collective-permute-start | bytes 614408 | tf_op jit(solution)/shard_map/ppermute | solution.py:486
  57.5 25.9 %copy-start.3 = (bf16[128,512]{1,0:T(8,128)(2,1)S(1)}, bf16[128,512]{1,0:T(8,128)(2,1)}, u32[]{:S(2)}) copy-start(bf16[128,512]{1,0:T(8,128)(2,1)} %expand.1) | copy-start | bytes 393220
  57.5 25.9 %copy-start.4 = (bf16[512,128]{1,0:T(8,128)(2,1)S(1)}, bf16[512,128]{1,0:T(8,128)(2,1)}, u32[]{:S(2)}) copy-start(bf16[512,128]{1,0:T(8,128)(2,1)} %shrink.1) | copy-start | bytes 393220
  57.5 25.9 %copy-start.7 = (f32[128]{0:T(128)S(1)}, f32[128]{0:T(128)}, u32[]{:S(2)}) copy-start(f32[128]{0:T(128)} %param.15) | copy-start | bytes 1540
  59.5 7.3 %collective-permute-start.15 = (bf16[16,3200]{1,0:T(8,128)(2,1)S(1)}, bf16[16,3200]{1,0:T(8,128)(2,1)S(1)}, u32[]{:S(2)}, u32[]{:S(2)}) collective-permute-start(bf16[16,3200]{1,0:T(8,128)(2,1)S(1)} %get-tuple-element.65), channel_id=1, source_target_pairs={{0,2},{1,3},{2,0},{3,1},{4,6},{5,7},{6,4},{7,5},{8,10},{9,11},{10,... | collective-permute-start | bytes 307208 | tf_op jit(solution)/shard_map/ppermute | solution.py:486
  61.0 8.9 %collective-permute-start.16 = (bf16[16,3200]{1,0:T(8,128)(2,1)S(1)}, bf16[16,3200]{1,0:T(8,128)(2,1)S(1)}, u32[]{:S(2)}, u32[]{:S(2)}) collective-permute-start(bf16[16,3200]{1,0:T(8,128)(2,1)S(1)} %get-tuple-element.66), channel_id=1, source_target_pairs={{0,4},{1,5},{2,6},{3,7},{4,0},{5,1},{6,2},{7,3},{8,12},{9,13},{10,... | collective-permute-start | bytes 307208 | tf_op jit(solution)/shard_map/ppermute | solution.py:486
  61.6 9.7 %collective-permute-start.17 = (bf16[16,3200]{1,0:T(8,128)(2,1)S(1)}, bf16[16,3200]{1,0:T(8,128)(2,1)S(1)}, u32[]{:S(2)}, u32[]{:S(2)}) collective-permute-start(bf16[16,3200]{1,0:T(8,128)(2,1)S(1)} %get-tuple-element.67), channel_id=1, source_target_pairs={{0,6},{1,7},{2,4},{3,5},{4,2},{5,3},{6,0},{7,1},{8,14},{9,15},{10,... | collective-permute-start | bytes 307208 | tf_op jit(solution)/shard_map/ppermute | solution.py:486
  63.1 8.2 %collective-permute-start.18 = (bf16[16,3200]{1,0:T(8,128)(2,1)S(1)}, bf16[16,3200]{1,0:T(8,128)(2,1)S(1)}, u32[]{:S(2)}, u32[]{:S(2)}) collective-permute-start(bf16[16,3200]{1,0:T(8,128)(2,1)S(1)} %get-tuple-element.68), channel_id=1, source_target_pairs={{0,8},{1,9},{2,10},{3,11},{4,12},{5,13},{6,14},{7,15},{8,0},{9,1},... | collective-permute-start | bytes 307208 | tf_op jit(solution)/shard_map/ppermute | solution.py:486
  66.4 15.1 %collective-permute-start.19 = (bf16[16,3200]{1,0:T(8,128)(2,1)S(1)}, bf16[16,3200]{1,0:T(8,128)(2,1)S(1)}, u32[]{:S(2)}, u32[]{:S(2)}) collective-permute-start(bf16[16,3200]{1,0:T(8,128)(2,1)S(1)} %get-tuple-element.69), channel_id=1, source_target_pairs={{0,10},{1,11},{2,8},{3,9},{4,14},{5,15},{6,12},{7,13},{8,2},{9,3},... | collective-permute-start | bytes 307208 | tf_op jit(solution)/shard_map/ppermute | solution.py:486
  66.9 14.6 %collective-permute-start.20 = (bf16[16,3200]{1,0:T(8,128)(2,1)S(1)}, bf16[16,3200]{1,0:T(8,128)(2,1)S(1)}, u32[]{:S(2)}, u32[]{:S(2)}) collective-permute-start(bf16[16,3200]{1,0:T(8,128)(2,1)S(1)} %get-tuple-element.70), channel_id=1, source_target_pairs={{0,12},{1,13},{2,14},{3,15},{4,8},{5,9},{6,10},{7,11},{8,4},{9,5},... | collective-permute-start | bytes 307208 | tf_op jit(solution)/shard_map/ppermute | solution.py:486
  69.9 11.6 %collective-permute-start.21 = (bf16[16,3200]{1,0:T(8,128)(2,1)S(1)}, bf16[16,3200]{1,0:T(8,128)(2,1)S(1)}, u32[]{:S(2)}, u32[]{:S(2)}) collective-permute-start(bf16[16,3200]{1,0:T(8,128)(2,1)S(1)} %get-tuple-element.71), channel_id=1, source_target_pairs={{0,14},{1,15},{2,12},{3,13},{4,10},{5,11},{6,8},{7,9},{8,6},{9,7},... | collective-permute-start | bytes 307208 | tf_op jit(solution)/shard_map/ppermute | solution.py:486
  81.6 1.8 %collective-permute-start.22 = (bf16[64,3200]{1,0:T(8,128)(2,1)S(1)}, bf16[64,3200]{1,0:T(8,128)(2,1)S(1)}, u32[]{:S(2)}, u32[]{:S(2)}) collective-permute-start(bf16[64,3200]{1,0:T(8,128)(2,1)S(1)} %add_convert_fusion.own), channel_id=1, source_target_pairs={{0,1},{1,0},{2,3},{3,2},{4,5},{5,4},{6,7},{7,6},{8,9},{9,8},{10,11... | collective-permute-start | bytes 1228808 | tf_op jit(solution)/shard_map/ppermute | solution.py:490

commit v4 on v3

--- a/solution.py
+++ b/solution.py
@@ -131,7 +131,8 @@
     return result.astype(jnp.bfloat16).reshape(row_count, col_count, channels)
 
 
-EVERYWHERE = (4, 5, 2, 6, 3, 7, 1, 0)
+FIRST_ORDER = (4, 5, 2, 6, 3, 7, 1, 0)
+LAST_ORDER = (4, 2, 5, 3, 6, 1, 7, 0)
 WITHIN_HALF = (3, 2, 1, 0)
 
 
@@ -185,7 +186,8 @@
     return lax.broadcasted_iota(jnp.int32, (GROUP, LANES), 1)
 
 
-def split_group(chunk, width, lane):
+def split_group(chunk, width):
+    lane = lane_index()
     pieces = []
     for row in range(GROUP):
         first, offset = divmod(row * width, LANES)
@@ -196,7 +198,7 @@
                 after = chunk[:, (first + 1) * LANES : (first + 2) * LANES]
                 after = pltpu.roll(after, LANES - offset, 1)
                 piece = jnp.where(lane < LANES - offset, piece, after)
-        pieces.append(jnp.where(lane < width, piece, 0.0))
+        pieces.append(piece)
     return pieces
 
 
@@ -233,11 +235,11 @@
     return jnp.concatenate(picked, axis=0).astype(BF16)
 
 
-def send_sides(normed, weights, mask, messages, lanes):
+def send_sides(normed, weights, messages, lanes):
     quarter = weights.shape[0] // 4
     projected = jnp.dot(weights, normed, preferred_element_type=F32)
-    left = mask * sigmoid(projected[quarter : 2 * quarter]) * projected[:quarter]
-    right = mask * sigmoid(projected[3 * quarter :]) * projected[2 * quarter : 3 * quarter]
+    left = sigmoid(projected[quarter : 2 * quarter]) * projected[:quarter]
+    right = sigmoid(projected[3 * quarter :]) * projected[2 * quarter : 3 * quarter]
     size = quarter // 4
     for k in range(4):
         rows = slice(k * size, (k + 1) * size)
@@ -252,12 +254,12 @@
     )
 
 
-def first_kernel(meta, own, other, mask, weight, *refs):
+def first_kernel(meta, own, other, gain, weight, *refs):
     stream, normed_out, *messages, table = refs
     first = meta[0] == 0
     rows, cols, channels = own.shape
     width = GROUP * 2 * cols
-    factors = column_of(mask[:, stream.shape[1] :], channels)
+    factors = column_of(gain[...], channels)
     table[...] = weight[...].astype(F32).T
     weights = side_weights(table, meta)
 
@@ -273,7 +275,7 @@
     def _(lanes):
         normed = norm_rows(stream[:, lanes], factors).astype(BF16)
         normed_out[:, lanes] = normed
-        send_sides(normed, weights, mask[:, lanes], messages, lanes)
+        send_sides(normed, weights, messages, lanes)
 
 
 def gate_of(normed, weight, update):
@@ -283,8 +285,21 @@
     return sigmoid(jnp.dot(table, normed[...], preferred_element_type=F32))
 
 
-def first_gate_kernel(meta, normed, weight, entry_gain, middle_gain, out_weight, *refs):
-    gate, out_weights, middle, factor, weights, table, out_table, square = refs
+def chip_masks(bits, column, meta, masks, width):
+    dap, sub = meta[1] >> 1, meta[1] & 1
+    rows = masks.shape[1]
+    values = bits[...].astype(F32)
+    column[...] = jnp.broadcast_to(values, (LANES, values.shape[1])).T
+    parts = [values[:, b * width : (b + 1) * width] for b in range(2)]
+    parts = [jnp.concatenate([p, jnp.zeros((1, LANES - width), F32)], axis=1) for p in parts]
+    for k in range(8):
+        begin = aligned((dap ^ (k >> 1)) * rows, GROUP)
+        masks[k] = column[pl.ds(begin, rows), :] * jnp.where(sub == (k & 1), parts[0], parts[1])
+
+
+def first_gate_kernel(meta, normed, weight, entry_gain, middle_gain, out_weight, bits, *refs):
+    gate, out_weights, middle, factor, weights, masks, table, out_table, square, column = refs
+    chip_masks(bits, column, meta, masks, bits.shape[1] // 2)
     gate[...] = gate_of(normed, weight, 0)
     out_table[...] = out_weight[0].astype(F32)
     out_weights[...], middle[...] = output_weights(out_table, square, middle_gain[0:1, :], meta)
@@ -300,8 +315,24 @@
     out_weights[...], middle[...] = output_weights(out_table, square, middle_gain[1:2, :], meta)
 
 
-def outgoing_kernel(meta, *refs, rows, width):
-    messages, outs = dict(zip(EVERYWHERE, refs[:8])), refs[8:12]
+def spread_group(side, part, masks, begin, pitch, width):
+    for c in range(0, part.shape[0], GROUP):
+        for i, piece in enumerate(split_group(part[c : c + GROUP], width)):
+            side[pl.ds(c * pitch + begin + i, GROUP, stride=pitch), :] = piece * masks[i : i + 1]
+
+
+def gather_group(total, count, begin, pitch, width, lane):
+    joined = []
+    for c in range(0, count, GROUP):
+        pieces = [
+            total[pl.ds(c * pitch + begin + i, GROUP, stride=pitch), :] for i in range(GROUP)
+        ]
+        joined.append(join_group(pieces, width, lane))
+    return jnp.concatenate(joined, axis=0).astype(BF16)
+
+
+def outgoing_kernel(meta, masks, *refs, rows, width):
+    messages, outs = dict(zip(FIRST_ORDER, refs[:8])), refs[8:12]
     left, right, total = refs[12:]
     dap, sub = meta[1] >> 1, meta[1] & 1
     lane = lane_index()
@@ -311,29 +342,23 @@
 
     @steps(rows // GROUP)
     def _(step):
-        lanes = pl.ds(aligned(step * GROUP * width, LANES), GROUP * width)
+        lanes = pl.ds(step * GROUP * width, GROUP * width)
         for k in range(8):
             values = messages[k][:, lanes].astype(F32)
+            bits = masks[k, step * GROUP : (step + 1) * GROUP, :]
+            if k < 4:
+                begin = (k >> 1) * rows + step * GROUP
+                spread_group(left.at[k & 1], values[:count], bits, begin, pitch, width)
+                values = values[count:]
             source = dap ^ (k >> 1)
-            half = (source >> 1) ^ sub
-            near = (source & 1) * rows
-            if k < 4:
-                begin = ((k >> 1) & 1) * rows + step * GROUP
-                for c in range(0, count, GROUP):
-                    for i, piece in enumerate(split_group(values[c : c + GROUP], width, lane)):
-                        left[k & 1, pl.ds(c * pitch + begin + i, GROUP, stride=pitch), :] = piece
-                values = values[count:]
-            begin = half * (count * pitch) + near + step * GROUP
-            for c in range(0, count, GROUP):
-                for i, piece in enumerate(split_group(values[c : c + GROUP], width, lane)):
-                    right[k & 1, pl.ds(c * pitch + begin + i, GROUP, stride=pitch), :] = piece
-
-    @steps(count)
-    def _(c):
-        here = pl.ds(aligned(c * pitch, GROUP), span)
+            begin = ((source >> 1) ^ sub) * (count * pitch) + (source & 1) * rows + step * GROUP
+            spread_group(right.at[k & 1], values, bits, begin, pitch, width)
+
+    for c in range(count):
+        here = pl.ds(c * pitch, span)
         a = jnp.concatenate([left[0, here, :], left[1, here, :]], axis=1).astype(BF16)
         for half in range(2):
-            there = pl.ds(aligned(half * (count * pitch) + c * pitch, GROUP), span)
+            there = pl.ds((half * count + c) * pitch, span)
             b = jnp.concatenate([right[0, there, :], right[1, there, :]], axis=1).astype(BF16)
             total[half, here, 0:width] = lax.dot_general(
                 a, b, (((1,), (1,)), ((), ())), preferred_element_type=F32
@@ -341,20 +366,13 @@
 
     @steps(rows // GROUP)
     def _(step):
-        lanes = pl.ds(aligned(step * GROUP * width, LANES), GROUP * width)
+        lanes = pl.ds(step * GROUP * width, GROUP * width)
         for k in range(4):
             begin = (k >> 1) * rows + step * GROUP
-            joined = []
-            for c in range(0, count, GROUP):
-                pieces = [
-                    total[k & 1, pl.ds(c * pitch + begin + i, GROUP, stride=pitch), :]
-                    for i in range(GROUP)
-                ]
-                joined.append(join_group(pieces, width, lane))
-            outs[k][:, lanes] = jnp.concatenate(joined, axis=0).astype(BF16)
-
-
-def incoming_kernel(meta, *refs, rows, width):
+            outs[k][:, lanes] = gather_group(total.at[k & 1], count, begin, pitch, width, lane)
+
+
+def incoming_kernel(meta, masks, *refs, rows, width):
     messages, outs = dict(zip(WITHIN_HALF, refs[:4])), refs[4:12]
     left, right, total = refs[12:]
     dap, sub = meta[1] >> 1, meta[1] & 1
@@ -362,45 +380,35 @@
     count = outs[0].shape[0]
     span = 2 * rows
     pitch = span + GROUP
-    tall = 2 * width
-    tall_pitch = tall + GROUP
+    tall = 2 * width + GROUP
 
     @steps(rows // GROUP)
     def _(step):
-        lanes = pl.ds(aligned(step * GROUP * width, LANES), GROUP * width)
+        lanes = pl.ds(step * GROUP * width, GROUP * width)
         for k in range(4):
             values = messages[k][:, lanes].astype(F32)
+            bits = masks[k, step * GROUP : (step + 1) * GROUP, :]
             begin = (k >> 1) * rows + step * GROUP
-            for side, part in ((left, values[:count]), (right, values[count:])):
-                for c in range(0, count, GROUP):
-                    for i, piece in enumerate(split_group(part[c : c + GROUP], width, lane)):
-                        side[k & 1, pl.ds(c * pitch + begin + i, GROUP, stride=pitch), :] = piece
-
-    @steps(count)
-    def _(c):
-        here = pl.ds(aligned(c * pitch, GROUP), span)
+            spread_group(left.at[k & 1], values[:count], bits, begin, pitch, width)
+            spread_group(right.at[k & 1], values[count:], bits, begin, pitch, width)
+
+    for c in range(count):
+        here = pl.ds(c * pitch, span)
         b = jnp.concatenate([right[0, here, :], right[1, here, :]], axis=1).astype(BF16)
         for block in range(2):
             a = left[block, here, 0:width].astype(BF16)
             product = lax.dot_general(a, b, (((0,), (0,)), ((), ())), preferred_element_type=F32)
-            there = pl.ds(aligned(c * tall_pitch + block * width, GROUP), width)
+            there = pl.ds(c * tall + block * width, width)
             total[0, there, :] = product[:, :LANES]
             total[1, there, :] = product[:, LANES:]
 
     @steps(rows // GROUP)
     def _(step):
-        lanes = pl.ds(aligned(step * GROUP * width, LANES), GROUP * width)
+        lanes = pl.ds(step * GROUP * width, GROUP * width)
         for k in range(8):
             target = dap ^ (k >> 1)
             begin = ((target >> 1) ^ sub) * width + (target & 1) * rows + step * GROUP
-            joined = []
-            for c in range(0, count, GROUP):
-                pieces = [
-                    total[k & 1, pl.ds(c * tall_pitch + begin + i, GROUP, stride=tall_pitch), :]
-                    for i in range(GROUP)
-                ]
-                joined.append(join_group(pieces, width, lane))
-            outs[k][:, lanes] = jnp.concatenate(joined, axis=0).astype(BF16)
+            outs[k][:, lanes] = gather_group(total.at[k & 1], count, begin, tall, width, lane)
 
 
 def output_weights(table, square, gain, meta):
@@ -421,7 +429,7 @@
 
 
 def second_kernel(
-    own, other, stream, gate, mask, out_weights, middle, factor, weights, *refs, width
+    own, other, stream, gate, out_weights, middle, factor, weights, *refs, width
 ):
     stream_out, normed_out, *messages = refs
     channels = stream.shape[0]
@@ -434,7 +442,7 @@
         stream_out[:, lanes] = values
         normed = norm_rows(values, factors).astype(BF16)
         normed_out[:, lanes] = normed
-        send_sides(normed, weights[...], mask[:, lanes], messages, lanes)
+        send_sides(normed, weights[...], messages, lanes)
 
 
 def last_scratch(channels, pairs):
@@ -517,28 +525,27 @@
 
     square32, square16 = shape((channels, channels), F32), shape((hidden, channels), BF16)
     side_weight = shape((2 * hidden, channels), BF16)
-    mask_values = residue_mask.astype(F32)
-    row_mask = lax.dynamic_slice_in_dim(mask_values, dap * rows, rows)
-    col_mask = lax.dynamic_slice_in_dim(mask_values, sub * width, width)
-    mask = (row_mask[:, None] * col_mask[None, :]).reshape(1, pairs)
-    mask = jnp.concatenate([mask, entry_gain[0:1]], axis=1)
-
     stream, normed, *messages = call(
         first_kernel,
         [flat32, flat16] + [sides] * 4 + [rights] * 4,
         [pltpu.VMEM((4 * hidden, channels), F32)],
-        (meta, pair_input, other_input, mask, input_weight[0, :, : 4 * hidden]),
-    )
-    arrived = [to_chip(messages[k], k) for k in EVERYWHERE]
-    gate, out_weights, middle, factor, weights = call(
+        (meta, pair_input, other_input, entry_gain[0:1], input_weight[0, :, : 4 * hidden]),
+    )
+    arrived = [to_chip(messages[k], k) for k in FIRST_ORDER]
+    length = residue_mask.shape[0]
+    gate, out_weights, middle, factor, weights, masks = call(
         first_gate_kernel,
-        [flat32, square16, square32, square32, side_weight],
+        [flat32, square16, square32, square32, side_weight, shape((8, rows, LANES), F32)],
         [
             pltpu.VMEM((4 * hidden, channels), F32),
             pltpu.VMEM((hidden, channels), F32),
             pltpu.VMEM((hidden, LANES), F32),
+            pltpu.VMEM((length, LANES), F32),
         ],
-        (meta, normed, input_weight, entry_gain, middle_gain, output_weight),
+        (
+            meta, normed, input_weight, entry_gain, middle_gain, output_weight,
+            residue_mask.reshape(1, length),
+        ),
     )
     sums = call(
         functools.partial(outgoing_kernel, rows=rows, width=width),
@@ -548,7 +555,7 @@
             pltpu.VMEM((2, 2 * part * span, LANES), F32),
             pltpu.VMEM((2, part * span, LANES), F32),
         ],
-        (meta, *arrived),
+        (meta, masks, *arrived),
     )
     returned = [to_chip(sums[k], k) for k in WITHIN_HALF]
     own = jnp.concatenate(returned[::-1], axis=0)
@@ -557,7 +564,7 @@
         functools.partial(second_kernel, width=wide),
         [flat32, flat16] + [sides] * 4,
         [],
-        (own, other, stream, gate, mask, out_weights, middle, factor, weights),
+        (own, other, stream, gate, out_weights, middle, factor, weights),
         0,
     )
     arrived = [to_chip(messages[k], k) for k in WITHIN_HALF]
@@ -575,9 +582,9 @@
             pltpu.VMEM((2, part * span, LANES), F32),
             pltpu.VMEM((2, part * tall, LANES), F32),
         ],
-        (meta, *arrived),
-    )
-    returned = {k: to_chip(sums[k], k) for k in EVERYWHERE}
+        (meta, masks, *arrived),
+    )
+    returned = {k: to_chip(sums[k], k) for k in LAST_ORDER}
     near = jnp.concatenate([returned[k] for k in range(4)], axis=0)
     far = jnp.concatenate([returned[4 + k] for k in range(4)], axis=0)
     own = (near.astype(F32) + far.astype(F32)).astype(BF16)

time: 88.7 us -> 87.6 us (0.988)
  waiting for transfers between devices: 34.2 us -> 30 us
  local copies, waits for them, and re-layouts: 2.97 us -> 6.51 us
    ppermute x20, waiting for transfers between devices: 32.8 us -> 27.5 us  [to_chip(): return lax.ppermute(value, CHIPS, pairs)]
    unnamed x19 -> x25, local copies, waits for them, and re-layouts: 1.06 us -> 4.9 us
    ppermute x3, waiting for transfers between devices: 1.41 us -> 2.45 us  [swap_cores(): return lax.ppermute(value, 'pair', [(0, 1), (1, 0)])]
  transfers between devices with their start and end apart: 23 -> 23, of which waited for: 11 -> 11; matrix products, arithmetic and copies ran while one was open for 3% -> 2% of each run, Pallas kernels for 2% -> 2%
where the time goes in v4:
time: 87.6 us; the launch traced here: 86.2 us
  starting transfers between devices  35.5 us (41%)
  waiting for transfers between devices  30 us (34%)
  Pallas kernels  13.9 us (16%)
  local copies, waits for them, and re-layouts  6.51 us (7%)
    ppermute x20, starting transfers between devices, to_chip(): return lax.ppermute(value, CHIPS, pairs)  34.9 us
    ppermute x20, waiting for transfers between devices, to_chip(): return lax.ppermute(value, CHIPS, pairs)  27.5 us
    pallas_call x7, Pallas kernels, call(): pl.pallas_call(kernel, out_shape=outs, in_specs=in_specs, out_specs=[pl.B...  13.9 us
    unnamed x25, local copies, waits for them, and re-layouts  4.9 us
    ppermute x3, waiting for transfers between devices, swap_cores(): return lax.ppermute(value, 'pair', [(0, 1), (1, 0)])  2.45 us
  transfers between devices with their start and end apart: 23, of which 11 were waited for; matrix products, arithmetic and copies ran while one was open for 2% of the time, Pallas kernels for 2%

profile of v4, /device:TPU:0, one launch (start us, length us, event | category | flops | bytes accessed | tf_op | source)
XLA Modules:
  0.0 86.2 jit_solution(15549788428624647419)
XLA Ops:
  0.0 0.5 collective-permute-start
  0.5 0.7 slice.6.gain
  1.1 0.1 pad_add_fusion.meta
  1.2 0.9 %slice_bitcast_fusion.weight = bf16[128,512]{1,0:T(8,128)(2,1)S(1)} fusion(bf16[2,128,640]{2,1,0:T(8,128)(2,1)} %weight.3), kind=kLoop, calls=%fused_computation.1 | loop fusion | bytes 262144 | tf_op jit(solution)/shard_map/squeeze | solution.py:532
  2.1 1.0 %copy-done.2 = bf16[40,40,128]{2,1,0:T(8,128)(2,1)S(1)} copy-done((bf16[40,40,128]{2,1,0:T(8,128)(2,1)S(1)}, bf16[40,40,128]{2,1,0:T(8,128)(2,1)}, u32[]{:S(2)}) %copy-start.2) | copy-done | bytes 409624
  3.1 1.7 %shard_map.91 = (f32[128,3200]{1,0:T(8,128)S(1)}, bf16[128,3200]{1,0:T(8,128)(2,1)S(1)}, bf16[32,3200]{1,0:T(8,128)(2,1)S(1)}, bf16[32,3200]{1,0:T(8,128)(2,1)S(...) custom-call(s32[2]{0:T(128)S(1)} %pad_add_fusion.meta, ...), custom_call_target="tpu_custom_call" | custom-call | bytes 4637192 | tf_op jit(solution)/shard_map/pallas_call | solution.py:479
  4.9 3.9 %collective-permute-start.1 = (bf16[16,3200]{1,0:T(8,128)(2,1)S(1)}, bf16[16,3200]{1,0:T(8,128)(2,1)S(1)}, u32[]{:S(2)}, u32[]{:S(2)}) collective-permute-start(bf16[16,3200]{1,0:T(8,128)(2,1)S(1)} %get-tuple-element.44), channel_id=1, source_target_pairs={{0,8},{1,9},{2,10},{3,11},{4,12},{5,13},{6,14},{7,15},{8,0},{9,1},... | collective-permute-start | bytes 307208 | tf_op jit(solution)/shard_map/ppermute | solution.py:494
  8.8 1.3 %collective-permute-start.2 = (bf16[16,3200]{1,0:T(8,128)(2,1)S(1)}, bf16[16,3200]{1,0:T(8,128)(2,1)S(1)}, u32[]{:S(2)}, u32[]{:S(2)}) collective-permute-start(bf16[16,3200]{1,0:T(8,128)(2,1)S(1)} %get-tuple-element.45), channel_id=1, source_target_pairs={{0,10},{1,11},{2,8},{3,9},{4,14},{5,15},{6,12},{7,13},{8,2},{9,3},... | collective-permute-start | bytes 307208 | tf_op jit(solution)/shard_map/ppermute | solution.py:494
  10.1 1.6 %collective-permute-start.3 = (bf16[32,3200]{1,0:T(8,128)(2,1)S(1)}, bf16[32,3200]{1,0:T(8,128)(2,1)S(1)}, u32[]{:S(2)}, u32[]{:S(2)}) collective-permute-start(bf16[32,3200]{1,0:T(8,128)(2,1)S(1)} %get-tuple-element.46), channel_id=1, source_target_pairs={{0,4},{1,5},{2,6},{3,7},{4,0},{5,1},{6,2},{7,3},{8,12},{9,13},{10,... | collective-permute-start | bytes 614408 | tf_op jit(solution)/shard_map/ppermute | solution.py:494
  11.6 0.2 collective-permute-start.5
  11.8 1.7 %collective-permute-start.7 = (bf16[32,3200]{1,0:T(8,128)(2,1)S(1)}, bf16[32,3200]{1,0:T(8,128)(2,1)S(1)}, u32[]{:S(2)}, u32[]{:S(2)}) collective-permute-start(bf16[32,3200]{1,0:T(8,128)(2,1)S(1)} %get-tuple-element.50), channel_id=1, source_target_pairs={{0,2},{1,3},{2,0},{3,1},{4,6},{5,7},{6,4},{7,5},{8,10},{9,11},{10,... | collective-permute-start | bytes 614408 | tf_op jit(solution)/shard_map/ppermute | solution.py:494
  13.5 2.7 %collective-permute-done.1.refs_0_ = bf16[16,3200]{1,0:T(8,128)(2,1)S(1)} collective-permute-done((bf16[16,3200]{1,0:T(8,128)(2,1)S(1)}, bf16[16,3200]{1,0:T(8,128)(2,1)S(1)}, u32[]{:S(2)}, u32[]{:S(2)}) %collective-permute-start.1) | collective-permute-done | bytes 102432 | tf_op jit(solution)/shard_map/ppermute | solution.py:494
  16.3 3.9 %collective-permute-start.4 = (bf16[16,3200]{1,0:T(8,128)(2,1)S(1)}, bf16[16,3200]{1,0:T(8,128)(2,1)S(1)}, u32[]{:S(2)}, u32[]{:S(2)}) collective-permute-start(bf16[16,3200]{1,0:T(8,128)(2,1)S(1)} %get-tuple-element.47), channel_id=1, source_target_pairs={{0,12},{1,13},{2,14},{3,15},{4,8},{5,9},{6,10},{7,11},{8,4},{9,5},... | collective-permute-start | bytes 307208 | tf_op jit(solution)/shard_map/ppermute | solution.py:494
  20.2 3.1 %collective-permute-start.6 = (bf16[16,3200]{1,0:T(8,128)(2,1)S(1)}, bf16[16,3200]{1,0:T(8,128)(2,1)S(1)}, u32[]{:S(2)}, u32[]{:S(2)}) collective-permute-start(bf16[16,3200]{1,0:T(8,128)(2,1)S(1)} %get-tuple-element.49), channel_id=1, source_target_pairs={{0,14},{1,15},{2,12},{3,13},{4,10},{5,11},{6,8},{7,9},{8,6},{9,7},... | collective-permute-start | bytes 307208 | tf_op jit(solution)/shard_map/ppermute | solution.py:494
  23.3 1.0 %copy-done = bf16[2,128,640]{2,1,0:T(8,128)(2,1)S(1)} copy-done((bf16[2,128,640]{2,1,0:T(8,128)(2,1)S(1)}, bf16[2,128,640]{2,1,0:T(8,128)(2,1)}, u32[]{:S(2)}) %copy-start) | copy-done | bytes 327704
  24.3 0.8 copy-done.3
  25.1 0.7 copy-done.7
  25.8 0.7 copy-done.8
  26.5 0.7 copy-done.9
  27.2 1.0 %shard_map.92 = (f32[128,3200]{1,0:T(8,128)S(1)}, bf16[128,128]{1,0:T(8,128)(2,1)S(1)}, f32[128,128]{1,0:T(8,128)S(1)}, f32[128,128]{1,0:T(8,128)S(1)}, bf16[256...) custom-call(s32[2]{0:T(128)S(1)} %pad_add_fusion.meta, bf16[128,3200]{1,0:T(8,128)(2,1)S(1)} %get-tuple-element.42.normed, ...), custom_call_target="tpu_custom_call" | custom-call | bytes 3246728 | tf_op jit(solution)/shard_map/pallas_call | solution.py:479
  28.2 0.4 collective-permute-done.4.refs_3_
  28.6 0.9 %collective-permute-done.6.refs_5_ = bf16[16,3200]{1,0:T(8,128)(2,1)S(1)} collective-permute-done((bf16[16,3200]{1,0:T(8,128)(2,1)S(1)}, bf16[16,3200]{1,0:T(8,128)(2,1)S(1)}, u32[]{:S(2)}, u32[]{:S(2)}) %collective-permute-start.6) | collective-permute-done | bytes 102432 | tf_op jit(solution)/shard_map/ppermute | solution.py:494
  29.6 2.0 %shard_map.93 = (bf16[16,3200]{1,0:T(8,128)(2,1)S(1)}, bf16[16,3200]{1,0:T(8,128)(2,1)S(1)}, bf16[16,3200]{1,0:T(8,128)(2,1)S(1)}, bf16[16,3200]{1,0:T(8,128)(2,1)S(1)}) custom-call(s32[2]{0:T(128)S(1)} %pad_add_fusion.meta, f32[8,40,128]{2,1,0:T(8,128)S(1)} %get-tuple-element.43.masks, bf16[16,3200]{1,0:T(8,128)(2,1)S(1)} %collective-permute-done.1.refs_0_, ...), custom_call_target="tpu_custom_call" | custom-call | bytes 1802248 | tf_op jit(solution)/shard_map/pallas_call | solution.py:479
  31.6 1.8 %collective-permute-start.8 = (bf16[16,3200]{1,0:T(8,128)(2,1)S(1)}, bf16[16,3200]{1,0:T(8,128)(2,1)S(1)}, u32[]{:S(2)}, u32[]{:S(2)}) collective-permute-start(bf16[16,3200]{1,0:T(8,128)(2,1)S(1)} %get-tuple-element.53), channel_id=1, source_target_pairs={{0,2},{1,3},{2,0},{3,1},{4,6},{5,7},{6,4},{7,5},{8,10},{9,11},{10,... | collective-permute-start | bytes 307208 | tf_op jit(solution)/shard_map/ppermute | solution.py:494
  33.4 1.8 %collective-permute-start.10 = (bf16[16,3200]{1,0:T(8,128)(2,1)S(1)}, bf16[16,3200]{1,0:T(8,128)(2,1)S(1)}, u32[]{:S(2)}, u32[]{:S(2)}) collective-permute-start(bf16[16,3200]{1,0:T(8,128)(2,1)S(1)} %get-tuple-element.55), channel_id=1, source_target_pairs={{0,6},{1,7},{2,4},{3,5},{4,2},{5,3},{6,0},{7,1},{8,14},{9,15},{10,... | collective-permute-start | bytes 307208 | tf_op jit(solution)/shard_map/ppermute | solution.py:494
  35.2 2.3 %collective-permute-done.8 = bf16[16,3200]{1,0:T(8,128)(2,1)S(1)} collective-permute-done((bf16[16,3200]{1,0:T(8,128)(2,1)S(1)}, bf16[16,3200]{1,0:T(8,128)(2,1)S(1)}, u32[]{:S(2)}, u32[]{:S(2)}) %collective-permute-start.8) | collective-permute-done | bytes 102432 | tf_op jit(solution)/shard_map/ppermute | solution.py:494
  37.5 0.7 collective-permute-done.9
  38.2 0.9 %collective-permute-done.10 = bf16[16,3200]{1,0:T(8,128)(2,1)S(1)} collective-permute-done((bf16[16,3200]{1,0:T(8,128)(2,1)S(1)}, bf16[16,3200]{1,0:T(8,128)(2,1)S(1)}, u32[]{:S(2)}, u32[]{:S(2)}) %collective-permute-start.10) | collective-permute-done | bytes 102432 | tf_op jit(solution)/shard_map/ppermute | solution.py:494
  39.1 1.7 %collective-permute-done.11.other = bf16[64,3200]{1,0:T(8,128)(2,1)S(1)} collective-permute-done((bf16[64,3200]{1,0:T(8,128)(2,1)S(1)}, bf16[64,3200]{1,0:T(8,128)(2,1)S(1)}, u32[]{:S(2)}, u32[]{:S(2)}) %collective-permute-start.11) | collective-permute-done | bytes 409632 | tf_op jit(solution)/shard_map/ppermute | solution.py:498
  40.9 2.2 %shard_map.94 = (f32[128,3200]{1,0:T(8,128)S(1)}, bf16[128,3200]{1,0:T(8,128)(2,1)S(1)}, bf16[32,3200]{1,0:T(8,128)(2,1)S(1)}, bf16[32,3200]{1,0:T(8,128)(2,1)S(...) custom-call(bf16[64,3200]{1,0:T(8,128)(2,1)S(1)} %constant_dynamic-update-slice_fusion.own, ...), custom_call_target="tpu_custom_call" | custom-call | bytes 7602176 | tf_op jit(solution)/shard_map/pallas_call | solution.py:479
  43.1 1.7 %collective-permute-start.12 = (bf16[32,3200]{1,0:T(8,128)(2,1)S(1)}, bf16[32,3200]{1,0:T(8,128)(2,1)S(1)}, u32[]{:S(2)}, u32[]{:S(2)}) collective-permute-start(bf16[32,3200]{1,0:T(8,128)(2,1)S(1)} %get-tuple-element.62), channel_id=1, source_target_pairs={{0,6},{1,7},{2,4},{3,5},{4,2},{5,3},{6,0},{7,1},{8,14},{9,15},{10,... | collective-permute-start | bytes 614408 | tf_op jit(solution)/shard_map/ppermute | solution.py:494
  44.8 1.4 %collective-permute-start.13 = (bf16[32,3200]{1,0:T(8,128)(2,1)S(1)}, bf16[32,3200]{1,0:T(8,128)(2,1)S(1)}, u32[]{:S(2)}, u32[]{:S(2)}) collective-permute-start(bf16[32,3200]{1,0:T(8,128)(2,1)S(1)} %get-tuple-element.63), channel_id=1, source_target_pairs={{0,4},{1,5},{2,6},{3,7},{4,0},{5,1},{6,2},{7,3},{8,12},{9,13},{10,... | collective-permute-start | bytes 614408 | tf_op jit(solution)/shard_map/ppermute | solution.py:494
  46.3 0.4 collective-permute-start.14
  46.6 5.4 %collective-permute-done.12.refs_0_ = bf16[32,3200]{1,0:T(8,128)(2,1)S(1)} collective-permute-done((bf16[32,3200]{1,0:T(8,128)(2,1)S(1)}, bf16[32,3200]{1,0:T(8,128)(2,1)S(1)}, u32[]{:S(2)}, u32[]{:S(2)}) %collective-permute-start.12) | collective-permute-done | bytes 204832 | tf_op jit(solution)/shard_map/ppermute | solution.py:494
  52.0 3.8 %collective-permute-done.13.refs_1_ = bf16[32,3200]{1,0:T(8,128)(2,1)S(1)} collective-permute-done((bf16[32,3200]{1,0:T(8,128)(2,1)S(1)}, bf16[32,3200]{1,0:T(8,128)(2,1)S(1)}, u32[]{:S(2)}, u32[]{:S(2)}) %collective-permute-start.13) | collective-permute-done | bytes 204832 | tf_op jit(solution)/shard_map/ppermute | solution.py:494
  55.8 2.0 %shard_map.95 = (bf16[16,3200]{1,0:T(8,128)(2,1)S(1)}, bf16[16,3200]{1,0:T(8,128)(2,1)S(1)}, bf16[16,3200]{1,0:T(8,128)(2,1)S(1)}, bf16[16,3200]{1,0:T(8,128)(2,...) custom-call(s32[2]{0:T(128)S(1)} %pad_add_fusion.meta, ...), custom_call_target="tpu_custom_call" | custom-call | bytes 1802248 | tf_op jit(solution)/shard_map/pallas_call | solution.py:479
  57.9 1.5 %collective-permute-start.15 = (bf16[16,3200]{1,0:T(8,128)(2,1)S(1)}, bf16[16,3200]{1,0:T(8,128)(2,1)S(1)}, u32[]{:S(2)}, u32[]{:S(2)}) collective-permute-start(bf16[16,3200]{1,0:T(8,128)(2,1)S(1)} %get-tuple-element.67), channel_id=1, source_target_pairs={{0,2},{1,3},{2,0},{3,1},{4,6},{5,7},{6,4},{7,5},{8,10},{9,11},{10,... | collective-permute-start | bytes 307208 | tf_op jit(solution)/shard_map/ppermute | solution.py:494
  59.3 0.9 %collective-permute-start.16 = (bf16[16,3200]{1,0:T(8,128)(2,1)S(1)}, bf16[16,3200]{1,0:T(8,128)(2,1)S(1)}, u32[]{:S(2)}, u32[]{:S(2)}) collective-permute-start(bf16[16,3200]{1,0:T(8,128)(2,1)S(1)} %get-tuple-element.68), channel_id=1, source_target_pairs={{0,4},{1,5},{2,6},{3,7},{4,0},{5,1},{6,2},{7,3},{8,12},{9,13},{10,... | collective-permute-start | bytes 307208 | tf_op jit(solution)/shard_map/ppermute | solution.py:494
  60.2 1.2 %collective-permute-start.17 = (bf16[16,3200]{1,0:T(8,128)(2,1)S(1)}, bf16[16,3200]{1,0:T(8,128)(2,1)S(1)}, u32[]{:S(2)}, u32[]{:S(2)}) collective-permute-start(bf16[16,3200]{1,0:T(8,128)(2,1)S(1)} %get-tuple-element.69), channel_id=1, source_target_pairs={{0,6},{1,7},{2,4},{3,5},{4,2},{5,3},{6,0},{7,1},{8,14},{9,15},{10,... | collective-permute-start | bytes 307208 | tf_op jit(solution)/shard_map/ppermute | solution.py:494
  61.4 3.8 %collective-permute-start.18 = (bf16[16,3200]{1,0:T(8,128)(2,1)S(1)}, bf16[16,3200]{1,0:T(8,128)(2,1)S(1)}, u32[]{:S(2)}, u32[]{:S(2)}) collective-permute-start(bf16[16,3200]{1,0:T(8,128)(2,1)S(1)} %get-tuple-element.70), channel_id=1, source_target_pairs={{0,8},{1,9},{2,10},{3,11},{4,12},{5,13},{6,14},{7,15},{8,0},{9,1},... | collective-permute-start | bytes 307208 | tf_op jit(solution)/shard_map/ppermute | solution.py:494
  65.2 3.4 %collective-permute-start.20 = (bf16[16,3200]{1,0:T(8,128)(2,1)S(1)}, bf16[16,3200]{1,0:T(8,128)(2,1)S(1)}, u32[]{:S(2)}, u32[]{:S(2)}) collective-permute-start(bf16[16,3200]{1,0:T(8,128)(2,1)S(1)} %get-tuple-element.72), channel_id=1, source_target_pairs={{0,12},{1,13},{2,14},{3,15},{4,8},{5,9},{6,10},{7,11},{8,4},{9,5},... | collective-permute-start | bytes 307208 | tf_op jit(solution)/shard_map/ppermute | solution.py:494
  68.7 1.3 %collective-permute-start.21 = (bf16[16,3200]{1,0:T(8,128)(2,1)S(1)}, bf16[16,3200]{1,0:T(8,128)(2,1)S(1)}, u32[]{:S(2)}, u32[]{:S(2)}) collective-permute-start(bf16[16,3200]{1,0:T(8,128)(2,1)S(1)} %get-tuple-element.73), channel_id=1, source_target_pairs={{0,14},{1,15},{2,12},{3,13},{4,10},{5,11},{6,8},{7,9},{8,6},{9,7},... | collective-permute-start | bytes 307208 | tf_op jit(solution)/shard_map/ppermute | solution.py:494
  69.9 10.4 %collective-permute-done.19 = bf16[16,3200]{1,0:T(8,128)(2,1)S(1)} collective-permute-done((bf16[16,3200]{1,0:T(8,128)(2,1)S(1)}, bf16[16,3200]{1,0:T(8,128)(2,1)S(1)}, u32[]{:S(2)}, u32[]{:S(2)}) %collective-permute-start.19) | collective-permute-done | bytes 102432 | tf_op jit(solution)/shard_map/ppermute | solution.py:494
  80.3 0.1 add_convert_fusion.own
  80.4 0.1 collective-permute-start.22
  80.5 1.0 %shard_map.96 = (f32[128,3200]{1,0:T(8,128)S(1)}, bf16[128,128]{1,0:T(8,128)(2,1)S(1)}, f32[128,128]{1,0:T(8,128)S(1)}) custom-call(s32[2]{0:T(128)S(1)} %pad_add_fusion.meta, bf16[128,3200]{1,0:T(8,128)(2,1)S(1)} %get-tuple-element.75.normed, bf16[2,128,640]{2,1,0:T(8,128)(2,1)S(1)} %copy-done.1, f32[2,128]{1,0:T(2,128)S(1)} %copy-done.7, ...), custom_call_target="tpu_custom_call" | custom-call | bytes 2950152 | tf_op jit(solution)/shard_map/pallas_call | solution.py:479
  81.5 0.7 collective-permute-done.22.other
  82.3 3.9 %shard_map.97 = bf16[40,40,128]{2,1,0:T(8,128)(2,1)} custom-call(s32[2]{0:T(128)S(1)} %pad_add_fusion.meta, bf16[64,3200]{1,0:T(8,128)(2,1)S(1)} %add_convert_fusion.own, bf16[64,3200]{1,0:T(8,128)(2,1)S(1)} %collective-permute-done.22.other, f32[128,3200]{1,0:T(8,128)S(1)} %get-tuple-element.74.stream, f32[128,3200]{1,0:T(8,128)S(1)} %get-tuple-element.76.gate, ...), custom_call_target="tpu_custom_call" | custom-call | bytes 4866568 | tf_op jit(solution)/shard_map/pallas_call | solution.py:479
  (35 shorter events, 0.2 us)
Async XLA Ops:
  0.0 2.1 %collective-permute-start = (bf16[40,40,128]{2,1,0:T(8,128)(2,1)}, bf16[40,40,128]{2,1,0:T(8,128)(2,1)S(1)}, u32[]{:S(2)}, u32[]{:S(2)}) collective-permute-start(bf16[40,40,128]{2,1,0:T(8,128)(2,1)} %own.1), channel_id=1, source_target_pairs={{0,1},{1,0},{2,3},{3,2},{4,5},{5,4},{6,7},{7,6},{8,9},{9,8},{10,11... | collective-permute-start | bytes 1228808 | tf_op jit(solution)/shard_map/ppermute | solution.py:498
  2.1 1.0 %copy-start.2 = (bf16[40,40,128]{2,1,0:T(8,128)(2,1)S(1)}, bf16[40,40,128]{2,1,0:T(8,128)(2,1)}, u32[]{:S(2)}) copy-start(bf16[40,40,128]{2,1,0:T(8,128)(2,1)} %own.1) | copy-start | bytes 1228804
  4.9 11.4 %collective-permute-start.1 = (bf16[16,3200]{1,0:T(8,128)(2,1)S(1)}, bf16[16,3200]{1,0:T(8,128)(2,1)S(1)}, u32[]{:S(2)}, u32[]{:S(2)}) collective-permute-start(bf16[16,3200]{1,0:T(8,128)(2,1)S(1)} %get-tuple-element.44), channel_id=1, source_target_pairs={{0,8},{1,9},{2,10},{3,11},{4,12},{5,13},{6,14},{7,15},{8,0},{9,1},... | collective-permute-start | bytes 307208 | tf_op jit(solution)/shard_map/ppermute | solution.py:494
  8.8 11.4 %collective-permute-start.2 = (bf16[16,3200]{1,0:T(8,128)(2,1)S(1)}, bf16[16,3200]{1,0:T(8,128)(2,1)S(1)}, u32[]{:S(2)}, u32[]{:S(2)}) collective-permute-start(bf16[16,3200]{1,0:T(8,128)(2,1)S(1)} %get-tuple-element.45), channel_id=1, source_target_pairs={{0,10},{1,11},{2,8},{3,9},{4,14},{5,15},{6,12},{7,13},{8,2},{9,3},... | collective-permute-start | bytes 307208 | tf_op jit(solution)/shard_map/ppermute | solution.py:494
  10.1 19.5 %collective-permute-start.3 = (bf16[32,3200]{1,0:T(8,128)(2,1)S(1)}, bf16[32,3200]{1,0:T(8,128)(2,1)S(1)}, u32[]{:S(2)}, u32[]{:S(2)}) collective-permute-start(bf16[32,3200]{1,0:T(8,128)(2,1)S(1)} %get-tuple-element.46), channel_id=1, source_target_pairs={{0,4},{1,5},{2,6},{3,7},{4,0},{5,1},{6,2},{7,3},{8,12},{9,13},{10,... | collective-permute-start | bytes 614408 | tf_op jit(solution)/shard_map/ppermute | solution.py:494
  11.6 17.9 %collective-permute-start.5 = (bf16[32,3200]{1,0:T(8,128)(2,1)S(1)}, bf16[32,3200]{1,0:T(8,128)(2,1)S(1)}, u32[]{:S(2)}, u32[]{:S(2)}) collective-permute-start(bf16[32,3200]{1,0:T(8,128)(2,1)S(1)} %get-tuple-element.48), channel_id=1, source_target_pairs={{0,6},{1,7},{2,4},{3,5},{4,2},{5,3},{6,0},{7,1},{8,14},{9,15},{10,... | collective-permute-start | bytes 614408 | tf_op jit(solution)/shard_map/ppermute | solution.py:494
  11.8 17.8 %collective-permute-start.7 = (bf16[32,3200]{1,0:T(8,128)(2,1)S(1)}, bf16[32,3200]{1,0:T(8,128)(2,1)S(1)}, u32[]{:S(2)}, u32[]{:S(2)}) collective-permute-start(bf16[32,3200]{1,0:T(8,128)(2,1)S(1)} %get-tuple-element.50), channel_id=1, source_target_pairs={{0,2},{1,3},{2,0},{3,1},{4,6},{5,7},{6,4},{7,5},{8,10},{9,11},{10,... | collective-permute-start | bytes 614408 | tf_op jit(solution)/shard_map/ppermute | solution.py:494
  16.3 12.4 %collective-permute-start.4 = (bf16[16,3200]{1,0:T(8,128)(2,1)S(1)}, bf16[16,3200]{1,0:T(8,128)(2,1)S(1)}, u32[]{:S(2)}, u32[]{:S(2)}) collective-permute-start(bf16[16,3200]{1,0:T(8,128)(2,1)S(1)} %get-tuple-element.47), channel_id=1, source_target_pairs={{0,12},{1,13},{2,14},{3,15},{4,8},{5,9},{6,10},{7,11},{8,4},{9,5},... | collective-permute-start | bytes 307208 | tf_op jit(solution)/shard_map/ppermute | solution.py:494
  20.2 9.4 %collective-permute-start.6 = (bf16[16,3200]{1,0:T(8,128)(2,1)S(1)}, bf16[16,3200]{1,0:T(8,128)(2,1)S(1)}, u32[]{:S(2)}, u32[]{:S(2)}) collective-permute-start(bf16[16,3200]{1,0:T(8,128)(2,1)S(1)} %get-tuple-element.49), channel_id=1, source_target_pairs={{0,14},{1,15},{2,12},{3,13},{4,10},{5,11},{6,8},{7,9},{8,6},{9,7},... | collective-permute-start | bytes 307208 | tf_op jit(solution)/shard_map/ppermute | solution.py:494
  23.3 1.0 %copy-start = (bf16[2,128,640]{2,1,0:T(8,128)(2,1)S(1)}, bf16[2,128,640]{2,1,0:T(8,128)(2,1)}, u32[]{:S(2)}) copy-start(bf16[2,128,640]{2,1,0:T(8,128)(2,1)} %weight.3) | copy-start | bytes 983044
  24.3 0.8 copy-start.3
  25.1 0.7 copy-start.7
  25.8 0.7 copy-start.8
  26.5 0.7 copy-start.9
  31.6 5.8 %collective-permute-start.8 = (bf16[16,3200]{1,0:T(8,128)(2,1)S(1)}, bf16[16,3200]{1,0:T(8,128)(2,1)S(1)}, u32[]{:S(2)}, u32[]{:S(2)}) collective-permute-start(bf16[16,3200]{1,0:T(8,128)(2,1)S(1)} %get-tuple-element.53), channel_id=1, source_target_pairs={{0,2},{1,3},{2,0},{3,1},{4,6},{5,7},{6,4},{7,5},{8,10},{9,11},{10,... | collective-permute-start | bytes 307208 | tf_op jit(solution)/shard_map/ppermute | solution.py:494
  33.4 4.8 %collective-permute-start.9 = (bf16[16,3200]{1,0:T(8,128)(2,1)S(1)}, bf16[16,3200]{1,0:T(8,128)(2,1)S(1)}, u32[]{:S(2)}, u32[]{:S(2)}) collective-permute-start(bf16[16,3200]{1,0:T(8,128)(2,1)S(1)} %get-tuple-element.54), channel_id=1, source_target_pairs={{0,4},{1,5},{2,6},{3,7},{4,0},{5,1},{6,2},{7,3},{8,12},{9,13},{10,... | collective-permute-start | bytes 307208 | tf_op jit(solution)/shard_map/ppermute | solution.py:494
  33.4 5.7 %collective-permute-start.10 = (bf16[16,3200]{1,0:T(8,128)(2,1)S(1)}, bf16[16,3200]{1,0:T(8,128)(2,1)S(1)}, u32[]{:S(2)}, u32[]{:S(2)}) collective-permute-start(bf16[16,3200]{1,0:T(8,128)(2,1)S(1)} %get-tuple-element.55), channel_id=1, source_target_pairs={{0,6},{1,7},{2,4},{3,5},{4,2},{5,3},{6,0},{7,1},{8,14},{9,15},{10,... | collective-permute-start | bytes 307208 | tf_op jit(solution)/shard_map/ppermute | solution.py:494
  39.1 1.8 %collective-permute-start.11 = (bf16[64,3200]{1,0:T(8,128)(2,1)S(1)}, bf16[64,3200]{1,0:T(8,128)(2,1)S(1)}, u32[]{:S(2)}, u32[]{:S(2)}) collective-permute-start(bf16[64,3200]{1,0:T(8,128)(2,1)S(1)} %constant_dynamic-update-slice_fusion.own), channel_id=1, source_target_pairs={{0,1},{1,0},{2,3},{3,2},{4,5},{5,4},{6,7},{7,6},{8,9},{9,8},{10,11... | collective-permute-start | bytes 1228808 | tf_op jit(solution)/shard_map/ppermute | solution.py:498
  43.1 37.5 %copy-start.1 = (bf16[2,128,640]{2,1,0:T(8,128)(2,1)S(1)}, bf16[2,128,640]{2,1,0:T(8,128)(2,1)}, u32[]{:S(2)}) copy-start(bf16[2,128,640]{2,1,0:T(8,128)(2,1)} %weight.3) | copy-start | bytes 983044
  43.1 37.5 %copy-start.4 = (bf16[2,128,128]{2,1,0:T(8,128)(2,1)S(1)}, bf16[2,128,128]{2,1,0:T(8,128)(2,1)}, u32[]{:S(2)}) copy-start(bf16[2,128,128]{2,1,0:T(8,128)(2,1)} %out_weight.3) | copy-start | bytes 196612
  43.1 8.9 %collective-permute-start.12 = (bf16[32,3200]{1,0:T(8,128)(2,1)S(1)}, bf16[32,3200]{1,0:T(8,128)(2,1)S(1)}, u32[]{:S(2)}, u32[]{:S(2)}) collective-permute-start(bf16[32,3200]{1,0:T(8,128)(2,1)S(1)} %get-tuple-element.62), channel_id=1, source_target_pairs={{0,6},{1,7},{2,4},{3,5},{4,2},{5,3},{6,0},{7,1},{8,14},{9,15},{10,... | collective-permute-start | bytes 614408 | tf_op jit(solution)/shard_map/ppermute | solution.py:494
  44.8 11.0 %collective-permute-start.13 = (bf16[32,3200]{1,0:T(8,128)(2,1)S(1)}, bf16[32,3200]{1,0:T(8,128)(2,1)S(1)}, u32[]{:S(2)}, u32[]{:S(2)}) collective-permute-start(bf16[32,3200]{1,0:T(8,128)(2,1)S(1)} %get-tuple-element.63), channel_id=1, source_target_pairs={{0,4},{1,5},{2,6},{3,7},{4,0},{5,1},{6,2},{7,3},{8,12},{9,13},{10,... | collective-permute-start | bytes 614408 | tf_op jit(solution)/shard_map/ppermute | solution.py:494
  46.3 9.5 %collective-permute-start.14 = (bf16[32,3200]{1,0:T(8,128)(2,1)S(1)}, bf16[32,3200]{1,0:T(8,128)(2,1)S(1)}, u32[]{:S(2)}, u32[]{:S(2)}) collective-permute-start(bf16[32,3200]{1,0:T(8,128)(2,1)S(1)} %get-tuple-element.64), channel_id=1, source_target_pairs={{0,2},{1,3},{2,0},{3,1},{4,6},{5,7},{6,4},{7,5},{8,10},{9,11},{10,... | collective-permute-start | bytes 614408 | tf_op jit(solution)/shard_map/ppermute | solution.py:494
  55.8 26.4 %copy-start.5 = (bf16[128,512]{1,0:T(8,128)(2,1)S(1)}, bf16[128,512]{1,0:T(8,128)(2,1)}, u32[]{:S(2)}) copy-start(bf16[128,512]{1,0:T(8,128)(2,1)} %expand.1) | copy-start | bytes 393220
  55.8 26.4 %copy-start.6 = (bf16[512,128]{1,0:T(8,128)(2,1)S(1)}, bf16[512,128]{1,0:T(8,128)(2,1)}, u32[]{:S(2)}) copy-start(bf16[512,128]{1,0:T(8,128)(2,1)} %shrink.1) | copy-start | bytes 393220
  55.8 26.4 %copy-start.10 = (f32[128]{0:T(128)S(1)}, f32[128]{0:T(128)}, u32[]{:S(2)}) copy-start(f32[128]{0:T(128)} %param.15) | copy-start | bytes 1540
  57.9 7.4 %collective-permute-start.15 = (bf16[16,3200]{1,0:T(8,128)(2,1)S(1)}, bf16[16,3200]{1,0:T(8,128)(2,1)S(1)}, u32[]{:S(2)}, u32[]{:S(2)}) collective-permute-start(bf16[16,3200]{1,0:T(8,128)(2,1)S(1)} %get-tuple-element.67), channel_id=1, source_target_pairs={{0,2},{1,3},{2,0},{3,1},{4,6},{5,7},{6,4},{7,5},{8,10},{9,11},{10,... | collective-permute-start | bytes 307208 | tf_op jit(solution)/shard_map/ppermute | solution.py:494
  59.3 9.3 %collective-permute-start.16 = (bf16[16,3200]{1,0:T(8,128)(2,1)S(1)}, bf16[16,3200]{1,0:T(8,128)(2,1)S(1)}, u32[]{:S(2)}, u32[]{:S(2)}) collective-permute-start(bf16[16,3200]{1,0:T(8,128)(2,1)S(1)} %get-tuple-element.68), channel_id=1, source_target_pairs={{0,4},{1,5},{2,6},{3,7},{4,0},{5,1},{6,2},{7,3},{8,12},{9,13},{10,... | collective-permute-start | bytes 307208 | tf_op jit(solution)/shard_map/ppermute | solution.py:494
  60.2 9.7 %collective-permute-start.17 = (bf16[16,3200]{1,0:T(8,128)(2,1)S(1)}, bf16[16,3200]{1,0:T(8,128)(2,1)S(1)}, u32[]{:S(2)}, u32[]{:S(2)}) collective-permute-start(bf16[16,3200]{1,0:T(8,128)(2,1)S(1)} %get-tuple-element.69), channel_id=1, source_target_pairs={{0,6},{1,7},{2,4},{3,5},{4,2},{5,3},{6,0},{7,1},{8,14},{9,15},{10,... | collective-permute-start | bytes 307208 | tf_op jit(solution)/shard_map/ppermute | solution.py:494
  61.4 8.5 %collective-permute-start.18 = (bf16[16,3200]{1,0:T(8,128)(2,1)S(1)}, bf16[16,3200]{1,0:T(8,128)(2,1)S(1)}, u32[]{:S(2)}, u32[]{:S(2)}) collective-permute-start(bf16[16,3200]{1,0:T(8,128)(2,1)S(1)} %get-tuple-element.70), channel_id=1, source_target_pairs={{0,8},{1,9},{2,10},{3,11},{4,12},{5,13},{6,14},{7,15},{8,0},{9,1},... | collective-permute-start | bytes 307208 | tf_op jit(solution)/shard_map/ppermute | solution.py:494
  65.2 15.2 %collective-permute-start.19 = (bf16[16,3200]{1,0:T(8,128)(2,1)S(1)}, bf16[16,3200]{1,0:T(8,128)(2,1)S(1)}, u32[]{:S(2)}, u32[]{:S(2)}) collective-permute-start(bf16[16,3200]{1,0:T(8,128)(2,1)S(1)} %get-tuple-element.71), channel_id=1, source_target_pairs={{0,10},{1,11},{2,8},{3,9},{4,14},{5,15},{6,12},{7,13},{8,2},{9,3},... | collective-permute-start | bytes 307208 | tf_op jit(solution)/shard_map/ppermute | solution.py:494
  65.2 15.1 %collective-permute-start.20 = (bf16[16,3200]{1,0:T(8,128)(2,1)S(1)}, bf16[16,3200]{1,0:T(8,128)(2,1)S(1)}, u32[]{:S(2)}, u32[]{:S(2)}) collective-permute-start(bf16[16,3200]{1,0:T(8,128)(2,1)S(1)} %get-tuple-element.72), channel_id=1, source_target_pairs={{0,12},{1,13},{2,14},{3,15},{4,8},{5,9},{6,10},{7,11},{8,4},{9,5},... | collective-permute-start | bytes 307208 | tf_op jit(solution)/shard_map/ppermute | solution.py:494
  68.7 11.7 %collective-permute-start.21 = (bf16[16,3200]{1,0:T(8,128)(2,1)S(1)}, bf16[16,3200]{1,0:T(8,128)(2,1)S(1)}, u32[]{:S(2)}, u32[]{:S(2)}) collective-permute-start(bf16[16,3200]{1,0:T(8,128)(2,1)S(1)} %get-tuple-element.73), channel_id=1, source_target_pairs={{0,14},{1,15},{2,12},{3,13},{4,10},{5,11},{6,8},{7,9},{8,6},{9,7},... | collective-permute-start | bytes 307208 | tf_op jit(solution)/shard_map/ppermute | solution.py:494
  80.4 1.8 %collective-permute-start.22 = (bf16[64,3200]{1,0:T(8,128)(2,1)S(1)}, bf16[64,3200]{1,0:T(8,128)(2,1)S(1)}, u32[]{:S(2)}, u32[]{:S(2)}) collective-permute-start(bf16[64,3200]{1,0:T(8,128)(2,1)S(1)} %add_convert_fusion.own), channel_id=1, source_target_pairs={{0,1},{1,0},{2,3},{3,2},{4,5},{5,4},{6,7},{7,6},{8,9},{9,8},{10,11... | collective-permute-start | bytes 1228808 | tf_op jit(solution)/shard_map/ppermute | solution.py:498

commit v5 on v4

--- a/solution.py
+++ b/solution.py
@@ -134,6 +134,7 @@
 FIRST_ORDER = (4, 5, 2, 6, 3, 7, 1, 0)
 LAST_ORDER = (4, 2, 5, 3, 6, 1, 7, 0)
 WITHIN_HALF = (3, 2, 1, 0)
+SIDES_WITHIN = (2, 3, 1, 0)
 
 
 def aligned(start, size):
@@ -156,8 +157,8 @@
     return run
 
 
-def sigmoid(values):
-    return 0.5 * jnp.tanh(0.5 * values) + 0.5
+def sigmoid_of_double(values):
+    return 0.5 * jnp.tanh(values) + 0.5
 
 
 def norm_rows(values, factor):
@@ -232,14 +233,14 @@
     for base in range(4):
         starts = [base * hidden + core * mine + size * ((chip & 3) ^ k) for k in range(4)]
         picked.append(pick_rows(table, starts, size))
-    return jnp.concatenate(picked, axis=0).astype(BF16)
+    return (0.5 * jnp.concatenate(picked, axis=0)).astype(BF16)
 
 
 def send_sides(normed, weights, messages, lanes):
     quarter = weights.shape[0] // 4
     projected = jnp.dot(weights, normed, preferred_element_type=F32)
-    left = sigmoid(projected[quarter : 2 * quarter]) * projected[:quarter]
-    right = sigmoid(projected[3 * quarter :]) * projected[2 * quarter : 3 * quarter]
+    left = (jnp.tanh(projected[quarter : 2 * quarter]) + 1.0) * projected[:quarter]
+    right = (jnp.tanh(projected[3 * quarter :]) + 1.0) * projected[2 * quarter : 3 * quarter]
     size = quarter // 4
     for k in range(4):
         rows = slice(k * size, (k + 1) * size)
@@ -281,8 +282,8 @@
 def gate_of(normed, weight, update):
     channels = normed.shape[0]
     hidden = (weight.shape[2] - channels) // 4
-    table = weight[update, :, 4 * hidden :].astype(F32).T.astype(BF16)
-    return sigmoid(jnp.dot(table, normed[...], preferred_element_type=F32))
+    table = (0.5 * weight[update, :, 4 * hidden :].astype(F32).T).astype(BF16)
+    return sigmoid_of_double(jnp.dot(table, normed[...], preferred_element_type=F32))
 
 
 def chip_masks(bits, column, meta, masks, width):
@@ -373,7 +374,7 @@
 
 
 def incoming_kernel(meta, masks, *refs, rows, width):
-    messages, outs = dict(zip(WITHIN_HALF, refs[:4])), refs[4:12]
+    messages, outs = dict(zip(SIDES_WITHIN, refs[:4])), refs[4:12]
     left, right, total = refs[12:]
     dap, sub = meta[1] >> 1, meta[1] & 1
     lane = lane_index()
@@ -434,9 +435,9 @@
     stream_out, normed_out, *messages = refs
     channels = stream.shape[0]
     middles = jnp.concatenate([middle[...]] * (width // channels), axis=1)
-    factors = jnp.concatenate([factor[...]] * (width // channels), axis=1)
-
-    @blocks(stream.shape[1])
+    factors = factor[...]
+
+    @blocks(stream.shape[1], width)
     def _(lanes):
         values = add_update(own, other, stream, gate, out_weights[...], middles, lanes)
         stream_out[:, lanes] = values
@@ -567,7 +568,7 @@
         (own, other, stream, gate, out_weights, middle, factor, weights),
         0,
     )
-    arrived = [to_chip(messages[k], k) for k in WITHIN_HALF]
+    arrived = [to_chip(messages[k], k) for k in SIDES_WITHIN]
     gate, out_weights, middle = call(
         second_gate_kernel,
         [flat32, square16, square32],

time: 87.6 us -> 86.8 us (level)
  starting transfers between devices: 35.5 us -> 34.6 us
  transfers between devices with their start and end apart: 23 -> 23, of which waited for: 11 -> 13; matrix products, arithmetic and copies ran while one was open for 2% -> 2% of each run, Pallas kernels for 2% -> 2%
where the time goes in v5:
time: 86.8 us; the launch traced here: 86 us
  starting transfers between devices  34.6 us (40%)
  waiting for transfers between devices  30.8 us (35%)
  Pallas kernels  13.7 us (16%)
  local copies, waits for them, and re-layouts  6.51 us (8%)
    ppermute x20, starting transfers between devices, to_chip(): return lax.ppermute(value, CHIPS, pairs)  34.1 us
    ppermute x20, waiting for transfers between devices, to_chip(): return lax.ppermute(value, CHIPS, pairs)  28.4 us
    pallas_call x7, Pallas kernels, call(): pl.pallas_call(kernel, out_shape=outs, in_specs=in_specs, out_specs=[pl.B...  13.7 us
    unnamed x25, local copies, waits for them, and re-layouts  4.9 us
    ppermute x3, waiting for transfers between devices, swap_cores(): return lax.ppermute(value, 'pair', [(0, 1), (1, 0)])  2.47 us
  transfers between devices with their start and end apart: 23, of which 13 were waited for; matrix products, arithmetic and copies ran while one was open for 2% of the time, Pallas kernels for 2%

profile of v5, /device:TPU:0, one launch (start us, length us, event | category | flops | bytes accessed | tf_op | source)
XLA Modules:
  0.0 86.0 jit_solution(14433901699759242540)
XLA Ops:
  0.0 0.5 collective-permute-start
  0.5 0.7 slice.6.gain
  1.2 0.9 %slice_bitcast_fusion.weight = bf16[128,512]{1,0:T(8,128)(2,1)S(1)} fusion(bf16[2,128,640]{2,1,0:T(8,128)(2,1)} %weight.3), kind=kLoop, calls=%fused_computation.1 | loop fusion | bytes 262144 | tf_op jit(solution)/shard_map/squeeze | solution.py:533
  2.1 1.0 %copy-done.2 = bf16[40,40,128]{2,1,0:T(8,128)(2,1)S(1)} copy-done((bf16[40,40,128]{2,1,0:T(8,128)(2,1)S(1)}, bf16[40,40,128]{2,1,0:T(8,128)(2,1)}, u32[]{:S(2)}) %copy-start.2) | copy-done | bytes 409624
  3.1 1.7 %shard_map.91 = (f32[128,3200]{1,0:T(8,128)S(1)}, bf16[128,3200]{1,0:T(8,128)(2,1)S(1)}, bf16[32,3200]{1,0:T(8,128)(2,1)S(1)}, bf16[32,3200]{1,0:T(8,128)(2,1)S(...) custom-call(s32[2]{0:T(128)S(1)} %pad_add_fusion.meta, ...), custom_call_target="tpu_custom_call" | custom-call | bytes 4637192 | tf_op jit(solution)/shard_map/pallas_call | solution.py:480
  4.8 3.9 %collective-permute-start.1 = (bf16[16,3200]{1,0:T(8,128)(2,1)S(1)}, bf16[16,3200]{1,0:T(8,128)(2,1)S(1)}, u32[]{:S(2)}, u32[]{:S(2)}) collective-permute-start(bf16[16,3200]{1,0:T(8,128)(2,1)S(1)} %get-tuple-element.44), channel_id=1, source_target_pairs={{0,8},{1,9},{2,10},{3,11},{4,12},{5,13},{6,14},{7,15},{8,0},{9,1},... | collective-permute-start | bytes 307208 | tf_op jit(solution)/shard_map/ppermute | solution.py:495
  8.7 1.3 %collective-permute-start.2 = (bf16[16,3200]{1,0:T(8,128)(2,1)S(1)}, bf16[16,3200]{1,0:T(8,128)(2,1)S(1)}, u32[]{:S(2)}, u32[]{:S(2)}) collective-permute-start(bf16[16,3200]{1,0:T(8,128)(2,1)S(1)} %get-tuple-element.45), channel_id=1, source_target_pairs={{0,10},{1,11},{2,8},{3,9},{4,14},{5,15},{6,12},{7,13},{8,2},{9,3},... | collective-permute-start | bytes 307208 | tf_op jit(solution)/shard_map/ppermute | solution.py:495
  10.0 1.6 %collective-permute-start.3 = (bf16[32,3200]{1,0:T(8,128)(2,1)S(1)}, bf16[32,3200]{1,0:T(8,128)(2,1)S(1)}, u32[]{:S(2)}, u32[]{:S(2)}) collective-permute-start(bf16[32,3200]{1,0:T(8,128)(2,1)S(1)} %get-tuple-element.46), channel_id=1, source_target_pairs={{0,4},{1,5},{2,6},{3,7},{4,0},{5,1},{6,2},{7,3},{8,12},{9,13},{10,... | collective-permute-start | bytes 614408 | tf_op jit(solution)/shard_map/ppermute | solution.py:495
  11.6 0.2 collective-permute-start.5
  11.7 1.7 %collective-permute-start.7 = (bf16[32,3200]{1,0:T(8,128)(2,1)S(1)}, bf16[32,3200]{1,0:T(8,128)(2,1)S(1)}, u32[]{:S(2)}, u32[]{:S(2)}) collective-permute-start(bf16[32,3200]{1,0:T(8,128)(2,1)S(1)} %get-tuple-element.50), channel_id=1, source_target_pairs={{0,2},{1,3},{2,0},{3,1},{4,6},{5,7},{6,4},{7,5},{8,10},{9,11},{10,... | collective-permute-start | bytes 614408 | tf_op jit(solution)/shard_map/ppermute | solution.py:495
  13.5 2.7 %collective-permute-done.1.refs_0_ = bf16[16,3200]{1,0:T(8,128)(2,1)S(1)} collective-permute-done((bf16[16,3200]{1,0:T(8,128)(2,1)S(1)}, bf16[16,3200]{1,0:T(8,128)(2,1)S(1)}, u32[]{:S(2)}, u32[]{:S(2)}) %collective-permute-start.1) | collective-permute-done | bytes 102432 | tf_op jit(solution)/shard_map/ppermute | solution.py:495
  16.2 3.9 %collective-permute-start.4 = (bf16[16,3200]{1,0:T(8,128)(2,1)S(1)}, bf16[16,3200]{1,0:T(8,128)(2,1)S(1)}, u32[]{:S(2)}, u32[]{:S(2)}) collective-permute-start(bf16[16,3200]{1,0:T(8,128)(2,1)S(1)} %get-tuple-element.47), channel_id=1, source_target_pairs={{0,12},{1,13},{2,14},{3,15},{4,8},{5,9},{6,10},{7,11},{8,4},{9,5},... | collective-permute-start | bytes 307208 | tf_op jit(solution)/shard_map/ppermute | solution.py:495
  20.1 3.1 %collective-permute-start.6 = (bf16[16,3200]{1,0:T(8,128)(2,1)S(1)}, bf16[16,3200]{1,0:T(8,128)(2,1)S(1)}, u32[]{:S(2)}, u32[]{:S(2)}) collective-permute-start(bf16[16,3200]{1,0:T(8,128)(2,1)S(1)} %get-tuple-element.49), channel_id=1, source_target_pairs={{0,14},{1,15},{2,12},{3,13},{4,10},{5,11},{6,8},{7,9},{8,6},{9,7},... | collective-permute-start | bytes 307208 | tf_op jit(solution)/shard_map/ppermute | solution.py:495
  23.3 1.0 %copy-done = bf16[2,128,640]{2,1,0:T(8,128)(2,1)S(1)} copy-done((bf16[2,128,640]{2,1,0:T(8,128)(2,1)S(1)}, bf16[2,128,640]{2,1,0:T(8,128)(2,1)}, u32[]{:S(2)}) %copy-start) | copy-done | bytes 327704
  24.2 0.8 copy-done.3
  25.1 0.7 copy-done.7
  25.7 0.7 copy-done.8
  26.4 0.7 copy-done.9
  27.1 1.0 %shard_map.92 = (f32[128,3200]{1,0:T(8,128)S(1)}, bf16[128,128]{1,0:T(8,128)(2,1)S(1)}, f32[128,128]{1,0:T(8,128)S(1)}, f32[128,128]{1,0:T(8,128)S(1)}, bf16[256...) custom-call(s32[2]{0:T(128)S(1)} %pad_add_fusion.meta, bf16[128,3200]{1,0:T(8,128)(2,1)S(1)} %get-tuple-element.42.normed, ...), custom_call_target="tpu_custom_call" | custom-call | bytes 3246728 | tf_op jit(solution)/shard_map/pallas_call | solution.py:480
  28.1 0.4 collective-permute-done.4.refs_3_
  28.5 1.0 %collective-permute-done.6.refs_5_ = bf16[16,3200]{1,0:T(8,128)(2,1)S(1)} collective-permute-done((bf16[16,3200]{1,0:T(8,128)(2,1)S(1)}, bf16[16,3200]{1,0:T(8,128)(2,1)S(1)}, u32[]{:S(2)}, u32[]{:S(2)}) %collective-permute-start.6) | collective-permute-done | bytes 102432 | tf_op jit(solution)/shard_map/ppermute | solution.py:495
  29.5 2.0 %shard_map.93 = (bf16[16,3200]{1,0:T(8,128)(2,1)S(1)}, bf16[16,3200]{1,0:T(8,128)(2,1)S(1)}, bf16[16,3200]{1,0:T(8,128)(2,1)S(1)}, bf16[16,3200]{1,0:T(8,128)(2,1)S(1)}) custom-call(s32[2]{0:T(128)S(1)} %pad_add_fusion.meta, f32[8,40,128]{2,1,0:T(8,128)S(1)} %get-tuple-element.43.masks, bf16[16,3200]{1,0:T(8,128)(2,1)S(1)} %collective-permute-done.1.refs_0_, ...), custom_call_target="tpu_custom_call" | custom-call | bytes 1802248 | tf_op jit(solution)/shard_map/pallas_call | solution.py:480
  31.6 1.8 %collective-permute-start.8 = (bf16[16,3200]{1,0:T(8,128)(2,1)S(1)}, bf16[16,3200]{1,0:T(8,128)(2,1)S(1)}, u32[]{:S(2)}, u32[]{:S(2)}) collective-permute-start(bf16[16,3200]{1,0:T(8,128)(2,1)S(1)} %get-tuple-element.53), channel_id=1, source_target_pairs={{0,2},{1,3},{2,0},{3,1},{4,6},{5,7},{6,4},{7,5},{8,10},{9,11},{10,... | collective-permute-start | bytes 307208 | tf_op jit(solution)/shard_map/ppermute | solution.py:495
  33.3 1.8 %collective-permute-start.10 = (bf16[16,3200]{1,0:T(8,128)(2,1)S(1)}, bf16[16,3200]{1,0:T(8,128)(2,1)S(1)}, u32[]{:S(2)}, u32[]{:S(2)}) collective-permute-start(bf16[16,3200]{1,0:T(8,128)(2,1)S(1)} %get-tuple-element.55), channel_id=1, source_target_pairs={{0,6},{1,7},{2,4},{3,5},{4,2},{5,3},{6,0},{7,1},{8,14},{9,15},{10,... | collective-permute-start | bytes 307208 | tf_op jit(solution)/shard_map/ppermute | solution.py:495
  35.1 2.3 %collective-permute-done.8 = bf16[16,3200]{1,0:T(8,128)(2,1)S(1)} collective-permute-done((bf16[16,3200]{1,0:T(8,128)(2,1)S(1)}, bf16[16,3200]{1,0:T(8,128)(2,1)S(1)}, u32[]{:S(2)}, u32[]{:S(2)}) %collective-permute-start.8) | collective-permute-done | bytes 102432 | tf_op jit(solution)/shard_map/ppermute | solution.py:495
  37.4 0.7 collective-permute-done.9
  38.1 0.9 %collective-permute-done.10 = bf16[16,3200]{1,0:T(8,128)(2,1)S(1)} collective-permute-done((bf16[16,3200]{1,0:T(8,128)(2,1)S(1)}, bf16[16,3200]{1,0:T(8,128)(2,1)S(1)}, u32[]{:S(2)}, u32[]{:S(2)}) %collective-permute-start.10) | collective-permute-done | bytes 102432 | tf_op jit(solution)/shard_map/ppermute | solution.py:495
  39.1 1.7 %collective-permute-done.11.other = bf16[64,3200]{1,0:T(8,128)(2,1)S(1)} collective-permute-done((bf16[64,3200]{1,0:T(8,128)(2,1)S(1)}, bf16[64,3200]{1,0:T(8,128)(2,1)S(1)}, u32[]{:S(2)}, u32[]{:S(2)}) %collective-permute-start.11) | collective-permute-done | bytes 409632 | tf_op jit(solution)/shard_map/ppermute | solution.py:499
  40.8 2.1 %shard_map.94 = (f32[128,3200]{1,0:T(8,128)S(1)}, bf16[128,3200]{1,0:T(8,128)(2,1)S(1)}, bf16[32,3200]{1,0:T(8,128)(2,1)S(1)}, bf16[32,3200]{1,0:T(8,128)(2,1)S(...) custom-call(bf16[64,3200]{1,0:T(8,128)(2,1)S(1)} %constant_dynamic-update-slice_fusion.own, ...), custom_call_target="tpu_custom_call" | custom-call | bytes 7602176 | tf_op jit(solution)/shard_map/pallas_call | solution.py:480
  42.9 2.0 %collective-permute-start.12 = (bf16[32,3200]{1,0:T(8,128)(2,1)S(1)}, bf16[32,3200]{1,0:T(8,128)(2,1)S(1)}, u32[]{:S(2)}, u32[]{:S(2)}) collective-permute-start(bf16[32,3200]{1,0:T(8,128)(2,1)S(1)} %get-tuple-element.62), channel_id=1, source_target_pairs={{0,4},{1,5},{2,6},{3,7},{4,0},{5,1},{6,2},{7,3},{8,12},{9,13},{10,... | collective-permute-start | bytes 614408 | tf_op jit(solution)/shard_map/ppermute | solution.py:495
  44.9 1.2 %collective-permute-start.13 = (bf16[32,3200]{1,0:T(8,128)(2,1)S(1)}, bf16[32,3200]{1,0:T(8,128)(2,1)S(1)}, u32[]{:S(2)}, u32[]{:S(2)}) collective-permute-start(bf16[32,3200]{1,0:T(8,128)(2,1)S(1)} %get-tuple-element.63), channel_id=1, source_target_pairs={{0,6},{1,7},{2,4},{3,5},{4,2},{5,3},{6,0},{7,1},{8,14},{9,15},{10,... | collective-permute-start | bytes 614408 | tf_op jit(solution)/shard_map/ppermute | solution.py:495
  46.1 0.4 collective-permute-start.14
  46.5 4.4 %collective-permute-done.12.refs_0_ = bf16[32,3200]{1,0:T(8,128)(2,1)S(1)} collective-permute-done((bf16[32,3200]{1,0:T(8,128)(2,1)S(1)}, bf16[32,3200]{1,0:T(8,128)(2,1)S(1)}, u32[]{:S(2)}, u32[]{:S(2)}) %collective-permute-start.12) | collective-permute-done | bytes 204832 | tf_op jit(solution)/shard_map/ppermute | solution.py:495
  50.9 4.8 %collective-permute-done.13.refs_1_ = bf16[32,3200]{1,0:T(8,128)(2,1)S(1)} collective-permute-done((bf16[32,3200]{1,0:T(8,128)(2,1)S(1)}, bf16[32,3200]{1,0:T(8,128)(2,1)S(1)}, u32[]{:S(2)}, u32[]{:S(2)}) %collective-permute-start.13) | collective-permute-done | bytes 204832 | tf_op jit(solution)/shard_map/ppermute | solution.py:495
  55.7 1.4 %collective-permute-done.14.refs_2_ = bf16[32,3200]{1,0:T(8,128)(2,1)S(1)} collective-permute-done((bf16[32,3200]{1,0:T(8,128)(2,1)S(1)}, bf16[32,3200]{1,0:T(8,128)(2,1)S(1)}, u32[]{:S(2)}, u32[]{:S(2)}) %collective-permute-start.14) | collective-permute-done | bytes 204832 | tf_op jit(solution)/shard_map/ppermute | solution.py:495
  57.0 2.0 %shard_map.95 = (bf16[16,3200]{1,0:T(8,128)(2,1)S(1)}, bf16[16,3200]{1,0:T(8,128)(2,1)S(1)}, bf16[16,3200]{1,0:T(8,128)(2,1)S(1)}, bf16[16,3200]{1,0:T(8,128)(2,...) custom-call(s32[2]{0:T(128)S(1)} %pad_add_fusion.meta, ...), custom_call_target="tpu_custom_call" | custom-call | bytes 1802248 | tf_op jit(solution)/shard_map/pallas_call | solution.py:480
  59.1 0.7 collective-permute-start.15
  59.8 1.7 %collective-permute-start.16 = (bf16[16,3200]{1,0:T(8,128)(2,1)S(1)}, bf16[16,3200]{1,0:T(8,128)(2,1)S(1)}, u32[]{:S(2)}, u32[]{:S(2)}) collective-permute-start(bf16[16,3200]{1,0:T(8,128)(2,1)S(1)} %get-tuple-element.68), channel_id=1, source_target_pairs={{0,4},{1,5},{2,6},{3,7},{4,0},{5,1},{6,2},{7,3},{8,12},{9,13},{10,... | collective-permute-start | bytes 307208 | tf_op jit(solution)/shard_map/ppermute | solution.py:495
  61.4 1.2 %collective-permute-start.17 = (bf16[16,3200]{1,0:T(8,128)(2,1)S(1)}, bf16[16,3200]{1,0:T(8,128)(2,1)S(1)}, u32[]{:S(2)}, u32[]{:S(2)}) collective-permute-start(bf16[16,3200]{1,0:T(8,128)(2,1)S(1)} %get-tuple-element.69), channel_id=1, source_target_pairs={{0,6},{1,7},{2,4},{3,5},{4,2},{5,3},{6,0},{7,1},{8,14},{9,15},{10,... | collective-permute-start | bytes 307208 | tf_op jit(solution)/shard_map/ppermute | solution.py:495
  62.6 2.9 %collective-permute-start.18 = (bf16[16,3200]{1,0:T(8,128)(2,1)S(1)}, bf16[16,3200]{1,0:T(8,128)(2,1)S(1)}, u32[]{:S(2)}, u32[]{:S(2)}) collective-permute-start(bf16[16,3200]{1,0:T(8,128)(2,1)S(1)} %get-tuple-element.70), channel_id=1, source_target_pairs={{0,8},{1,9},{2,10},{3,11},{4,12},{5,13},{6,14},{7,15},{8,0},{9,1},... | collective-permute-start | bytes 307208 | tf_op jit(solution)/shard_map/ppermute | solution.py:495
  65.6 0.9 %collective-permute-start.19 = (bf16[16,3200]{1,0:T(8,128)(2,1)S(1)}, bf16[16,3200]{1,0:T(8,128)(2,1)S(1)}, u32[]{:S(2)}, u32[]{:S(2)}) collective-permute-start(bf16[16,3200]{1,0:T(8,128)(2,1)S(1)} %get-tuple-element.71), channel_id=1, source_target_pairs={{0,10},{1,11},{2,8},{3,9},{4,14},{5,15},{6,12},{7,13},{8,2},{9,3},... | collective-permute-start | bytes 307208 | tf_op jit(solution)/shard_map/ppermute | solution.py:495
  66.5 2.7 %collective-permute-start.20 = (bf16[16,3200]{1,0:T(8,128)(2,1)S(1)}, bf16[16,3200]{1,0:T(8,128)(2,1)S(1)}, u32[]{:S(2)}, u32[]{:S(2)}) collective-permute-start(bf16[16,3200]{1,0:T(8,128)(2,1)S(1)} %get-tuple-element.72), channel_id=1, source_target_pairs={{0,12},{1,13},{2,14},{3,15},{4,8},{5,9},{6,10},{7,11},{8,4},{9,5},... | collective-permute-start | bytes 307208 | tf_op jit(solution)/shard_map/ppermute | solution.py:495
  69.2 1.1 %collective-permute-start.21 = (bf16[16,3200]{1,0:T(8,128)(2,1)S(1)}, bf16[16,3200]{1,0:T(8,128)(2,1)S(1)}, u32[]{:S(2)}, u32[]{:S(2)}) collective-permute-start(bf16[16,3200]{1,0:T(8,128)(2,1)S(1)} %get-tuple-element.73), channel_id=1, source_target_pairs={{0,14},{1,15},{2,12},{3,13},{4,10},{5,11},{6,8},{7,9},{8,6},{9,7},... | collective-permute-start | bytes 307208 | tf_op jit(solution)/shard_map/ppermute | solution.py:495
  70.3 6.6 %collective-permute-done.18 = bf16[16,3200]{1,0:T(8,128)(2,1)S(1)} collective-permute-done((bf16[16,3200]{1,0:T(8,128)(2,1)S(1)}, bf16[16,3200]{1,0:T(8,128)(2,1)S(1)}, u32[]{:S(2)}, u32[]{:S(2)}) %collective-permute-start.18) | collective-permute-done | bytes 102432 | tf_op jit(solution)/shard_map/ppermute | solution.py:495
  76.9 3.3 %collective-permute-done.19 = bf16[16,3200]{1,0:T(8,128)(2,1)S(1)} collective-permute-done((bf16[16,3200]{1,0:T(8,128)(2,1)S(1)}, bf16[16,3200]{1,0:T(8,128)(2,1)S(1)}, u32[]{:S(2)}, u32[]{:S(2)}) %collective-permute-start.19) | collective-permute-done | bytes 102432 | tf_op jit(solution)/shard_map/ppermute | solution.py:495
  80.4 1.0 %shard_map.96 = (f32[128,3200]{1,0:T(8,128)S(1)}, bf16[128,128]{1,0:T(8,128)(2,1)S(1)}, f32[128,128]{1,0:T(8,128)S(1)}) custom-call(s32[2]{0:T(128)S(1)} %pad_add_fusion.meta, bf16[128,3200]{1,0:T(8,128)(2,1)S(1)} %get-tuple-element.75.normed, bf16[2,128,640]{2,1,0:T(8,128)(2,1)S(1)} %copy-done.1, f32[2,128]{1,0:T(2,128)S(1)} %copy-done.7, ...), custom_call_target="tpu_custom_call" | custom-call | bytes 2950152 | tf_op jit(solution)/shard_map/pallas_call | solution.py:480
  81.3 0.7 collective-permute-done.22.other
  82.1 3.9 %shard_map.97 = bf16[40,40,128]{2,1,0:T(8,128)(2,1)} custom-call(s32[2]{0:T(128)S(1)} %pad_add_fusion.meta, bf16[64,3200]{1,0:T(8,128)(2,1)S(1)} %add_convert_fusion.own, bf16[64,3200]{1,0:T(8,128)(2,1)S(1)} %collective-permute-done.22.other, f32[128,3200]{1,0:T(8,128)S(1)} %get-tuple-element.74.stream, f32[128,3200]{1,0:T(8,128)S(1)} %get-tuple-element.76.gate, ...), custom_call_target="tpu_custom_call" | custom-call | bytes 4866568 | tf_op jit(solution)/shard_map/pallas_call | solution.py:480
  (35 shorter events, 0.4 us)
Async XLA Ops:
  0.0 2.1 %collective-permute-start = (bf16[40,40,128]{2,1,0:T(8,128)(2,1)}, bf16[40,40,128]{2,1,0:T(8,128)(2,1)S(1)}, u32[]{:S(2)}, u32[]{:S(2)}) collective-permute-start(bf16[40,40,128]{2,1,0:T(8,128)(2,1)} %own.1), channel_id=1, source_target_pairs={{0,1},{1,0},{2,3},{3,2},{4,5},{5,4},{6,7},{7,6},{8,9},{9,8},{10,11... | collective-permute-start | bytes 1228808 | tf_op jit(solution)/shard_map/ppermute | solution.py:499
  2.1 1.0 %copy-start.2 = (bf16[40,40,128]{2,1,0:T(8,128)(2,1)S(1)}, bf16[40,40,128]{2,1,0:T(8,128)(2,1)}, u32[]{:S(2)}) copy-start(bf16[40,40,128]{2,1,0:T(8,128)(2,1)} %own.1) | copy-start | bytes 1228804
  4.8 11.4 %collective-permute-start.1 = (bf16[16,3200]{1,0:T(8,128)(2,1)S(1)}, bf16[16,3200]{1,0:T(8,128)(2,1)S(1)}, u32[]{:S(2)}, u32[]{:S(2)}) collective-permute-start(bf16[16,3200]{1,0:T(8,128)(2,1)S(1)} %get-tuple-element.44), channel_id=1, source_target_pairs={{0,8},{1,9},{2,10},{3,11},{4,12},{5,13},{6,14},{7,15},{8,0},{9,1},... | collective-permute-start | bytes 307208 | tf_op jit(solution)/shard_map/ppermute | solution.py:495
  8.7 11.4 %collective-permute-start.2 = (bf16[16,3200]{1,0:T(8,128)(2,1)S(1)}, bf16[16,3200]{1,0:T(8,128)(2,1)S(1)}, u32[]{:S(2)}, u32[]{:S(2)}) collective-permute-start(bf16[16,3200]{1,0:T(8,128)(2,1)S(1)} %get-tuple-element.45), channel_id=1, source_target_pairs={{0,10},{1,11},{2,8},{3,9},{4,14},{5,15},{6,12},{7,13},{8,2},{9,3},... | collective-permute-start | bytes 307208 | tf_op jit(solution)/shard_map/ppermute | solution.py:495
  10.0 19.5 %collective-permute-start.3 = (bf16[32,3200]{1,0:T(8,128)(2,1)S(1)}, bf16[32,3200]{1,0:T(8,128)(2,1)S(1)}, u32[]{:S(2)}, u32[]{:S(2)}) collective-permute-start(bf16[32,3200]{1,0:T(8,128)(2,1)S(1)} %get-tuple-element.46), channel_id=1, source_target_pairs={{0,4},{1,5},{2,6},{3,7},{4,0},{5,1},{6,2},{7,3},{8,12},{9,13},{10,... | collective-permute-start | bytes 614408 | tf_op jit(solution)/shard_map/ppermute | solution.py:495
  11.6 17.9 %collective-permute-start.5 = (bf16[32,3200]{1,0:T(8,128)(2,1)S(1)}, bf16[32,3200]{1,0:T(8,128)(2,1)S(1)}, u32[]{:S(2)}, u32[]{:S(2)}) collective-permute-start(bf16[32,3200]{1,0:T(8,128)(2,1)S(1)} %get-tuple-element.48), channel_id=1, source_target_pairs={{0,6},{1,7},{2,4},{3,5},{4,2},{5,3},{6,0},{7,1},{8,14},{9,15},{10,... | collective-permute-start | bytes 614408 | tf_op jit(solution)/shard_map/ppermute | solution.py:495
  11.7 17.8 %collective-permute-start.7 = (bf16[32,3200]{1,0:T(8,128)(2,1)S(1)}, bf16[32,3200]{1,0:T(8,128)(2,1)S(1)}, u32[]{:S(2)}, u32[]{:S(2)}) collective-permute-start(bf16[32,3200]{1,0:T(8,128)(2,1)S(1)} %get-tuple-element.50), channel_id=1, source_target_pairs={{0,2},{1,3},{2,0},{3,1},{4,6},{5,7},{6,4},{7,5},{8,10},{9,11},{10,... | collective-permute-start | bytes 614408 | tf_op jit(solution)/shard_map/ppermute | solution.py:495
  16.2 12.3 %collective-permute-start.4 = (bf16[16,3200]{1,0:T(8,128)(2,1)S(1)}, bf16[16,3200]{1,0:T(8,128)(2,1)S(1)}, u32[]{:S(2)}, u32[]{:S(2)}) collective-permute-start(bf16[16,3200]{1,0:T(8,128)(2,1)S(1)} %get-tuple-element.47), channel_id=1, source_target_pairs={{0,12},{1,13},{2,14},{3,15},{4,8},{5,9},{6,10},{7,11},{8,4},{9,5},... | collective-permute-start | bytes 307208 | tf_op jit(solution)/shard_map/ppermute | solution.py:495
  20.1 9.4 %collective-permute-start.6 = (bf16[16,3200]{1,0:T(8,128)(2,1)S(1)}, bf16[16,3200]{1,0:T(8,128)(2,1)S(1)}, u32[]{:S(2)}, u32[]{:S(2)}) collective-permute-start(bf16[16,3200]{1,0:T(8,128)(2,1)S(1)} %get-tuple-element.49), channel_id=1, source_target_pairs={{0,14},{1,15},{2,12},{3,13},{4,10},{5,11},{6,8},{7,9},{8,6},{9,7},... | collective-permute-start | bytes 307208 | tf_op jit(solution)/shard_map/ppermute | solution.py:495
  23.3 1.0 %copy-start = (bf16[2,128,640]{2,1,0:T(8,128)(2,1)S(1)}, bf16[2,128,640]{2,1,0:T(8,128)(2,1)}, u32[]{:S(2)}) copy-start(bf16[2,128,640]{2,1,0:T(8,128)(2,1)} %weight.3) | copy-start | bytes 983044
  24.2 0.8 copy-start.3
  25.1 0.7 copy-start.7
  25.7 0.7 copy-start.8
  26.4 0.7 copy-start.9
  31.6 5.8 %collective-permute-start.8 = (bf16[16,3200]{1,0:T(8,128)(2,1)S(1)}, bf16[16,3200]{1,0:T(8,128)(2,1)S(1)}, u32[]{:S(2)}, u32[]{:S(2)}) collective-permute-start(bf16[16,3200]{1,0:T(8,128)(2,1)S(1)} %get-tuple-element.53), channel_id=1, source_target_pairs={{0,2},{1,3},{2,0},{3,1},{4,6},{5,7},{6,4},{7,5},{8,10},{9,11},{10,... | collective-permute-start | bytes 307208 | tf_op jit(solution)/shard_map/ppermute | solution.py:495
  33.3 4.8 %collective-permute-start.9 = (bf16[16,3200]{1,0:T(8,128)(2,1)S(1)}, bf16[16,3200]{1,0:T(8,128)(2,1)S(1)}, u32[]{:S(2)}, u32[]{:S(2)}) collective-permute-start(bf16[16,3200]{1,0:T(8,128)(2,1)S(1)} %get-tuple-element.54), channel_id=1, source_target_pairs={{0,4},{1,5},{2,6},{3,7},{4,0},{5,1},{6,2},{7,3},{8,12},{9,13},{10,... | collective-permute-start | bytes 307208 | tf_op jit(solution)/shard_map/ppermute | solution.py:495
  33.3 5.7 %collective-permute-start.10 = (bf16[16,3200]{1,0:T(8,128)(2,1)S(1)}, bf16[16,3200]{1,0:T(8,128)(2,1)S(1)}, u32[]{:S(2)}, u32[]{:S(2)}) collective-permute-start(bf16[16,3200]{1,0:T(8,128)(2,1)S(1)} %get-tuple-element.55), channel_id=1, source_target_pairs={{0,6},{1,7},{2,4},{3,5},{4,2},{5,3},{6,0},{7,1},{8,14},{9,15},{10,... | collective-permute-start | bytes 307208 | tf_op jit(solution)/shard_map/ppermute | solution.py:495
  39.0 1.8 %collective-permute-start.11 = (bf16[64,3200]{1,0:T(8,128)(2,1)S(1)}, bf16[64,3200]{1,0:T(8,128)(2,1)S(1)}, u32[]{:S(2)}, u32[]{:S(2)}) collective-permute-start(bf16[64,3200]{1,0:T(8,128)(2,1)S(1)} %constant_dynamic-update-slice_fusion.own), channel_id=1, source_target_pairs={{0,1},{1,0},{2,3},{3,2},{4,5},{5,4},{6,7},{7,6},{8,9},{9,8},{10,11... | collective-permute-start | bytes 1228808 | tf_op jit(solution)/shard_map/ppermute | solution.py:499
  42.9 37.5 %copy-start.1 = (bf16[2,128,640]{2,1,0:T(8,128)(2,1)S(1)}, bf16[2,128,640]{2,1,0:T(8,128)(2,1)}, u32[]{:S(2)}) copy-start(bf16[2,128,640]{2,1,0:T(8,128)(2,1)} %weight.3) | copy-start | bytes 983044
  42.9 37.5 %copy-start.4 = (bf16[2,128,128]{2,1,0:T(8,128)(2,1)S(1)}, bf16[2,128,128]{2,1,0:T(8,128)(2,1)}, u32[]{:S(2)}) copy-start(bf16[2,128,128]{2,1,0:T(8,128)(2,1)} %out_weight.3) | copy-start | bytes 196612
  42.9 8.0 %collective-permute-start.12 = (bf16[32,3200]{1,0:T(8,128)(2,1)S(1)}, bf16[32,3200]{1,0:T(8,128)(2,1)S(1)}, u32[]{:S(2)}, u32[]{:S(2)}) collective-permute-start(bf16[32,3200]{1,0:T(8,128)(2,1)S(1)} %get-tuple-element.62), channel_id=1, source_target_pairs={{0,4},{1,5},{2,6},{3,7},{4,0},{5,1},{6,2},{7,3},{8,12},{9,13},{10,... | collective-permute-start | bytes 614408 | tf_op jit(solution)/shard_map/ppermute | solution.py:495
  44.9 10.8 %collective-permute-start.13 = (bf16[32,3200]{1,0:T(8,128)(2,1)S(1)}, bf16[32,3200]{1,0:T(8,128)(2,1)S(1)}, u32[]{:S(2)}, u32[]{:S(2)}) collective-permute-start(bf16[32,3200]{1,0:T(8,128)(2,1)S(1)} %get-tuple-element.63), channel_id=1, source_target_pairs={{0,6},{1,7},{2,4},{3,5},{4,2},{5,3},{6,0},{7,1},{8,14},{9,15},{10,... | collective-permute-start | bytes 614408 | tf_op jit(solution)/shard_map/ppermute | solution.py:495
  46.1 11.0 %collective-permute-start.14 = (bf16[32,3200]{1,0:T(8,128)(2,1)S(1)}, bf16[32,3200]{1,0:T(8,128)(2,1)S(1)}, u32[]{:S(2)}, u32[]{:S(2)}) collective-permute-start(bf16[32,3200]{1,0:T(8,128)(2,1)S(1)} %get-tuple-element.64), channel_id=1, source_target_pairs={{0,2},{1,3},{2,0},{3,1},{4,6},{5,7},{6,4},{7,5},{8,10},{9,11},{10,... | collective-permute-start | bytes 614408 | tf_op jit(solution)/shard_map/ppermute | solution.py:495
  57.0 25.0 %copy-start.5 = (bf16[128,512]{1,0:T(8,128)(2,1)S(1)}, bf16[128,512]{1,0:T(8,128)(2,1)}, u32[]{:S(2)}) copy-start(bf16[128,512]{1,0:T(8,128)(2,1)} %expand.1) | copy-start | bytes 393220
  57.0 25.0 %copy-start.6 = (bf16[512,128]{1,0:T(8,128)(2,1)S(1)}, bf16[512,128]{1,0:T(8,128)(2,1)}, u32[]{:S(2)}) copy-start(bf16[512,128]{1,0:T(8,128)(2,1)} %shrink.1) | copy-start | bytes 393220
  57.0 25.0 %copy-start.10 = (f32[128]{0:T(128)S(1)}, f32[128]{0:T(128)}, u32[]{:S(2)}) copy-start(f32[128]{0:T(128)} %param.15) | copy-start | bytes 1540
  59.1 7.4 %collective-permute-start.15 = (bf16[16,3200]{1,0:T(8,128)(2,1)S(1)}, bf16[16,3200]{1,0:T(8,128)(2,1)S(1)}, u32[]{:S(2)}, u32[]{:S(2)}) collective-permute-start(bf16[16,3200]{1,0:T(8,128)(2,1)S(1)} %get-tuple-element.67), channel_id=1, source_target_pairs={{0,2},{1,3},{2,0},{3,1},{4,6},{5,7},{6,4},{7,5},{8,10},{9,11},{10,... | collective-permute-start | bytes 307208 | tf_op jit(solution)/shard_map/ppermute | solution.py:495
  59.8 9.4 %collective-permute-start.16 = (bf16[16,3200]{1,0:T(8,128)(2,1)S(1)}, bf16[16,3200]{1,0:T(8,128)(2,1)S(1)}, u32[]{:S(2)}, u32[]{:S(2)}) collective-permute-start(bf16[16,3200]{1,0:T(8,128)(2,1)S(1)} %get-tuple-element.68), channel_id=1, source_target_pairs={{0,4},{1,5},{2,6},{3,7},{4,0},{5,1},{6,2},{7,3},{8,12},{9,13},{10,... | collective-permute-start | bytes 307208 | tf_op jit(solution)/shard_map/ppermute | solution.py:495
  61.4 8.9 %collective-permute-start.17 = (bf16[16,3200]{1,0:T(8,128)(2,1)S(1)}, bf16[16,3200]{1,0:T(8,128)(2,1)S(1)}, u32[]{:S(2)}, u32[]{:S(2)}) collective-permute-start(bf16[16,3200]{1,0:T(8,128)(2,1)S(1)} %get-tuple-element.69), channel_id=1, source_target_pairs={{0,6},{1,7},{2,4},{3,5},{4,2},{5,3},{6,0},{7,1},{8,14},{9,15},{10,... | collective-permute-start | bytes 307208 | tf_op jit(solution)/shard_map/ppermute | solution.py:495
  62.6 14.2 %collective-permute-start.18 = (bf16[16,3200]{1,0:T(8,128)(2,1)S(1)}, bf16[16,3200]{1,0:T(8,128)(2,1)S(1)}, u32[]{:S(2)}, u32[]{:S(2)}) collective-permute-start(bf16[16,3200]{1,0:T(8,128)(2,1)S(1)} %get-tuple-element.70), channel_id=1, source_target_pairs={{0,8},{1,9},{2,10},{3,11},{4,12},{5,13},{6,14},{7,15},{8,0},{9,1},... | collective-permute-start | bytes 307208 | tf_op jit(solution)/shard_map/ppermute | solution.py:495
  65.6 14.6 %collective-permute-start.19 = (bf16[16,3200]{1,0:T(8,128)(2,1)S(1)}, bf16[16,3200]{1,0:T(8,128)(2,1)S(1)}, u32[]{:S(2)}, u32[]{:S(2)}) collective-permute-start(bf16[16,3200]{1,0:T(8,128)(2,1)S(1)} %get-tuple-element.71), channel_id=1, source_target_pairs={{0,10},{1,11},{2,8},{3,9},{4,14},{5,15},{6,12},{7,13},{8,2},{9,3},... | collective-permute-start | bytes 307208 | tf_op jit(solution)/shard_map/ppermute | solution.py:495
  66.5 13.7 %collective-permute-start.20 = (bf16[16,3200]{1,0:T(8,128)(2,1)S(1)}, bf16[16,3200]{1,0:T(8,128)(2,1)S(1)}, u32[]{:S(2)}, u32[]{:S(2)}) collective-permute-start(bf16[16,3200]{1,0:T(8,128)(2,1)S(1)} %get-tuple-element.72), channel_id=1, source_target_pairs={{0,12},{1,13},{2,14},{3,15},{4,8},{5,9},{6,10},{7,11},{8,4},{9,5},... | collective-permute-start | bytes 307208 | tf_op jit(solution)/shard_map/ppermute | solution.py:495
  69.2 11.0 %collective-permute-start.21 = (bf16[16,3200]{1,0:T(8,128)(2,1)S(1)}, bf16[16,3200]{1,0:T(8,128)(2,1)S(1)}, u32[]{:S(2)}, u32[]{:S(2)}) collective-permute-start(bf16[16,3200]{1,0:T(8,128)(2,1)S(1)} %get-tuple-element.73), channel_id=1, source_target_pairs={{0,14},{1,15},{2,12},{3,13},{4,10},{5,11},{6,8},{7,9},{8,6},{9,7},... | collective-permute-start | bytes 307208 | tf_op jit(solution)/shard_map/ppermute | solution.py:495
  80.3 1.8 %collective-permute-start.22 = (bf16[64,3200]{1,0:T(8,128)(2,1)S(1)}, bf16[64,3200]{1,0:T(8,128)(2,1)S(1)}, u32[]{:S(2)}, u32[]{:S(2)}) collective-permute-start(bf16[64,3200]{1,0:T(8,128)(2,1)S(1)} %add_convert_fusion.own), channel_id=1, source_target_pairs={{0,1},{1,0},{2,3},{3,2},{4,5},{5,4},{6,7},{7,6},{8,9},{9,8},{10,11... | collective-permute-start | bytes 1228808 | tf_op jit(solution)/shard_map/ppermute | solution.py:499

commit v6 on v5

--- a/solution.py
+++ b/solution.py
@@ -134,7 +134,7 @@
 FIRST_ORDER = (4, 5, 2, 6, 3, 7, 1, 0)
 LAST_ORDER = (4, 2, 5, 3, 6, 1, 7, 0)
 WITHIN_HALF = (3, 2, 1, 0)
-SIDES_WITHIN = (2, 3, 1, 0)
+SIDES_WITHIN = (2, 1, 3, 0)
 
 
 def aligned(start, size):
@@ -410,6 +410,14 @@
             target = dap ^ (k >> 1)
             begin = ((target >> 1) ^ sub) * width + (target & 1) * rows + step * GROUP
             outs[k][:, lanes] = gather_group(total.at[k & 1], count, begin, tall, width, lane)
+
+
+def add_halves_kernel(*refs):
+    parts, out = dict(zip(LAST_ORDER, refs[:8])), refs[8]
+    size = parts[0].shape[0]
+    for k in range(4):
+        value = parts[k][...].astype(F32) + parts[4 + k][...].astype(F32)
+        out[k * size : (k + 1) * size, :] = value.astype(BF16)
 
 
 def output_weights(table, square, gain, meta):
@@ -585,10 +593,8 @@
         ],
         (meta, masks, *arrived),
     )
-    returned = {k: to_chip(sums[k], k) for k in LAST_ORDER}
-    near = jnp.concatenate([returned[k] for k in range(4)], axis=0)
-    far = jnp.concatenate([returned[4 + k] for k in range(4)], axis=0)
-    own = (near.astype(F32) + far.astype(F32)).astype(BF16)
+    returned = [to_chip(sums[k], k) for k in LAST_ORDER]
+    (own,) = call(add_halves_kernel, [shape((4 * part, pairs), BF16)], [], returned, 0)
     other = swap_cores(own)
     (result,) = call(
         last_kernel,

time: 86.8 us -> 83.3 us (0.960)
  waiting for transfers between devices: 30.8 us -> 24.1 us
  starting transfers between devices: 34.6 us -> 37.2 us
    ppermute x20, waiting for transfers between devices: 28.4 us -> 21.6 us  [to_chip(): return lax.ppermute(value, CHIPS, pairs)]
    ppermute x20, starting transfers between devices: 34.1 us -> 36.6 us  [to_chip(): return lax.ppermute(value, CHIPS, pairs)]
    pallas_call x7 -> x8, Pallas kernels: 13.7 us -> 13.8 us  [call(): pl.pallas_call(kernel, out_shape=outs, in_specs=in_specs, out_specs=[pl.B...]
    unnamed x25 -> x27, local copies, waits for them, and re-layouts: 4.9 us -> 4.91 us
  transfers between devices with their start and end apart: 23 -> 23, of which waited for: 13 -> 14; matrix products, arithmetic and copies ran while one was open for 2% -> 2% of each run, Pallas kernels for 2% -> 2%
where the time goes in v6:
time: 83.3 us; the launch traced here: 81.8 us
  starting transfers between devices  37.2 us (45%)
  waiting for transfers between devices  24.1 us (29%)
  Pallas kernels  13.8 us (17%)
  local copies, waits for them, and re-layouts  6.51 us (8%)
    ppermute x20, starting transfers between devices, to_chip(): return lax.ppermute(value, CHIPS, pairs)  36.6 us
    ppermute x20, waiting for transfers between devices, to_chip(): return lax.ppermute(value, CHIPS, pairs)  21.6 us
    pallas_call x8, Pallas kernels, call(): pl.pallas_call(kernel, out_shape=outs, in_specs=in_specs, out_specs=[pl.B...  13.8 us
    unnamed x27, local copies, waits for them, and re-layouts  4.91 us
    ppermute x3, waiting for transfers between devices, swap_cores(): return lax.ppermute(value, 'pair', [(0, 1), (1, 0)])  2.46 us
  transfers between devices with their start and end apart: 23, of which 14 were waited for; matrix products, arithmetic and copies ran while one was open for 2% of the time, Pallas kernels for 2%

profile of v6, /device:TPU:0, one launch (start us, length us, event | category | flops | bytes accessed | tf_op | source)
XLA Modules:
  0.0 81.8 jit_solution(8329360449122088863)
XLA Ops:
  0.0 0.5 collective-permute-start
  0.5 0.7 slice.6.gain
  1.2 0.9 %slice_bitcast_fusion.weight = bf16[128,512]{1,0:T(8,128)(2,1)S(1)} fusion(bf16[2,128,640]{2,1,0:T(8,128)(2,1)} %weight.3), kind=kLoop, calls=%fused_computation | loop fusion | bytes 262144 | tf_op jit(solution)/shard_map/squeeze | solution.py:541
  2.1 1.0 %copy-done.2 = bf16[40,40,128]{2,1,0:T(8,128)(2,1)S(1)} copy-done((bf16[40,40,128]{2,1,0:T(8,128)(2,1)S(1)}, bf16[40,40,128]{2,1,0:T(8,128)(2,1)}, u32[]{:S(2)}) %copy-start.2) | copy-done | bytes 409624
  3.1 1.7 %shard_map.91 = (f32[128,3200]{1,0:T(8,128)S(1)}, bf16[128,3200]{1,0:T(8,128)(2,1)S(1)}, bf16[32,3200]{1,0:T(8,128)(2,1)S(1)}, bf16[32,3200]{1,0:T(8,128)(2,1)S(...) custom-call(s32[2]{0:T(128)S(1)} %pad_add_fusion.meta, ...), custom_call_target="tpu_custom_call" | custom-call | bytes 4637192 | tf_op jit(solution)/shard_map/pallas_call | solution.py:488
  4.8 3.9 %collective-permute-start.1 = (bf16[16,3200]{1,0:T(8,128)(2,1)S(1)}, bf16[16,3200]{1,0:T(8,128)(2,1)S(1)}, u32[]{:S(2)}, u32[]{:S(2)}) collective-permute-start(bf16[16,3200]{1,0:T(8,128)(2,1)S(1)} %get-tuple-element.44), channel_id=1, source_target_pairs={{0,8},{1,9},{2,10},{3,11},{4,12},{5,13},{6,14},{7,15},{8,0},{9,1},... | collective-permute-start | bytes 307208 | tf_op jit(solution)/shard_map/ppermute | solution.py:503
  8.7 1.3 %collective-permute-start.2 = (bf16[16,3200]{1,0:T(8,128)(2,1)S(1)}, bf16[16,3200]{1,0:T(8,128)(2,1)S(1)}, u32[]{:S(2)}, u32[]{:S(2)}) collective-permute-start(bf16[16,3200]{1,0:T(8,128)(2,1)S(1)} %get-tuple-element.45), channel_id=1, source_target_pairs={{0,10},{1,11},{2,8},{3,9},{4,14},{5,15},{6,12},{7,13},{8,2},{9,3},... | collective-permute-start | bytes 307208 | tf_op jit(solution)/shard_map/ppermute | solution.py:503
  10.0 1.6 %collective-permute-start.3 = (bf16[32,3200]{1,0:T(8,128)(2,1)S(1)}, bf16[32,3200]{1,0:T(8,128)(2,1)S(1)}, u32[]{:S(2)}, u32[]{:S(2)}) collective-permute-start(bf16[32,3200]{1,0:T(8,128)(2,1)S(1)} %get-tuple-element.46), channel_id=1, source_target_pairs={{0,4},{1,5},{2,6},{3,7},{4,0},{5,1},{6,2},{7,3},{8,12},{9,13},{10,... | collective-permute-start | bytes 614408 | tf_op jit(solution)/shard_map/ppermute | solution.py:503
  11.6 0.2 collective-permute-start.5
  11.7 1.7 %collective-permute-start.7 = (bf16[32,3200]{1,0:T(8,128)(2,1)S(1)}, bf16[32,3200]{1,0:T(8,128)(2,1)S(1)}, u32[]{:S(2)}, u32[]{:S(2)}) collective-permute-start(bf16[32,3200]{1,0:T(8,128)(2,1)S(1)} %get-tuple-element.50), channel_id=1, source_target_pairs={{0,2},{1,3},{2,0},{3,1},{4,6},{5,7},{6,4},{7,5},{8,10},{9,11},{10,... | collective-permute-start | bytes 614408 | tf_op jit(solution)/shard_map/ppermute | solution.py:503
  13.5 2.7 %collective-permute-done.1.refs_0_ = bf16[16,3200]{1,0:T(8,128)(2,1)S(1)} collective-permute-done((bf16[16,3200]{1,0:T(8,128)(2,1)S(1)}, bf16[16,3200]{1,0:T(8,128)(2,1)S(1)}, u32[]{:S(2)}, u32[]{:S(2)}) %collective-permute-start.1) | collective-permute-done | bytes 102432 | tf_op jit(solution)/shard_map/ppermute | solution.py:503
  16.2 3.9 %collective-permute-start.4 = (bf16[16,3200]{1,0:T(8,128)(2,1)S(1)}, bf16[16,3200]{1,0:T(8,128)(2,1)S(1)}, u32[]{:S(2)}, u32[]{:S(2)}) collective-permute-start(bf16[16,3200]{1,0:T(8,128)(2,1)S(1)} %get-tuple-element.47), channel_id=1, source_target_pairs={{0,12},{1,13},{2,14},{3,15},{4,8},{5,9},{6,10},{7,11},{8,4},{9,5},... | collective-permute-start | bytes 307208 | tf_op jit(solution)/shard_map/ppermute | solution.py:503
  20.1 3.1 %collective-permute-start.6 = (bf16[16,3200]{1,0:T(8,128)(2,1)S(1)}, bf16[16,3200]{1,0:T(8,128)(2,1)S(1)}, u32[]{:S(2)}, u32[]{:S(2)}) collective-permute-start(bf16[16,3200]{1,0:T(8,128)(2,1)S(1)} %get-tuple-element.49), channel_id=1, source_target_pairs={{0,14},{1,15},{2,12},{3,13},{4,10},{5,11},{6,8},{7,9},{8,6},{9,7},... | collective-permute-start | bytes 307208 | tf_op jit(solution)/shard_map/ppermute | solution.py:503
  23.3 1.0 %copy-done = bf16[2,128,640]{2,1,0:T(8,128)(2,1)S(1)} copy-done((bf16[2,128,640]{2,1,0:T(8,128)(2,1)S(1)}, bf16[2,128,640]{2,1,0:T(8,128)(2,1)}, u32[]{:S(2)}) %copy-start) | copy-done | bytes 327704
  24.2 0.8 %copy-done.3 = bf16[2,128,128]{2,1,0:T(8,128)(2,1)S(1)} copy-done((bf16[2,128,128]{2,1,0:T(8,128)(2,1)S(1)}, bf16[2,128,128]{2,1,0:T(8,128)(2,1)}, u32[]{:S(2)}) %copy-start.3) | copy-done | bytes 65560
  25.1 0.7 copy-done.7
  25.7 0.7 copy-done.9
  26.4 0.7 copy-done.10
  27.1 1.0 %shard_map.92 = (f32[128,3200]{1,0:T(8,128)S(1)}, bf16[128,128]{1,0:T(8,128)(2,1)S(1)}, f32[128,128]{1,0:T(8,128)S(1)}, f32[128,128]{1,0:T(8,128)S(1)}, bf16[256...) custom-call(s32[2]{0:T(128)S(1)} %pad_add_fusion.meta, bf16[128,3200]{1,0:T(8,128)(2,1)S(1)} %get-tuple-element.42.normed, ...), custom_call_target="tpu_custom_call" | custom-call | bytes 3246728 | tf_op jit(solution)/shard_map/pallas_call | solution.py:488
  28.1 0.4 collective-permute-done.4.refs_3_
  28.5 1.0 %collective-permute-done.6.refs_5_ = bf16[16,3200]{1,0:T(8,128)(2,1)S(1)} collective-permute-done((bf16[16,3200]{1,0:T(8,128)(2,1)S(1)}, bf16[16,3200]{1,0:T(8,128)(2,1)S(1)}, u32[]{:S(2)}, u32[]{:S(2)}) %collective-permute-start.6) | collective-permute-done | bytes 102432 | tf_op jit(solution)/shard_map/ppermute | solution.py:503
  29.5 2.0 %shard_map.93 = (bf16[16,3200]{1,0:T(8,128)(2,1)S(1)}, bf16[16,3200]{1,0:T(8,128)(2,1)S(1)}, bf16[16,3200]{1,0:T(8,128)(2,1)S(1)}, bf16[16,3200]{1,0:T(8,128)(2,1)S(1)}) custom-call(s32[2]{0:T(128)S(1)} %pad_add_fusion.meta, f32[8,40,128]{2,1,0:T(8,128)S(1)} %get-tuple-element.43.masks, bf16[16,3200]{1,0:T(8,128)(2,1)S(1)} %collective-permute-done.1.refs_0_, ...), custom_call_target="tpu_custom_call" | custom-call | bytes 1802248 | tf_op jit(solution)/shard_map/pallas_call | solution.py:488
  31.6 1.8 %collective-permute-start.8 = (bf16[16,3200]{1,0:T(8,128)(2,1)S(1)}, bf16[16,3200]{1,0:T(8,128)(2,1)S(1)}, u32[]{:S(2)}, u32[]{:S(2)}) collective-permute-start(bf16[16,3200]{1,0:T(8,128)(2,1)S(1)} %get-tuple-element.53), channel_id=1, source_target_pairs={{0,2},{1,3},{2,0},{3,1},{4,6},{5,7},{6,4},{7,5},{8,10},{9,11},{10,... | collective-permute-start | bytes 307208 | tf_op jit(solution)/shard_map/ppermute | solution.py:503
  33.3 1.8 %collective-permute-start.10 = (bf16[16,3200]{1,0:T(8,128)(2,1)S(1)}, bf16[16,3200]{1,0:T(8,128)(2,1)S(1)}, u32[]{:S(2)}, u32[]{:S(2)}) collective-permute-start(bf16[16,3200]{1,0:T(8,128)(2,1)S(1)} %get-tuple-element.55), channel_id=1, source_target_pairs={{0,6},{1,7},{2,4},{3,5},{4,2},{5,3},{6,0},{7,1},{8,14},{9,15},{10,... | collective-permute-start | bytes 307208 | tf_op jit(solution)/shard_map/ppermute | solution.py:503
  35.1 2.3 %collective-permute-done.8 = bf16[16,3200]{1,0:T(8,128)(2,1)S(1)} collective-permute-done((bf16[16,3200]{1,0:T(8,128)(2,1)S(1)}, bf16[16,3200]{1,0:T(8,128)(2,1)S(1)}, u32[]{:S(2)}, u32[]{:S(2)}) %collective-permute-start.8) | collective-permute-done | bytes 102432 | tf_op jit(solution)/shard_map/ppermute | solution.py:503
  37.4 0.7 collective-permute-done.9
  38.1 0.9 %collective-permute-done.10 = bf16[16,3200]{1,0:T(8,128)(2,1)S(1)} collective-permute-done((bf16[16,3200]{1,0:T(8,128)(2,1)S(1)}, bf16[16,3200]{1,0:T(8,128)(2,1)S(1)}, u32[]{:S(2)}, u32[]{:S(2)}) %collective-permute-start.10) | collective-permute-done | bytes 102432 | tf_op jit(solution)/shard_map/ppermute | solution.py:503
  39.1 1.7 %collective-permute-done.11.other = bf16[64,3200]{1,0:T(8,128)(2,1)S(1)} collective-permute-done((bf16[64,3200]{1,0:T(8,128)(2,1)S(1)}, bf16[64,3200]{1,0:T(8,128)(2,1)S(1)}, u32[]{:S(2)}, u32[]{:S(2)}) %collective-permute-start.11) | collective-permute-done | bytes 409632 | tf_op jit(solution)/shard_map/ppermute | solution.py:507
  40.8 2.1 %shard_map.94 = (f32[128,3200]{1,0:T(8,128)S(1)}, bf16[128,3200]{1,0:T(8,128)(2,1)S(1)}, bf16[32,3200]{1,0:T(8,128)(2,1)S(1)}, bf16[32,3200]{1,0:T(8,128)(2,1)S(...) custom-call(bf16[64,3200]{1,0:T(8,128)(2,1)S(1)} %constant_dynamic-update-slice_fusion.own, ...), custom_call_target="tpu_custom_call" | custom-call | bytes 7602176 | tf_op jit(solution)/shard_map/pallas_call | solution.py:488
  42.9 2.0 %collective-permute-start.12 = (bf16[32,3200]{1,0:T(8,128)(2,1)S(1)}, bf16[32,3200]{1,0:T(8,128)(2,1)S(1)}, u32[]{:S(2)}, u32[]{:S(2)}) collective-permute-start(bf16[32,3200]{1,0:T(8,128)(2,1)S(1)} %get-tuple-element.62), channel_id=1, source_target_pairs={{0,4},{1,5},{2,6},{3,7},{4,0},{5,1},{6,2},{7,3},{8,12},{9,13},{10,... | collective-permute-start | bytes 614408 | tf_op jit(solution)/shard_map/ppermute | solution.py:503
  44.9 0.3 collective-permute-start.13
  45.2 1.2 %collective-permute-start.14 = (bf16[32,3200]{1,0:T(8,128)(2,1)S(1)}, bf16[32,3200]{1,0:T(8,128)(2,1)S(1)}, u32[]{:S(2)}, u32[]{:S(2)}) collective-permute-start(bf16[32,3200]{1,0:T(8,128)(2,1)S(1)} %get-tuple-element.64), channel_id=1, source_target_pairs={{0,6},{1,7},{2,4},{3,5},{4,2},{5,3},{6,0},{7,1},{8,14},{9,15},{10,... | collective-permute-start | bytes 614408 | tf_op jit(solution)/shard_map/ppermute | solution.py:503
  46.5 4.4 %collective-permute-done.12.refs_0_ = bf16[32,3200]{1,0:T(8,128)(2,1)S(1)} collective-permute-done((bf16[32,3200]{1,0:T(8,128)(2,1)S(1)}, bf16[32,3200]{1,0:T(8,128)(2,1)S(1)}, u32[]{:S(2)}, u32[]{:S(2)}) %collective-permute-start.12) | collective-permute-done | bytes 204832 | tf_op jit(solution)/shard_map/ppermute | solution.py:503
  50.9 5.3 %collective-permute-done.13.refs_1_ = bf16[32,3200]{1,0:T(8,128)(2,1)S(1)} collective-permute-done((bf16[32,3200]{1,0:T(8,128)(2,1)S(1)}, bf16[32,3200]{1,0:T(8,128)(2,1)S(1)}, u32[]{:S(2)}, u32[]{:S(2)}) %collective-permute-start.13) | collective-permute-done | bytes 204832 | tf_op jit(solution)/shard_map/ppermute | solution.py:503
  56.1 2.0 %shard_map.95 = (bf16[16,3200]{1,0:T(8,128)(2,1)S(1)}, bf16[16,3200]{1,0:T(8,128)(2,1)S(1)}, bf16[16,3200]{1,0:T(8,128)(2,1)S(1)}, bf16[16,3200]{1,0:T(8,128)(2,...) custom-call(s32[2]{0:T(128)S(1)} %pad_add_fusion.meta, ...), custom_call_target="tpu_custom_call" | custom-call | bytes 1802248 | tf_op jit(solution)/shard_map/pallas_call | solution.py:488
  58.2 2.5 %collective-permute-start.15 = (bf16[16,3200]{1,0:T(8,128)(2,1)S(1)}, bf16[16,3200]{1,0:T(8,128)(2,1)S(1)}, u32[]{:S(2)}, u32[]{:S(2)}) collective-permute-start(bf16[16,3200]{1,0:T(8,128)(2,1)S(1)} %get-tuple-element.66), channel_id=1, source_target_pairs={{0,8},{1,9},{2,10},{3,11},{4,12},{5,13},{6,14},{7,15},{8,0},{9,1},... | collective-permute-start | bytes 307208 | tf_op jit(solution)/shard_map/ppermute | solution.py:503
  60.7 1.7 %collective-permute-start.16 = (bf16[16,3200]{1,0:T(8,128)(2,1)S(1)}, bf16[16,3200]{1,0:T(8,128)(2,1)S(1)}, u32[]{:S(2)}, u32[]{:S(2)}) collective-permute-start(bf16[16,3200]{1,0:T(8,128)(2,1)S(1)} %get-tuple-element.67), channel_id=1, source_target_pairs={{0,4},{1,5},{2,6},{3,7},{4,0},{5,1},{6,2},{7,3},{8,12},{9,13},{10,... | collective-permute-start | bytes 307208 | tf_op jit(solution)/shard_map/ppermute | solution.py:503
  62.5 1.6 %collective-permute-start.18 = (bf16[16,3200]{1,0:T(8,128)(2,1)S(1)}, bf16[16,3200]{1,0:T(8,128)(2,1)S(1)}, u32[]{:S(2)}, u32[]{:S(2)}) collective-permute-start(bf16[16,3200]{1,0:T(8,128)(2,1)S(1)} %get-tuple-element.69), channel_id=1, source_target_pairs={{0,6},{1,7},{2,4},{3,5},{4,2},{5,3},{6,0},{7,1},{8,14},{9,15},{10,... | collective-permute-start | bytes 307208 | tf_op jit(solution)/shard_map/ppermute | solution.py:503
  64.1 3.6 %collective-permute-start.19 = (bf16[16,3200]{1,0:T(8,128)(2,1)S(1)}, bf16[16,3200]{1,0:T(8,128)(2,1)S(1)}, u32[]{:S(2)}, u32[]{:S(2)}) collective-permute-start(bf16[16,3200]{1,0:T(8,128)(2,1)S(1)} %get-tuple-element.70), channel_id=1, source_target_pairs={{0,12},{1,13},{2,14},{3,15},{4,8},{5,9},{6,10},{7,11},{8,4},{9,5},... | collective-permute-start | bytes 307208 | tf_op jit(solution)/shard_map/ppermute | solution.py:503
  67.7 0.6 collective-permute-start.20
  68.2 0.3 collective-permute-done.16.refs_1_
  68.5 3.7 %collective-permute-start.21 = (bf16[16,3200]{1,0:T(8,128)(2,1)S(1)}, bf16[16,3200]{1,0:T(8,128)(2,1)S(1)}, u32[]{:S(2)}, u32[]{:S(2)}) collective-permute-start(bf16[16,3200]{1,0:T(8,128)(2,1)S(1)} %get-tuple-element.72), channel_id=1, source_target_pairs={{0,14},{1,15},{2,12},{3,13},{4,10},{5,11},{6,8},{7,9},{8,6},{9,7},... | collective-permute-start | bytes 307208 | tf_op jit(solution)/shard_map/ppermute | solution.py:503
  72.2 2.1 %collective-permute-done.17.refs_2_ = bf16[16,3200]{1,0:T(8,128)(2,1)S(1)} collective-permute-done((bf16[16,3200]{1,0:T(8,128)(2,1)S(1)}, bf16[16,3200]{1,0:T(8,128)(2,1)S(1)}, u32[]{:S(2)}, u32[]{:S(2)}) %collective-permute-start.17) | collective-permute-done | bytes 102432 | tf_op jit(solution)/shard_map/ppermute | solution.py:503
  74.3 0.5 collective-permute-done.18.refs_3_
  74.8 1.1 %collective-permute-done.21.refs_6_ = bf16[16,3200]{1,0:T(8,128)(2,1)S(1)} collective-permute-done((bf16[16,3200]{1,0:T(8,128)(2,1)S(1)}, bf16[16,3200]{1,0:T(8,128)(2,1)S(1)}, u32[]{:S(2)}, u32[]{:S(2)}) %collective-permute-start.21) | collective-permute-done | bytes 102432 | tf_op jit(solution)/shard_map/ppermute | solution.py:503
  76.2 1.0 %shard_map.97 = (f32[128,3200]{1,0:T(8,128)S(1)}, bf16[128,128]{1,0:T(8,128)(2,1)S(1)}, f32[128,128]{1,0:T(8,128)S(1)}) custom-call(s32[2]{0:T(128)S(1)} %pad_add_fusion.meta, bf16[128,3200]{1,0:T(8,128)(2,1)S(1)} %get-tuple-element.75.normed, bf16[2,128,640]{2,1,0:T(8,128)(2,1)S(1)} %copy-done.1, f32[2,128]{1,0:T(2,128)S(1)} %copy-done.8, ...), custom_call_target="tpu_custom_call" | custom-call | bytes 2950152 | tf_op jit(solution)/shard_map/pallas_call | solution.py:488
  77.1 0.7 collective-permute-done.22.other
  77.9 3.9 %shard_map.98 = bf16[40,40,128]{2,1,0:T(8,128)(2,1)} custom-call(s32[2]{0:T(128)S(1)} %pad_add_fusion.meta, bf16[64,3200]{1,0:T(8,128)(2,1)S(1)} %shard_map.96.own, bf16[64,3200]{1,0:T(8,128)(2,1)S(1)} %collective-permute-done.22.other, f32[128,3200]{1,0:T(8,128)S(1)} %get-tuple-element.74.stream, f32[128,3200]{1,0:T(8,128)S(1)} %get-tuple-element.76.gate, ...), custom_call_target="tpu_custom_call" | custom-call | bytes 4866568 | tf_op jit(solution)/shard_map/pallas_call | solution.py:488
  (37 shorter events, 0.5 us)
Async XLA Ops:
  0.0 2.1 %collective-permute-start = (bf16[40,40,128]{2,1,0:T(8,128)(2,1)}, bf16[40,40,128]{2,1,0:T(8,128)(2,1)S(1)}, u32[]{:S(2)}, u32[]{:S(2)}) collective-permute-start(bf16[40,40,128]{2,1,0:T(8,128)(2,1)} %own.1), channel_id=1, source_target_pairs={{0,1},{1,0},{2,3},{3,2},{4,5},{5,4},{6,7},{7,6},{8,9},{9,8},{10,11... | collective-permute-start | bytes 1228808 | tf_op jit(solution)/shard_map/ppermute | solution.py:507
  2.1 1.0 %copy-start.2 = (bf16[40,40,128]{2,1,0:T(8,128)(2,1)S(1)}, bf16[40,40,128]{2,1,0:T(8,128)(2,1)}, u32[]{:S(2)}) copy-start(bf16[40,40,128]{2,1,0:T(8,128)(2,1)} %own.1) | copy-start | bytes 1228804
  4.8 11.4 %collective-permute-start.1 = (bf16[16,3200]{1,0:T(8,128)(2,1)S(1)}, bf16[16,3200]{1,0:T(8,128)(2,1)S(1)}, u32[]{:S(2)}, u32[]{:S(2)}) collective-permute-start(bf16[16,3200]{1,0:T(8,128)(2,1)S(1)} %get-tuple-element.44), channel_id=1, source_target_pairs={{0,8},{1,9},{2,10},{3,11},{4,12},{5,13},{6,14},{7,15},{8,0},{9,1},... | collective-permute-start | bytes 307208 | tf_op jit(solution)/shard_map/ppermute | solution.py:503
  8.7 11.4 %collective-permute-start.2 = (bf16[16,3200]{1,0:T(8,128)(2,1)S(1)}, bf16[16,3200]{1,0:T(8,128)(2,1)S(1)}, u32[]{:S(2)}, u32[]{:S(2)}) collective-permute-start(bf16[16,3200]{1,0:T(8,128)(2,1)S(1)} %get-tuple-element.45), channel_id=1, source_target_pairs={{0,10},{1,11},{2,8},{3,9},{4,14},{5,15},{6,12},{7,13},{8,2},{9,3},... | collective-permute-start | bytes 307208 | tf_op jit(solution)/shard_map/ppermute | solution.py:503
  10.0 19.5 %collective-permute-start.3 = (bf16[32,3200]{1,0:T(8,128)(2,1)S(1)}, bf16[32,3200]{1,0:T(8,128)(2,1)S(1)}, u32[]{:S(2)}, u32[]{:S(2)}) collective-permute-start(bf16[32,3200]{1,0:T(8,128)(2,1)S(1)} %get-tuple-element.46), channel_id=1, source_target_pairs={{0,4},{1,5},{2,6},{3,7},{4,0},{5,1},{6,2},{7,3},{8,12},{9,13},{10,... | collective-permute-start | bytes 614408 | tf_op jit(solution)/shard_map/ppermute | solution.py:503
  11.6 17.9 %collective-permute-start.5 = (bf16[32,3200]{1,0:T(8,128)(2,1)S(1)}, bf16[32,3200]{1,0:T(8,128)(2,1)S(1)}, u32[]{:S(2)}, u32[]{:S(2)}) collective-permute-start(bf16[32,3200]{1,0:T(8,128)(2,1)S(1)} %get-tuple-element.48), channel_id=1, source_target_pairs={{0,6},{1,7},{2,4},{3,5},{4,2},{5,3},{6,0},{7,1},{8,14},{9,15},{10,... | collective-permute-start | bytes 614408 | tf_op jit(solution)/shard_map/ppermute | solution.py:503
  11.7 17.8 %collective-permute-start.7 = (bf16[32,3200]{1,0:T(8,128)(2,1)S(1)}, bf16[32,3200]{1,0:T(8,128)(2,1)S(1)}, u32[]{:S(2)}, u32[]{:S(2)}) collective-permute-start(bf16[32,3200]{1,0:T(8,128)(2,1)S(1)} %get-tuple-element.50), channel_id=1, source_target_pairs={{0,2},{1,3},{2,0},{3,1},{4,6},{5,7},{6,4},{7,5},{8,10},{9,11},{10,... | collective-permute-start | bytes 614408 | tf_op jit(solution)/shard_map/ppermute | solution.py:503
  16.2 12.3 %collective-permute-start.4 = (bf16[16,3200]{1,0:T(8,128)(2,1)S(1)}, bf16[16,3200]{1,0:T(8,128)(2,1)S(1)}, u32[]{:S(2)}, u32[]{:S(2)}) collective-permute-start(bf16[16,3200]{1,0:T(8,128)(2,1)S(1)} %get-tuple-element.47), channel_id=1, source_target_pairs={{0,12},{1,13},{2,14},{3,15},{4,8},{5,9},{6,10},{7,11},{8,4},{9,5},... | collective-permute-start | bytes 307208 | tf_op jit(solution)/shard_map/ppermute | solution.py:503
  20.1 9.4 %collective-permute-start.6 = (bf16[16,3200]{1,0:T(8,128)(2,1)S(1)}, bf16[16,3200]{1,0:T(8,128)(2,1)S(1)}, u32[]{:S(2)}, u32[]{:S(2)}) collective-permute-start(bf16[16,3200]{1,0:T(8,128)(2,1)S(1)} %get-tuple-element.49), channel_id=1, source_target_pairs={{0,14},{1,15},{2,12},{3,13},{4,10},{5,11},{6,8},{7,9},{8,6},{9,7},... | collective-permute-start | bytes 307208 | tf_op jit(solution)/shard_map/ppermute | solution.py:503
  23.3 1.0 %copy-start = (bf16[2,128,640]{2,1,0:T(8,128)(2,1)S(1)}, bf16[2,128,640]{2,1,0:T(8,128)(2,1)}, u32[]{:S(2)}) copy-start(bf16[2,128,640]{2,1,0:T(8,128)(2,1)} %weight.3) | copy-start | bytes 983044
  24.2 0.8 %copy-start.3 = (bf16[2,128,128]{2,1,0:T(8,128)(2,1)S(1)}, bf16[2,128,128]{2,1,0:T(8,128)(2,1)}, u32[]{:S(2)}) copy-start(bf16[2,128,128]{2,1,0:T(8,128)(2,1)} %out_weight.3) | copy-start | bytes 196612
  25.1 0.7 copy-start.7
  25.7 0.7 copy-start.9
  26.4 0.7 copy-start.10
  31.6 5.8 %collective-permute-start.8 = (bf16[16,3200]{1,0:T(8,128)(2,1)S(1)}, bf16[16,3200]{1,0:T(8,128)(2,1)S(1)}, u32[]{:S(2)}, u32[]{:S(2)}) collective-permute-start(bf16[16,3200]{1,0:T(8,128)(2,1)S(1)} %get-tuple-element.53), channel_id=1, source_target_pairs={{0,2},{1,3},{2,0},{3,1},{4,6},{5,7},{6,4},{7,5},{8,10},{9,11},{10,... | collective-permute-start | bytes 307208 | tf_op jit(solution)/shard_map/ppermute | solution.py:503
  33.3 4.8 %collective-permute-start.9 = (bf16[16,3200]{1,0:T(8,128)(2,1)S(1)}, bf16[16,3200]{1,0:T(8,128)(2,1)S(1)}, u32[]{:S(2)}, u32[]{:S(2)}) collective-permute-start(bf16[16,3200]{1,0:T(8,128)(2,1)S(1)} %get-tuple-element.54), channel_id=1, source_target_pairs={{0,4},{1,5},{2,6},{3,7},{4,0},{5,1},{6,2},{7,3},{8,12},{9,13},{10,... | collective-permute-start | bytes 307208 | tf_op jit(solution)/shard_map/ppermute | solution.py:503
  33.3 5.7 %collective-permute-start.10 = (bf16[16,3200]{1,0:T(8,128)(2,1)S(1)}, bf16[16,3200]{1,0:T(8,128)(2,1)S(1)}, u32[]{:S(2)}, u32[]{:S(2)}) collective-permute-start(bf16[16,3200]{1,0:T(8,128)(2,1)S(1)} %get-tuple-element.55), channel_id=1, source_target_pairs={{0,6},{1,7},{2,4},{3,5},{4,2},{5,3},{6,0},{7,1},{8,14},{9,15},{10,... | collective-permute-start | bytes 307208 | tf_op jit(solution)/shard_map/ppermute | solution.py:503
  39.0 1.8 %collective-permute-start.11 = (bf16[64,3200]{1,0:T(8,128)(2,1)S(1)}, bf16[64,3200]{1,0:T(8,128)(2,1)S(1)}, u32[]{:S(2)}, u32[]{:S(2)}) collective-permute-start(bf16[64,3200]{1,0:T(8,128)(2,1)S(1)} %constant_dynamic-update-slice_fusion.own), channel_id=1, source_target_pairs={{0,1},{1,0},{2,3},{3,2},{4,5},{5,4},{6,7},{7,6},{8,9},{9,8},{10,11... | collective-permute-start | bytes 1228808 | tf_op jit(solution)/shard_map/ppermute | solution.py:507
  42.9 33.3 %copy-start.1 = (bf16[2,128,640]{2,1,0:T(8,128)(2,1)S(1)}, bf16[2,128,640]{2,1,0:T(8,128)(2,1)}, u32[]{:S(2)}) copy-start(bf16[2,128,640]{2,1,0:T(8,128)(2,1)} %weight.3) | copy-start | bytes 983044
  42.9 33.3 %copy-start.4 = (bf16[2,128,128]{2,1,0:T(8,128)(2,1)S(1)}, bf16[2,128,128]{2,1,0:T(8,128)(2,1)}, u32[]{:S(2)}) copy-start(bf16[2,128,128]{2,1,0:T(8,128)(2,1)} %out_weight.3) | copy-start | bytes 196612
  42.9 33.3 %copy-start.8 = (f32[2,128]{1,0:T(2,128)S(1)}, f32[2,128]{1,0:T(2,128)}, u32[]{:S(2)}) copy-start(f32[2,128]{1,0:T(2,128)} %middle_gain.3) | copy-start | bytes 3076
  42.9 8.0 %collective-permute-start.12 = (bf16[32,3200]{1,0:T(8,128)(2,1)S(1)}, bf16[32,3200]{1,0:T(8,128)(2,1)S(1)}, u32[]{:S(2)}, u32[]{:S(2)}) collective-permute-start(bf16[32,3200]{1,0:T(8,128)(2,1)S(1)} %get-tuple-element.62), channel_id=1, source_target_pairs={{0,4},{1,5},{2,6},{3,7},{4,0},{5,1},{6,2},{7,3},{8,12},{9,13},{10,... | collective-permute-start | bytes 614408 | tf_op jit(solution)/shard_map/ppermute | solution.py:503
  44.9 11.2 %collective-permute-start.13 = (bf16[32,3200]{1,0:T(8,128)(2,1)S(1)}, bf16[32,3200]{1,0:T(8,128)(2,1)S(1)}, u32[]{:S(2)}, u32[]{:S(2)}) collective-permute-start(bf16[32,3200]{1,0:T(8,128)(2,1)S(1)} %get-tuple-element.63), channel_id=1, source_target_pairs={{0,2},{1,3},{2,0},{3,1},{4,6},{5,7},{6,4},{7,5},{8,10},{9,11},{10,... | collective-permute-start | bytes 614408 | tf_op jit(solution)/shard_map/ppermute | solution.py:503
  45.2 10.9 %collective-permute-start.14 = (bf16[32,3200]{1,0:T(8,128)(2,1)S(1)}, bf16[32,3200]{1,0:T(8,128)(2,1)S(1)}, u32[]{:S(2)}, u32[]{:S(2)}) collective-permute-start(bf16[32,3200]{1,0:T(8,128)(2,1)S(1)} %get-tuple-element.64), channel_id=1, source_target_pairs={{0,6},{1,7},{2,4},{3,5},{4,2},{5,3},{6,0},{7,1},{8,14},{9,15},{10,... | collective-permute-start | bytes 614408 | tf_op jit(solution)/shard_map/ppermute | solution.py:503
  56.1 21.7 %copy-start.5 = (bf16[128,512]{1,0:T(8,128)(2,1)S(1)}, bf16[128,512]{1,0:T(8,128)(2,1)}, u32[]{:S(2)}) copy-start(bf16[128,512]{1,0:T(8,128)(2,1)} %expand.1) | copy-start | bytes 393220
  56.1 21.7 %copy-start.6 = (bf16[512,128]{1,0:T(8,128)(2,1)S(1)}, bf16[512,128]{1,0:T(8,128)(2,1)}, u32[]{:S(2)}) copy-start(bf16[512,128]{1,0:T(8,128)(2,1)} %shrink.1) | copy-start | bytes 393220
  56.1 21.7 %copy-start.11 = (f32[128]{0:T(128)S(1)}, f32[128]{0:T(128)}, u32[]{:S(2)}) copy-start(f32[128]{0:T(128)} %param.15) | copy-start | bytes 1540
  58.2 9.5 %collective-permute-start.15 = (bf16[16,3200]{1,0:T(8,128)(2,1)S(1)}, bf16[16,3200]{1,0:T(8,128)(2,1)S(1)}, u32[]{:S(2)}, u32[]{:S(2)}) collective-permute-start(bf16[16,3200]{1,0:T(8,128)(2,1)S(1)} %get-tuple-element.66), channel_id=1, source_target_pairs={{0,8},{1,9},{2,10},{3,11},{4,12},{5,13},{6,14},{7,15},{8,0},{9,1},... | collective-permute-start | bytes 307208 | tf_op jit(solution)/shard_map/ppermute | solution.py:503
  60.7 7.8 %collective-permute-start.16 = (bf16[16,3200]{1,0:T(8,128)(2,1)S(1)}, bf16[16,3200]{1,0:T(8,128)(2,1)S(1)}, u32[]{:S(2)}, u32[]{:S(2)}) collective-permute-start(bf16[16,3200]{1,0:T(8,128)(2,1)S(1)} %get-tuple-element.67), channel_id=1, source_target_pairs={{0,4},{1,5},{2,6},{3,7},{4,0},{5,1},{6,2},{7,3},{8,12},{9,13},{10,... | collective-permute-start | bytes 307208 | tf_op jit(solution)/shard_map/ppermute | solution.py:503
  62.4 11.9 %collective-permute-start.17 = (bf16[16,3200]{1,0:T(8,128)(2,1)S(1)}, bf16[16,3200]{1,0:T(8,128)(2,1)S(1)}, u32[]{:S(2)}, u32[]{:S(2)}) collective-permute-start(bf16[16,3200]{1,0:T(8,128)(2,1)S(1)} %get-tuple-element.68), channel_id=1, source_target_pairs={{0,10},{1,11},{2,8},{3,9},{4,14},{5,15},{6,12},{7,13},{8,2},{9,3},... | collective-permute-start | bytes 307208 | tf_op jit(solution)/shard_map/ppermute | solution.py:503
  62.5 12.4 %collective-permute-start.18 = (bf16[16,3200]{1,0:T(8,128)(2,1)S(1)}, bf16[16,3200]{1,0:T(8,128)(2,1)S(1)}, u32[]{:S(2)}, u32[]{:S(2)}) collective-permute-start(bf16[16,3200]{1,0:T(8,128)(2,1)S(1)} %get-tuple-element.69), channel_id=1, source_target_pairs={{0,6},{1,7},{2,4},{3,5},{4,2},{5,3},{6,0},{7,1},{8,14},{9,15},{10,... | collective-permute-start | bytes 307208 | tf_op jit(solution)/shard_map/ppermute | solution.py:503
  64.1 10.7 %collective-permute-start.19 = (bf16[16,3200]{1,0:T(8,128)(2,1)S(1)}, bf16[16,3200]{1,0:T(8,128)(2,1)S(1)}, u32[]{:S(2)}, u32[]{:S(2)}) collective-permute-start(bf16[16,3200]{1,0:T(8,128)(2,1)S(1)} %get-tuple-element.70), channel_id=1, source_target_pairs={{0,12},{1,13},{2,14},{3,15},{4,8},{5,9},{6,10},{7,11},{8,4},{9,5},... | collective-permute-start | bytes 307208 | tf_op jit(solution)/shard_map/ppermute | solution.py:503
  67.7 7.2 %collective-permute-start.20 = (bf16[16,3200]{1,0:T(8,128)(2,1)S(1)}, bf16[16,3200]{1,0:T(8,128)(2,1)S(1)}, u32[]{:S(2)}, u32[]{:S(2)}) collective-permute-start(bf16[16,3200]{1,0:T(8,128)(2,1)S(1)} %get-tuple-element.71), channel_id=1, source_target_pairs={{0,2},{1,3},{2,0},{3,1},{4,6},{5,7},{6,4},{7,5},{8,10},{9,11},{10,... | collective-permute-start | bytes 307208 | tf_op jit(solution)/shard_map/ppermute | solution.py:503
  68.5 7.5 %collective-permute-start.21 = (bf16[16,3200]{1,0:T(8,128)(2,1)S(1)}, bf16[16,3200]{1,0:T(8,128)(2,1)S(1)}, u32[]{:S(2)}, u32[]{:S(2)}) collective-permute-start(bf16[16,3200]{1,0:T(8,128)(2,1)S(1)} %get-tuple-element.72), channel_id=1, source_target_pairs={{0,14},{1,15},{2,12},{3,13},{4,10},{5,11},{6,8},{7,9},{8,6},{9,7},... | collective-permute-start | bytes 307208 | tf_op jit(solution)/shard_map/ppermute | solution.py:503
  76.1 1.8 %collective-permute-start.22 = (bf16[64,3200]{1,0:T(8,128)(2,1)S(1)}, bf16[64,3200]{1,0:T(8,128)(2,1)S(1)}, u32[]{:S(2)}, u32[]{:S(2)}) collective-permute-start(bf16[64,3200]{1,0:T(8,128)(2,1)S(1)} %shard_map.96.own), channel_id=1, source_target_pairs={{0,1},{1,0},{2,3},{3,2},{4,5},{5,4},{6,7},{7,6},{8,9},{9,8},{10,11... | collective-permute-start | bytes 1228808 | tf_op jit(solution)/shard_map/ppermute | solution.py:507
